TPU v7x, 256 devices: a whole 4x4x8 slice. The times are simulated.
256 devices in a mesh: replica: 16 (over z, core), fsdp: 16 (over x, y).
Axes of the slice: x: 4, y: 4, z: 8, core: 2. Of those that a mesh axis runs over, the one named last changes fastest.
Arguments:
- drift: bfloat16 [16, 2560, 10240], P('replica', 'fsdp'), may hold values from -12 to 12
- error: bfloat16 [16, 2560, 10240], P('replica', 'fsdp'), may hold values from -6 to 6
- start: float32 [10240, 64], replicated, may hold values from -0.0625 to 0.0625
- weights: float32 [2560, 10240], P('fsdp', 'replica'), may hold values from -3 to 3
- momentum: float32 [2560, 10240], P('fsdp', 'replica'), may hold values from -2 to 2
Outputs:
- new_weights: float32 [2560, 10240], P('fsdp', 'replica')
- new_error: bfloat16 [16, 2560, 10240], P('replica', 'fsdp')
- new_momentum: float32 [2560, 10240], P('fsdp', 'replica')
All inputs are finite; a program needn't handle non-finite values.
Results may differ from a plain program's by a relative error of at most 0.001.
Values sent between devices are 32-bit elements; how exact they have to be, the bound alone decides.
No kernel may reach another device: no remote copies, remote signals or barrier semaphores. Data moves between devices by JAX's collectives and lax.ppermute only.
A program may use at most 64 MiB of HBM per device.

v0:
```python
import jax
import jax.numpy as jnp
from jax import lax
from jax.sharding import PartitionSpec as P

outer_rate = 0.7
momentum_decay = 0.9
full_prec = lax.Precision.HIGHEST


def local(drift, error, start, weights, momentum):
    groups = lax.axis_size("replica")
    merged = drift[0].astype(jnp.float32) + error[0].astype(jnp.float32)
    partial_p = jnp.dot(merged, start, precision=full_prec, preferred_element_type=jnp.float32)
    mean_p = lax.psum(partial_p, "replica") / groups
    local_gram = jnp.dot(mean_p.T, mean_p, precision=full_prec, preferred_element_type=jnp.float32)
    gram = lax.psum(local_gram, "fsdp")
    lower = jnp.linalg.cholesky(gram)
    basis = lax.linalg.triangular_solve(
        lower, mean_p, left_side=False, lower=True, transpose_a=True
    )
    partial_q = lax.dot_general(
        merged,
        basis,
        (((0,), (0,)), ((), ())),
        precision=full_prec,
        preferred_element_type=jnp.float32,
    )
    total_q = lax.psum(partial_q, ("replica", "fsdp"))
    mean_q = total_q / groups
    approx = lax.dot_general(
        basis,
        mean_q,
        (((1,), (1,)), ((), ())),
        precision=full_prec,
        preferred_element_type=jnp.float32,
    )
    new_error = (merged - approx).astype(jnp.bfloat16)[None]
    block = weights.shape[1]
    begin = lax.axis_index("replica") * block
    update = lax.dynamic_slice_in_dim(approx, begin, block, 1)
    new_momentum = momentum_decay * momentum + update
    new_weights = weights - outer_rate * (update + momentum_decay * new_momentum)
    return (new_weights, new_error, new_momentum)


def solution(mesh):
    return jax.shard_map(
        local,
        mesh=mesh,
        in_specs=(
            P("replica", "fsdp", None),
            P("replica", "fsdp", None),
            P(),
            P("fsdp", "replica"),
            P("fsdp", "replica"),
        ),
        out_specs=(P("fsdp", "replica"), P("replica", "fsdp", None), P("fsdp", "replica")),
        check_vma=False,
    )
```

profile of v0, /device:TPU:1, one launch (start us, length us, event | category | flops | bytes accessed | tf_op | source)
XLA Modules:
  0.0 438.4 jit_solution(5386644826220517227)
XLA Ops:
  7.2 0.0 copy-start
  7.2 0.0 all-reduce.2.cloned.1.call-start
  7.2 1.7 copy-done
  8.9 8.9 %fusion.2 = f32[160,64]{0,1:T(8,128)S(1)} fusion(f32[10240,64]{0,1:T(8,128)S(1)} %copy-done, bf16[1,160,10240]{2,1,0:T(8,128)(2,1)} %param.6, bf16[1,160,10240]{2,1,0:T(8,128)(2,1)} %param.5), kind=kOutput, calls=%fused_computation.3 | convolution fusion | flops 1263206400 | bytes 9216000 | tf_op jit(solution)/shard_map/dot_general | solution.py:14
  17.8 48.9 %psum.21 = f32[160,64]{0,1:T(8,128)S(1)} all-reduce(f32[160,64]{0,1:T(8,128)S(1)} %fusion.2), channel_id=1, replica_groups=mesh['replica'=16,'fsdp'=16] {'replica'}, use_global_device_ids=true, to_apply=%region_0.0 | all-reduce | flops 10240 | bytes 81920 | tf_op jit(solution)/shard_map/psum | solution.py:15
  66.7 0.2 fusion.11
  66.9 60.7 %psum.22 = f32[64,64]{0,1:T(8,128)S(1)} all-reduce(f32[64,64]{0,1:T(8,128)S(1)} %fusion.11), channel_id=1, replica_groups=mesh['replica'=16,'fsdp'=16] {'fsdp'}, use_global_device_ids=true, to_apply=%region_1.0 | all-reduce | flops 4096 | bytes 32768 | tf_op jit(solution)/shard_map/psum | solution.py:17
  127.7 0.1 copy.11
  127.8 5.8 %cholesky.16 = f32[64,64]{1,0:T(8,128)S(1)} custom-call(f32[64,64]{1,0:T(8,128)S(1)} %fusion.15), custom_call_target="Cholesky" | custom-call | tf_op jit(solution)/shard_map/jit(cholesky)/cholesky | solution.py:18
  133.7 0.6 compare_reduce_fusion
  134.3 0.7 fusion.13
  135.0 4.9 %custom-call.6 = f32[1,64,64]{1,2,0:T(8,128)S(1)} custom-call(f32[1,64,64]{2,1,0:T(8,128)S(1)} %fusion.13), custom_call_target="InvertDiagBlocksLowerTriangular" | custom-call | tf_op jit(solution)/shard_map/triangular_solve | solution.py:19
  139.9 0.3 fusion.9
  140.1 8.8 %fusion = f32[10240,64]{0,1:T(8,128)} fusion(f32[160,64]{0,1:T(8,128)S(1)} %fusion.9, bf16[1,160,10240]{2,1,0:T(8,128)(2,1)} %param.6, bf16[1,160,10240]{2,1,0:T(8,128)(2,1)} %param.5), kind=kOutput, calls=%fused_computation.1 | convolution fusion | flops 1263206400 | bytes 9216000 | tf_op jit(solution)/shard_map/dot_general | solution.py:22
  148.9 0.0 all-reduce.2.cloned.1.call-update
  149.0 271.0 %all-reduce.2.cloned.1.call-done = f32[10240,64]{0,1:T(8,128)} async-done(((f32[10240,64]{0,1:T(8,128)}), f32[10240,64]{0,1:T(8,128)}) %all-reduce.2.cloned.1.call-update) | async-done | bytes 2621456 | tf_op jit(solution)/shard_map/psum | solution.py:29
  420.0 0.0 copy-start.1
  420.0 0.0 copy-start.2
  420.0 7.3 %fusion.6 = f32[160,10240]{1,0:T(8,128)S(1)} fusion(f32[160,64]{0,1:T(8,128)S(1)} %fusion.9, f32[10240,64]{0,1:T(8,128)} %all-reduce.2.cloned.1.call-done), kind=kOutput, calls=%fused_computation.8 | convolution fusion | flops 1258946560 | bytes 9216000 | tf_op jit(solution)/shard_map/dot_general | solution.py:31
  427.4 0.0 copy-done.1
  427.4 0.0 copy-done.2
  427.4 0.0 copy-start.3
  427.4 0.0 copy-start.4
  427.4 3.2 fusion.5
  430.6 0.0 copy-done.3
  430.6 0.0 copy-done.4
  430.6 1.0 multiply_subtract_fusion
  (2 shorter events, 0.0 us)
Async XLA Ops:
  7.2 1.7 copy-start
  7.2 412.8 %all-reduce.2.cloned.1.call-start = ((), (), s32[]{:S(2)}) async-start(), calls=%async_computation | async-start | bytes 5242880 | tf_op jit(solution)/shard_map/psum | solution.py:29
  420.0 7.4 %copy-start.1 = (bf16[1,160,10240]{2,1,0:T(8,128)(2,1)S(1)}, bf16[1,160,10240]{2,1,0:T(8,128)(2,1)}, u32[]{:S(2)}) copy-start(bf16[1,160,10240]{2,1,0:T(8,128)(2,1)} %param.6) | copy-start | bytes 9830404
  420.0 7.4 %copy-start.2 = (bf16[1,160,10240]{2,1,0:T(8,128)(2,1)S(1)}, bf16[1,160,10240]{2,1,0:T(8,128)(2,1)}, u32[]{:S(2)}) copy-start(bf16[1,160,10240]{2,1,0:T(8,128)(2,1)} %param.5) | copy-start | bytes 9830404
  427.4 3.2 copy-start.3
  427.4 3.2 copy-start.4
Sparse Core Ops, SparseCore 0:
  149.1 270.8 all-reduce.1
where the time goes:
time: 439 us; the launch traced here: 438 us
  waiting for transfers between devices  271 us (62%)
  blocking collectives  110 us (25%)
  matrix products  25.5 us (6%)
  other arithmetic  16.2 us (4%)
  between operations  14.1 us (3%)
    psum x1, waiting for transfers between devices, local(): total_q = lax.psum(partial_q, ('replica', 'fsdp'))  271 us
    psum x1, blocking collectives, local(): gram = lax.psum(local_gram, 'fsdp')  60.7 us
    psum x1, blocking collectives, local(): mean_p = lax.psum(partial_p, 'replica') / groups  48.9 us
    dot_general x1, matrix products, local(): jnp.dot(merged, start, precision=full_prec, preferred_element_type=jnp.fl...  8.91 us
    dot_general x1, matrix products, local(): lax.dot_general(merged, basis, (((0,), (0,)), ((), ())), precision=full_p...  8.79 us
  transfers between devices with their start and end apart: 1, of which 1 were waited for; matrix products, arithmetic and copies ran while one was open for 0% of the time, Pallas kernels for 0%

commit v1 on v0

v1 whole, which is shorter than its diff:
```python
import jax
import jax.numpy as jnp
from jax import lax
from jax.experimental import pallas as pl
from jax.experimental.pallas import tpu as pltpu
from jax.sharding import Mesh, PartitionSpec as P

outer_rate = 0.7
momentum_decay = 0.9

rows = 160
cols = 10240
rank = 64
wide = 1280
half_blocks = 4
blocks = 8
groups = 16
f32 = jnp.float32
bf16 = jnp.bfloat16
vmem_bytes = 40 * 1024 * 1024


def split(value, pieces):
    out = []
    for _ in range(pieces - 1):
        head = value.astype(bf16)
        out.append(head)
        value = value - head.astype(f32)
    out.append(value.astype(bf16))
    return out


def dot(a, b):
    return jnp.dot(a, b, preferred_element_type=f32)


def left_kernel(drift, error, start, out, acc):
    step = pl.program_id(0)
    both = jnp.concatenate([drift[...], error[...]], axis=0)
    factor = jnp.concatenate(split(start[...], 3), axis=1)
    term = dot(both, factor)

    @pl.when(step == 0)
    def _():
        acc[...] = term

    @pl.when(step > 0)
    def _():
        acc[...] += term

    @pl.when(step == blocks - 1)
    def _():
        total = acc[:rows, :] + acc[rows:, :]
        left = total[:, :rank] + total[:, rank : 2 * rank] + total[:, 2 * rank :]
        out[...] = jnp.concatenate([left[: rows // 2], left[rows // 2 :]], axis=1)


def left_factor(drift, error, start):
    return pl.pallas_call(
        left_kernel,
        grid=(blocks,),
        in_specs=[
            pl.BlockSpec((rows, wide), lambda s: (0, s)),
            pl.BlockSpec((rows, wide), lambda s: (0, s)),
            pl.BlockSpec((wide, rank), lambda s: (s, 0)),
        ],
        out_specs=pl.BlockSpec((rows // 2, 2 * rank), lambda s: (0, 0)),
        out_shape=jax.ShapeDtypeStruct((rows // 2, 2 * rank), f32),
        scratch_shapes=[pltpu.VMEM((2 * rows, 3 * rank), f32)],
        compiler_params=pltpu.CompilerParams(vmem_limit_bytes=vmem_bytes),
        name="left",
    )(drift, error, start)


def right_kernel(place, parts, drift, error, keep, send, left_out, pieces):
    step = pl.program_id(0)

    @pl.when(step == 0)
    def _():
        total = jnp.sum(parts[...], axis=0) * (1.0 / groups)
        left = jnp.concatenate([total[:, :rank], total[:, rank:]], axis=0)
        left_out[...] = left
        pieces[...] = jnp.concatenate(split(left.T, 3), axis=0)

    term = dot(pieces[...], drift[...]) + dot(pieces[...], error[...])
    block = term[:rank] + term[rank : 2 * rank] + term[2 * rank :]
    chunk = lax.rem(step, half_blocks)
    for x in range(4):
        part = block[16 * x : 16 * (x + 1)]

        @pl.when(step < half_blocks)
        def _():
            keep[4 * x + chunk] = part

        @pl.when(step >= half_blocks)
        def _():
            send[4 * x + chunk] = part


def column_block(step, place):
    half = step // half_blocks
    return (half + place[0] - 2 * half * place[0]) * half_blocks + lax.rem(step, half_blocks)


def right_factor(place, parts, drift, error):
    chunks = jax.ShapeDtypeStruct((16, 16, wide), f32)
    whole = pl.BlockSpec((16, 16, wide), lambda s, place: (0, 0, 0))
    return pl.pallas_call(
        right_kernel,
        grid_spec=pltpu.PrefetchScalarGridSpec(
            num_scalar_prefetch=1,
            grid=(blocks,),
            in_specs=[
                pl.BlockSpec((8, rows // 2, 2 * rank), lambda s, place: (0, 0, 0)),
                pl.BlockSpec((rows, wide), lambda s, place: (0, column_block(s, place))),
                pl.BlockSpec((rows, wide), lambda s, place: (0, column_block(s, place))),
            ],
            out_specs=[whole, whole, pl.BlockSpec((rows, rank), lambda s, place: (0, 0))],
            scratch_shapes=[pltpu.VMEM((3 * rank, rows), bf16)],
        ),
        out_shape=[chunks, chunks, jax.ShapeDtypeStruct((rows, rank), f32)],
        compiler_params=pltpu.CompilerParams(vmem_limit_bytes=vmem_bytes),
        name="right",
    )(place, parts, drift, error)


def inverse(gram):
    eye = (
        lax.broadcasted_iota(jnp.int32, (rank, rank), 0)
        == lax.broadcasted_iota(jnp.int32, (rank, rank), 1)
    ).astype(f32)
    work = jnp.concatenate([gram, eye], axis=1)
    row_id = lax.broadcasted_iota(jnp.int32, (rank, 2 * rank), 0)
    for k in range(rank):
        pivot = work[k : k + 1, :] / work[k : k + 1, k : k + 1]
        work = jnp.where(row_id == k, pivot, work - work[:, k : k + 1] * pivot)
    return work[:, rank:]


def gather_block(source, chunk):
    return jnp.concatenate([source[4 * x + chunk] for x in range(4)], axis=0)


def final_kernel(
    place, own, other, start, left, drift, error, weights, momentum,
    new_weights, new_error, new_momentum, factor, approx_buf,
):
    step = pl.program_id(0)

    @pl.when(step == 0)
    def _():
        core = place[0]
        total = jnp.zeros((3 * rank, 3 * rank), f32)
        for half, source in ((0, own), (1, other)):
            for chunk in range(half_blocks):
                block = gather_block(source, chunk)
                begin = (half + core - 2 * half * core) * (cols // 2) + chunk * wide
                basis = start[pl.ds(pl.multiple_of(begin, wide), wide), :]
                total += dot(
                    jnp.concatenate(split(block, 3), axis=0),
                    jnp.concatenate(split(basis, 3), axis=1),
                )
        total = total[:rank] + total[rank : 2 * rank] + total[2 * rank :]
        gram = (total[:, :rank] + total[:, rank : 2 * rank] + total[:, 2 * rank :]) * (1.0 / groups)
        gram = 0.5 * (gram + gram.T)
        solved = jnp.dot(
            left[...], inverse(gram) * (1.0 / groups), precision=lax.Precision.HIGHEST,
            preferred_element_type=f32,
        )
        high, low = split(solved, 2)
        factor[...] = jnp.concatenate([high, high, low], axis=1)

    chunk = lax.rem(step, half_blocks)

    def finish(source):
        high, low = split(gather_block(source, chunk), 2)
        approx = dot(factor[...], jnp.concatenate([high, low, high], axis=0))
        approx_buf[...] = approx
        merged = drift[...].astype(f32) + error[...].astype(f32)
        new_error[...] = (merged - approx).astype(bf16)

    @pl.when(step < half_blocks)
    def _():
        finish(own)

    @pl.when(step >= half_blocks)
    def _():
        finish(other)

    @pl.when(column_block(step, place) == place[1])
    def _():
        begin = pl.multiple_of(place[0] * (wide // 2), wide // 2)
        update = approx_buf[:, pl.ds(begin, wide // 2)]
        moved = momentum_decay * momentum[...] + update
        new_momentum[...] = moved
        new_weights[...] = weights[...] - outer_rate * (update + momentum_decay * moved)


def finish_step(place, own, other, start, left, drift, error, weights, momentum):
    fixed2 = lambda s, place: (0, 0)
    fixed3 = lambda s, place: (0, 0, 0)
    moving = pl.BlockSpec((rows, wide), lambda s, place: (0, column_block(s, place)))
    state = pl.BlockSpec((rows, wide // 2), fixed2)
    return pl.pallas_call(
        final_kernel,
        grid_spec=pltpu.PrefetchScalarGridSpec(
            num_scalar_prefetch=1,
            grid=(blocks,),
            in_specs=[
                pl.BlockSpec((16, 16, wide), fixed3),
                pl.BlockSpec((16, 16, wide), fixed3),
                pl.BlockSpec((cols, rank), fixed2),
                pl.BlockSpec((rows, rank), fixed2),
                moving,
                moving,
                state,
                state,
            ],
            out_specs=[state, moving, state],
            scratch_shapes=[pltpu.VMEM((rows, 3 * rank), bf16), pltpu.VMEM((rows, wide), f32)],
        ),
        out_shape=[
            jax.ShapeDtypeStruct((rows, wide // 2), f32),
            jax.ShapeDtypeStruct((rows, cols), bf16),
            jax.ShapeDtypeStruct((rows, wide // 2), f32),
        ],
        compiler_params=pltpu.CompilerParams(vmem_limit_bytes=vmem_bytes),
        name="finish",
    )(place, own, other, start, left, drift, error, weights, momentum)


def swap(value):
    return lax.ppermute(value, "core", [(0, 1), (1, 0)])


def spread(value, axes, count):
    copies = jnp.broadcast_to(value[None], (count, *value.shape))
    return lax.all_to_all(copies, axes, 0, 0)


def local(drift, error, start, weights, momentum):
    place = jnp.stack([lax.axis_index("core"), lax.axis_index("z")]).astype(jnp.int32)
    drift, error = drift[0], error[0]
    partial = left_factor(drift, error, start)
    parts = spread(partial + swap(partial), "z", 8)
    keep, send, left = right_factor(place, parts, drift, error)
    summed = lax.all_to_all(keep + swap(send), ("x", "y"), 0, 0).sum(axis=0)
    chunk = spread(summed, "z", 8).sum(axis=0)
    own = spread(chunk, ("x", "y"), 16)
    other = swap(own)
    new_weights, new_error, new_momentum = finish_step(
        place, own, other, start, left, drift, error, weights, momentum
    )
    return new_weights, new_error[None], new_momentum


def solution(mesh):
    fine = Mesh(mesh.devices.reshape(8, 2, 4, 4), ("z", "core", "x", "y"))
    replica, fsdp = ("z", "core"), ("x", "y")
    return jax.shard_map(
        local,
        mesh=fine,
        in_specs=(
            P(replica, fsdp, None),
            P(replica, fsdp, None),
            P(),
            P(fsdp, replica),
            P(fsdp, replica),
        ),
        out_specs=(P(fsdp, replica), P(replica, fsdp, None), P(fsdp, replica)),
        check_vma=False,
    )
```

time: 439 us -> 146 us (0.33)
  waiting for transfers between devices: 271 us -> 19.9 us
  blocking collectives: 110 us -> 67.4 us
  Pallas kernels: 0 us -> 26.7 us
  matrix products: 25.5 us -> 0 us
  starting transfers between devices: 0.04 us -> 14.7 us
  other arithmetic: 16.2 us -> 2.75 us
  between operations: 14.1 us -> 0.7 us
  local copies, waits for them, and re-layouts: 1.79 us -> 13.6 us
    psum x1 -> x0, waiting for transfers between devices: 271 us -> none  [local(): total_q = lax.psum(partial_q, ('replica', 'fsdp'))]
    psum x2 -> x0, blocking collectives: 110 us -> none  [the longest x1 60.7 us: local(): gram = lax.psum(local_gram, 'fsdp')]
    all_to_all x0 -> x3, blocking collectives: none -> 67.4 us  [the longest x2 41.8 us: spread(): return lax.all_to_all(copies, axes, 0, 0)]
    pallas_call x0 -> x3, Pallas kernels: none -> 26.7 us  [the longest x1 16 us: finish_step(): pl.pallas_call(final_kernel, grid_spec=pltpu.PrefetchScalarGridSpec(num_s...]
    dot_general x4 -> x0, matrix products: 25.3 us -> none  [the longest x1 8.91 us: local(): jnp.dot(merged, start, precision=full_prec, preferred_element_type=jnp.fl...]
    all_to_all x0 -> x1, waiting for transfers between devices: none -> 13.7 us  [spread(): return lax.all_to_all(copies, axes, 0, 0)]
    another operation x5 -> x1, other arithmetic: 12.1 us -> 0.07 us  [local(): jnp.stack([lax.axis_index('core'), lax.axis_index('z')]).astype(jnp.int32)]
    unnamed x10 -> x15, local copies, waits for them, and re-layouts: 1.71 us -> 12.7 us
  transfers between devices with their start and end apart: 1 -> 4, of which waited for: 1 -> 4; matrix products, arithmetic and copies ran while one was open for 0% -> 0% of each run, Pallas kernels for 0% -> 0%
where the time goes in v1:
time: 146 us
  blocking collectives  67.4 us (46%)
  Pallas kernels  26.7 us (18%)
  waiting for transfers between devices  19.9 us (14%)
  starting transfers between devices  14.7 us (10%)
  local copies, waits for them, and re-layouts  13.6 us (9%)
  other arithmetic  2.75 us (2%)
    all_to_all x2, blocking collectives, spread(): return lax.all_to_all(copies, axes, 0, 0)  41.8 us
    all_to_all x1, blocking collectives, local(): summed = lax.all_to_all(keep + swap(send), ('x', 'y'), 0, 0).sum(axis=0)  25.6 us
    pallas_call x1, Pallas kernels, finish_step(): pl.pallas_call(final_kernel, grid_spec=pltpu.PrefetchScalarGridSpec(num_s...  16 us
    all_to_all x1, waiting for transfers between devices, spread(): return lax.all_to_all(copies, axes, 0, 0)  13.7 us
    unnamed x15, local copies, waits for them, and re-layouts  12.7 us
    ppermute x3, starting transfers between devices, swap(): return lax.ppermute(value, 'core', [(0, 1), (1, 0)])  8.3 us
    all_to_all x1, starting transfers between devices, spread(): return lax.all_to_all(copies, axes, 0, 0)  6.45 us
    ppermute x3, waiting for transfers between devices, swap(): return lax.ppermute(value, 'core', [(0, 1), (1, 0)])  6.19 us
  transfers between devices with their start and end apart: 4, of which 4 were waited for; matrix products, arithmetic and copies ran while one was open for 0% of the time, Pallas kernels for 0%

profile of v1, /device:TPU:1, one launch (start us, length us, event | category | flops | bytes accessed | tf_op | source)
XLA Modules:
  0.0 145.7 jit_solution(5587933733472285733)
XLA Ops:
  0.6 0.0 copy-start.1
  0.6 5.4 %copy.10.start = f32[10240,64]{1,0:T(8,128)} copy(f32[10240,64]{0,1:T(8,128)} %param.7) | data formatting | bytes 5242880 | tf_op args[2]
  6.0 0.0 copy-done.1
  6.0 0.0 copy-start
  6.0 2.5 %copy-done = f32[10240,64]{1,0:T(8,128)S(1)} copy-done((f32[10240,64]{1,0:T(8,128)S(1)}, f32[10240,64]{1,0:T(8,128)}, u32[]{:S(2)}) %copy-start) | copy-done | bytes 2621464
  8.5 1.9 %copy-done.2 = bf16[1,160,10240]{2,1,0:T(8,128)(2,1)S(1)} copy-done((bf16[1,160,10240]{2,1,0:T(8,128)(2,1)S(1)}, bf16[1,160,10240]{2,1,0:T(8,128)(2,1)}, u32[]{:S(2)}) %copy-start.2) | copy-done | bytes 3276824
  10.4 4.6 %left.1 = f32[80,128]{1,0:T(8,128)S(1)} custom-call(bf16[160,10240]{1,0:T(8,128)(2,1)S(1)} %bitcast.5, bf16[160,10240]{1,0:T(8,128)(2,1)S(1)} %bitcast.8, f32[10240,64]{1,0:T(8,128)S(1)} %copy-done), custom_call_target="tpu_custom_call" | custom-call | tf_op jit(solution)/shard_map/left/pallas_call | solution.py:59
  15.1 3.3 %collective-permute-start = (f32[80,128]{1,0:T(8,128)S(1)}, f32[80,128]{1,0:T(8,128)S(1)}, u32[]{:S(2)}, u32[]{:S(2)}) collective-permute-start(f32[80,128]{1,0:T(8,128)S(1)} %left.1), channel_id=1, source_target_pairs={{0,16},{16,0},{1,17},{17,1},{2,18},{18,2},{3,19},{19,3},{4,20},{20... | collective-permute-start | bytes 122888 | tf_op jit(solution)/shard_map/ppermute | solution.py:233
  18.4 0.9 collective-permute-done
  19.3 0.7 broadcast_in_dim.8
  20.0 6.4 %all-to-all-start = ((f32[8,80,128]{2,1,0:T(8,128)}), f32[8,80,128]{2,1,0:T(8,128)}, u32[]{:S(2)}, u32[]{:S(2)}) async-start(f32[8,80,128]{2,1,0:T(8,128)} %broadcast_in_dim.8), calls=%async_computation | async-start | bytes 655360 | tf_op jit(solution)/shard_map/all_to_all | solution.py:238
  26.5 0.1 pad_add_fusion.place
  26.5 13.7 %all-to-all-done.parts = f32[8,80,128]{2,1,0:T(8,128)} async-done(((f32[8,80,128]{2,1,0:T(8,128)}), f32[8,80,128]{2,1,0:T(8,128)}, u32[]{:S(2)}, u32[]{:S(2)}) %all-to-all-start) | async-done | bytes 327712 | tf_op jit(solution)/shard_map/all_to_all | solution.py:238
  40.2 1.9 %copy-done.3 = bf16[1,160,10240]{2,1,0:T(8,128)(2,1)S(1)} copy-done((bf16[1,160,10240]{2,1,0:T(8,128)(2,1)S(1)}, bf16[1,160,10240]{2,1,0:T(8,128)(2,1)}, u32[]{:S(2)}) %copy-start.3) | copy-done | bytes 3276824
  42.2 6.0 %right.1 = (f32[16,16,1280]{2,1,0:T(8,128)S(1)}, f32[16,16,1280]{2,1,0:T(8,128)S(1)}, f32[160,64]{1,0:T(8,128)S(1)}) custom-call(s32[2]{0:T(128)S(1)} %pad_add_fusion.place, f32[8,80,128]{2,1,0:T(8,128)} %all-to-all-done.parts, bf16[160,10240]{1,0:T(8,128)(2,1)S(1)} %bitcast.6, bf16[160,10240]{1,0:T(8,128)(2,1)S(1)} %bitcast.9), custom_call_target="tpu_custom_call" | custom-call | tf_op jit(solution)/shard_map/right/pallas_call | solution.py:108
  48.2 0.7 collective-permute-start.1
  48.8 2.7 %collective-permute-done.1 = f32[16,16,1280]{2,1,0:T(8,128)S(1)} collective-permute-done((f32[16,16,1280]{2,1,0:T(8,128)S(1)}, f32[16,16,1280]{2,1,0:T(8,128)S(1)}, u32[]{:S(2)}, u32[]{:S(2)}) %collective-permute-start.1) | collective-permute-done | bytes 1310752 | tf_op jit(solution)/shard_map/ppermute | solution.py:233
  51.5 0.1 add.7
  51.6 25.6 %all_to_all.20 = f32[16,16,1280]{2,1,0:T(8,128)} all-to-all(f32[16,16,1280]{2,1,0:T(8,128)S(1)} %add.7), channel_id=1, replica_groups=mesh['z'=8,'core'=2,'x'=4,'y'=4] {'x','y'}, dimensions={0} | all-to-all | bytes 2621440 | tf_op jit(solution)/shard_map/all_to_all | solution.py:247
  77.2 1.4 reduce_sum.18
  78.7 21.0 %all_to_all.21 = f32[8,16,1280]{2,1,0:T(8,128)} all-to-all(f32[8,16,1280]{2,1,0:T(8,128)S(1)} %broadcast_in_dim.9), channel_id=1, replica_groups=mesh['z'=8,'core'=2,'x'=4,'y'=4] {'z'}, dimensions={0} | all-to-all | bytes 1310720 | tf_op jit(solution)/shard_map/all_to_all | solution.py:238
  99.7 1.1 reduce_sum.19
  100.9 0.0 copy-start.4
  100.9 0.1 broadcast_in_dim.10
  101.0 0.0 copy-start.5
  101.0 20.7 %all_to_all.22.own = f32[16,16,1280]{2,1,0:T(8,128)S(1)} all-to-all(f32[16,16,1280]{2,1,0:T(8,128)S(1)} %broadcast_in_dim.10), channel_id=1, replica_groups=mesh['z'=8,'core'=2,'x'=4,'y'=4] {'x','y'}, dimensions={0} | all-to-all | bytes 2621440 | tf_op jit(solution)/shard_map/all_to_all | solution.py:238
  121.7 4.3 %collective-permute-start.2 = (f32[16,16,1280]{2,1,0:T(8,128)S(1)}, f32[16,16,1280]{2,1,0:T(8,128)S(1)}, u32[]{:S(2)}, u32[]{:S(2)}) collective-permute-start(f32[16,16,1280]{2,1,0:T(8,128)S(1)} %all_to_all.22.own), channel_id=1, source_target_pairs={{0,16},{16,0},{1,17},{17,1},{2,18},{18,2},{3,19},{19,3},{4,20},{20... | collective-permute-start | bytes 3932168 | tf_op jit(solution)/shard_map/ppermute | solution.py:233
  126.1 2.7 %collective-permute-done.2.other = f32[16,16,1280]{2,1,0:T(8,128)S(1)} collective-permute-done((f32[16,16,1280]{2,1,0:T(8,128)S(1)}, f32[16,16,1280]{2,1,0:T(8,128)S(1)}, u32[]{:S(2)}, u32[]{:S(2)}) %collective-permute-start.2) | collective-permute-done | bytes 1310752 | tf_op jit(solution)/shard_map/ppermute | solution.py:233
  128.7 0.0 copy-done.4
  128.7 0.0 copy-done.5
  128.7 1.0 copy-done.6
  129.7 16.0 %finish.1 = (f32[160,640]{1,0:T(8,128)}, bf16[160,10240]{1,0:T(8,128)(2,1)}, f32[160,640]{1,0:T(8,128)}) custom-call(s32[2]{0:T(128)S(1)} %pad_add_fusion.place, f32[16,16,1280]{2,1,0:T(8,128)S(1)} %all_to_all.22.own, f32[16,16,1280]{2,1,0:T(8,128)S(1)} %collective-permute-done.2.other, f32[10240,64]{1,0:T(8,128)} %copy.10.start, ...), custom_call_target="tpu_custom_call" | custom-call | tf_op jit(solution)/shard_map/finish/pallas_call | solution.py:204
  (5 shorter events, 0.1 us)
Async XLA Ops:
  0.6 5.4 %copy-start.1 = (bf16[1,160,10240]{2,1,0:T(8,128)(2,1)S(1)}, bf16[1,160,10240]{2,1,0:T(8,128)(2,1)}, u32[]{:S(2)}) copy-start(bf16[1,160,10240]{2,1,0:T(8,128)(2,1)} %param.5) | copy-start | bytes 9830404
  6.0 2.5 %copy-start = (f32[10240,64]{1,0:T(8,128)S(1)}, f32[10240,64]{1,0:T(8,128)}, u32[]{:S(2)}) copy-start(f32[10240,64]{1,0:T(8,128)} %copy.10.start) | copy-start | bytes 7864324
  8.5 1.9 %copy-start.2 = (bf16[1,160,10240]{2,1,0:T(8,128)(2,1)S(1)}, bf16[1,160,10240]{2,1,0:T(8,128)(2,1)}, u32[]{:S(2)}) copy-start(bf16[1,160,10240]{2,1,0:T(8,128)(2,1)} %param.6) | copy-start | bytes 9830404
  15.1 4.2 %collective-permute-start = (f32[80,128]{1,0:T(8,128)S(1)}, f32[80,128]{1,0:T(8,128)S(1)}, u32[]{:S(2)}, u32[]{:S(2)}) collective-permute-start(f32[80,128]{1,0:T(8,128)S(1)} %left.1), channel_id=1, source_target_pairs={{0,16},{16,0},{1,17},{17,1},{2,18},{18,2},{3,19},{19,3},{4,20},{20... | collective-permute-start | bytes 122888 | tf_op jit(solution)/shard_map/ppermute | solution.py:233
  20.0 20.2 %all-to-all-start = ((f32[8,80,128]{2,1,0:T(8,128)}), f32[8,80,128]{2,1,0:T(8,128)}, u32[]{:S(2)}, u32[]{:S(2)}) async-start(f32[8,80,128]{2,1,0:T(8,128)} %broadcast_in_dim.8), calls=%async_computation | async-start | bytes 655360 | tf_op jit(solution)/shard_map/all_to_all | solution.py:238
  40.2 1.9 %copy-start.3 = (bf16[1,160,10240]{2,1,0:T(8,128)(2,1)S(1)}, bf16[1,160,10240]{2,1,0:T(8,128)(2,1)}, u32[]{:S(2)}) copy-start(bf16[1,160,10240]{2,1,0:T(8,128)(2,1)} %param.6) | copy-start | bytes 9830404
  48.2 3.3 %collective-permute-start.1 = (f32[16,16,1280]{2,1,0:T(8,128)S(1)}, f32[16,16,1280]{2,1,0:T(8,128)S(1)}, u32[]{:S(2)}, u32[]{:S(2)}) collective-permute-start(f32[16,16,1280]{2,1,0:T(8,128)S(1)} %get-tuple-element.10), channel_id=1, source_target_pairs={{0,16},{16,0},{1,17},{17,1},{2,18},{18,2},{3,19},{19,3},{4,20},{20... | collective-permute-start | bytes 3932168 | tf_op jit(solution)/shard_map/ppermute | solution.py:233
  100.9 27.9 %copy-start.4 = (bf16[1,160,10240]{2,1,0:T(8,128)(2,1)S(1)}, bf16[1,160,10240]{2,1,0:T(8,128)(2,1)}, u32[]{:S(2)}) copy-start(bf16[1,160,10240]{2,1,0:T(8,128)(2,1)} %param.6) | copy-start | bytes 9830404
  101.0 27.7 %copy-start.5 = (f32[160,640]{1,0:T(8,128)S(1)}, f32[160,640]{1,0:T(8,128)}, u32[]{:S(2)}) copy-start(f32[160,640]{1,0:T(8,128)} %weights.1) | copy-start | bytes 1228804
  121.7 7.0 %collective-permute-start.2 = (f32[16,16,1280]{2,1,0:T(8,128)S(1)}, f32[16,16,1280]{2,1,0:T(8,128)S(1)}, u32[]{:S(2)}, u32[]{:S(2)}) collective-permute-start(f32[16,16,1280]{2,1,0:T(8,128)S(1)} %all_to_all.22.own), channel_id=1, source_target_pairs={{0,16},{16,0},{1,17},{17,1},{2,18},{18,2},{3,19},{19,3},{4,20},{20... | collective-permute-start | bytes 3932168 | tf_op jit(solution)/shard_map/ppermute | solution.py:233
  128.7 1.0 copy-start.6

commit v2 on v1

v2 whole, which is shorter than its diff:
```python
import jax
import jax.numpy as jnp
from jax import lax
from jax.experimental import pallas as pl
from jax.experimental.pallas import tpu as pltpu
from jax.sharding import Mesh, PartitionSpec as P

outer_rate = 0.7
momentum_decay = 0.9

rows = 160
cols = 10240
half_cols = cols // 2
rank = 64
narrow = 640
wide = 1280
blocks = 8
groups = 16
f32 = jnp.float32
bf16 = jnp.bfloat16
exact = lax.Precision.HIGHEST
mib = 1024 * 1024


def split(value, pieces):
    out = []
    for _ in range(pieces - 1):
        head = value.astype(bf16)
        out.append(head)
        value = value - head.astype(f32)
    out.append(value.astype(bf16))
    return out


def dot(a, b):
    return jnp.dot(a, b, preferred_element_type=f32)


def dot_rows(a, b):
    return lax.dot_general(a, b, (((1,), (1,)), ((), ())), preferred_element_type=f32)


def params(size):
    return pltpu.CompilerParams(vmem_limit_bytes=size * mib)


def cost(flops, moved):
    return pl.CostEstimate(flops=flops, bytes_accessed=moved, transcendentals=0)


def left_kernel(place, drift, error, start, out, send, acc):
    step = pl.program_id(0)
    both = jnp.concatenate([drift[...], error[...]], axis=0)
    factor = jnp.concatenate(split(start[...], 3), axis=0)
    term = dot_rows(both, factor)
    begin = pl.multiple_of((1 - place[0]) * narrow, narrow)
    theirs = pl.ds(begin, narrow)
    send[...] = drift[:, theirs].astype(f32) + error[:, theirs].astype(f32)

    @pl.when(step == 0)
    def _():
        acc[...] = term

    @pl.when(step > 0)
    def _():
        acc[...] += term

    @pl.when(step == blocks - 1)
    def _():
        total = acc[:rows, :] + acc[rows:, :]
        left = total[:, :rank] + total[:, rank : 2 * rank] + total[:, 2 * rank :]
        packed = jnp.concatenate([left[: rows // 2], left[rows // 2 :]], axis=1)
        for z in range(8):
            out[z] = packed


def left_factor(place, drift, error, start):
    return pl.pallas_call(
        left_kernel,
        grid_spec=pltpu.PrefetchScalarGridSpec(
            num_scalar_prefetch=1,
            grid=(blocks,),
            in_specs=[
                pl.BlockSpec((rows, wide), lambda s, place: (0, s)),
                pl.BlockSpec((rows, wide), lambda s, place: (0, s)),
                pl.BlockSpec((rank, wide), lambda s, place: (0, s)),
            ],
            out_specs=[
                pl.BlockSpec((8, rows // 2, 2 * rank), lambda s, place: (0, 0, 0)),
                pl.BlockSpec((rows, narrow), lambda s, place: (0, s)),
            ],
            scratch_shapes=[pltpu.VMEM((2 * rows, 3 * rank), f32)],
        ),
        out_shape=[
            jax.ShapeDtypeStruct((8, rows // 2, 2 * rank), f32),
            jax.ShapeDtypeStruct((rows, half_cols), f32),
        ],
        compiler_params=params(56),
        cost_estimate=cost(2 * rows * cols * rank, 13_000_000),
        name="left",
    )(place, drift, error, start)


def right_kernel(
    place, mine, theirs, drift0, drift1, error0, error1, received, out, left_out, pieces, gram
):
    step = pl.program_id(0)

    @pl.when(step == 0)
    def _():
        total = (jnp.sum(mine[...], axis=0) + jnp.sum(theirs[...], axis=0)) * (1.0 / groups)
        left = jnp.concatenate([total[:, :rank], total[:, rank:]], axis=0)
        left_out[...] = left
        turned = left.T
        pieces[...] = jnp.concatenate(split(turned, 3), axis=0)
        gram[...] = jnp.dot(turned, left, precision=exact, preferred_element_type=f32)
        own = gram[pl.ds(pl.multiple_of(place[0] * 32, 32), 32), :]
        packed = jnp.concatenate([own[:16], own[16:]], axis=1)
        for j in range(16):
            out[j, :, wide:] = packed

    first = drift0[...].astype(f32) + error0[...].astype(f32)
    second = drift1[...].astype(f32) + error1[...].astype(f32)
    merged = jnp.concatenate([first, second], axis=1) + received[...]
    high, low = split(merged, 2)
    term = dot(pieces[...], high) + dot(pieces[...], low)
    block = term[:rank] + term[rank : 2 * rank] + term[2 * rank :]
    for x in range(4):
        out[4 * x + step, :, :wide] = block[16 * x : 16 * (x + 1)]


def right_factor(place, mine, theirs, drift, error, received):
    fixed3 = lambda s, place: (0, 0, 0)
    even = pl.BlockSpec((rows, narrow), lambda s, place: (0, 4 * s + place[0]))
    odd = pl.BlockSpec((rows, narrow), lambda s, place: (0, 4 * s + 2 + place[0]))
    return pl.pallas_call(
        right_kernel,
        grid_spec=pltpu.PrefetchScalarGridSpec(
            num_scalar_prefetch=1,
            grid=(4,),
            in_specs=[
                pl.BlockSpec((8, rows // 2, 2 * rank), fixed3),
                pl.BlockSpec((8, rows // 2, 2 * rank), fixed3),
                even,
                odd,
                even,
                odd,
                pl.BlockSpec((rows, wide), lambda s, place: (0, s)),
            ],
            out_specs=[
                pl.BlockSpec((16, 16, wide + 128), fixed3),
                pl.BlockSpec((rows, rank), lambda s, place: (0, 0)),
            ],
            scratch_shapes=[pltpu.VMEM((3 * rank, rows), bf16), pltpu.VMEM((rank, rank), f32)],
        ),
        out_shape=[
            jax.ShapeDtypeStruct((16, 16, wide + 128), f32),
            jax.ShapeDtypeStruct((rows, rank), f32),
        ],
        compiler_params=params(16),
        cost_estimate=cost(2 * rows * cols * rank, 9_000_000),
        name="right",
    )(place, mine, theirs, drift, drift, error, error, received)


def inverse(gram):
    eye = (
        lax.broadcasted_iota(jnp.int32, (rank, rank), 0)
        == lax.broadcasted_iota(jnp.int32, (rank, rank), 1)
    ).astype(f32)
    work = jnp.concatenate([gram, eye], axis=1)
    row_id = lax.broadcasted_iota(jnp.int32, (rank, 2 * rank), 0)
    for k in range(rank):
        pivot = work[k : k + 1, :] / work[k : k + 1, k : k + 1]
        work = jnp.where(row_id == k, pivot, work - work[:, k : k + 1] * pivot)
    return work[:, rank:]


def solve_kernel(place, mine, theirs, left, out):
    def unpack(packed):
        return jnp.concatenate([packed[:, :rank], packed[:, rank:]], axis=0)

    own, other = unpack(mine[...]), unpack(theirs[...])
    first = place[0] == 0
    gram = jnp.concatenate([jnp.where(first, own, other), jnp.where(first, other, own)], axis=0)
    solved = jnp.dot(
        left[...], inverse(gram) * (1.0 / groups), precision=exact, preferred_element_type=f32
    )
    high, low = split(solved, 2)
    out[...] = jnp.concatenate([high, high, low], axis=1)


def solve(place, mine, theirs, left):
    vmem = pl.BlockSpec(memory_space=pltpu.VMEM)
    return pl.pallas_call(
        solve_kernel,
        in_specs=[pl.BlockSpec(memory_space=pltpu.SMEM), vmem, vmem, vmem],
        out_specs=vmem,
        out_shape=jax.ShapeDtypeStruct((rows, 3 * rank), bf16),
        compiler_params=params(8),
        cost_estimate=cost(0, 30_000_000),
        name="solve",
    )(place, mine, theirs, left)


def apply_factor(factor, right, drift, error, new_error):
    step = pl.program_id(0)
    y, odd = step // 2, lax.rem(step, 2)
    lanes = pl.ds(pl.multiple_of(odd * narrow, narrow), narrow)
    block = jnp.concatenate([right[4 * x + y, :, lanes] for x in range(4)], axis=0)
    high, low = split(block, 2)
    approx = dot(factor[...], jnp.concatenate([high, low, high], axis=0))
    merged = drift[...].astype(f32) + error[...].astype(f32)
    new_error[...] = (merged - approx).astype(bf16)
    return approx


def own_kernel(
    place, factor, right, drift, error, weights, momentum, new_error, new_weights, new_momentum
):
    approx = apply_factor(factor, right, drift, error, new_error)

    @pl.when(pl.program_id(0) == place[1])
    def _():
        moved = momentum_decay * momentum[...] + approx
        new_momentum[...] = moved
        new_weights[...] = weights[...] - outer_rate * (approx + momentum_decay * moved)


def other_kernel(place, factor, right, drift, error, partial, new_error):
    apply_factor(factor, right, drift, error, new_error)


fixed2 = lambda s, place: (0, 0)
fixed3 = lambda s, place: (0, 0, 0)


def finish_own(place, factor, right, drift, error, weights, momentum):
    block = pl.BlockSpec((rows, narrow), lambda s, place: (0, 2 * s + place[0]))
    state = pl.BlockSpec((rows, narrow), fixed2)
    return pl.pallas_call(
        own_kernel,
        grid_spec=pltpu.PrefetchScalarGridSpec(
            num_scalar_prefetch=1,
            grid=(blocks,),
            in_specs=[
                pl.BlockSpec((rows, 3 * rank), fixed2),
                pl.BlockSpec((16, 16, wide), fixed3),
                block,
                block,
                state,
                state,
            ],
            out_specs=[block, state, state],
        ),
        out_shape=[
            jax.ShapeDtypeStruct((rows, cols), bf16),
            jax.ShapeDtypeStruct((rows, narrow), f32),
            jax.ShapeDtypeStruct((rows, narrow), f32),
        ],
        compiler_params=params(16),
        cost_estimate=cost(rows * cols * rank, 8_000_000),
        name="own",
    )(place, factor, right, drift, error, weights, momentum)


def finish_other(place, factor, right, drift, error, partial):
    block = pl.BlockSpec((rows, narrow), lambda s, place: (0, 2 * s + 1 - place[0]))
    return pl.pallas_call(
        other_kernel,
        grid_spec=pltpu.PrefetchScalarGridSpec(
            num_scalar_prefetch=1,
            grid=(blocks,),
            in_specs=[
                pl.BlockSpec((rows, 3 * rank), fixed2),
                pl.BlockSpec((16, 16, wide), fixed3),
                block,
                block,
                pl.BlockSpec(memory_space=pl.ANY),
            ],
            out_specs=block,
        ),
        out_shape=jax.ShapeDtypeStruct((rows, cols), bf16),
        input_output_aliases={5: 0},
        compiler_params=params(16),
        cost_estimate=cost(rows * cols * rank, 8_000_000),
        name="other",
    )(place, factor, right, drift, error, partial)


def swap(value):
    return lax.ppermute(value, "core", [(0, 1), (1, 0)])


def spread(value, axes, count):
    copies = jnp.broadcast_to(value[None], (count, *value.shape))
    return lax.all_to_all(copies, axes, 0, 0)


def local(drift, error, start, weights, momentum):
    place = jnp.stack([lax.axis_index("core"), lax.axis_index("z")]).astype(jnp.int32)
    drift, error = drift[0], error[0]
    copies, sent = left_factor(place, drift, error, start.T)
    received = swap(sent)
    mine = lax.all_to_all(copies, "z", 0, 0)
    chunks, left = right_factor(place, mine, swap(mine), drift, error, received)
    summed = lax.all_to_all(chunks, ("x", "y"), 0, 0).sum(axis=0)
    gram = summed[:, wide:]
    factor = solve(place, gram, swap(gram), left)
    chunk = spread(summed[:, :wide], "z", 8).sum(axis=0)
    own = spread(chunk, ("x", "y"), 16)
    other = swap(own)
    partial, new_weights, new_momentum = finish_own(
        place, factor, own, drift, error, weights, momentum
    )
    new_error = finish_other(place, factor, other, drift, error, partial)
    return new_weights, new_error[None], new_momentum


def solution(mesh):
    fine = Mesh(mesh.devices.reshape(8, 2, 4, 4), ("z", "core", "x", "y"))
    replica, fsdp = ("z", "core"), ("x", "y")
    return jax.shard_map(
        local,
        mesh=fine,
        in_specs=(
            P(replica, fsdp, None),
            P(replica, fsdp, None),
            P(),
            P(fsdp, replica),
            P(fsdp, replica),
        ),
        out_specs=(P(fsdp, replica), P(replica, fsdp, None), P(fsdp, replica)),
        check_vma=False,
    )
```

time: 146 us -> 136 us (0.932)
  blocking collectives: 67.4 us -> 88.9 us
  waiting for transfers between devices: 19.9 us -> 3.93 us
  local copies, waits for them, and re-layouts: 13.6 us -> 0.2 us
  starting transfers between devices: 14.7 us -> 8.02 us
  Pallas kernels: 26.7 us -> 30.4 us
    all_to_all x1 -> x2, blocking collectives: 25.6 us -> 46.5 us  [the longest x1 26.3 us: local(): summed = lax.all_to_all(chunks, ('x', 'y'), 0, 0).sum(axis=0)]
    all_to_all x1 -> x0, waiting for transfers between devices: 13.7 us -> none  [spread(): return lax.all_to_all(copies, axes, 0, 0)]
    unnamed x15 -> x12, local copies, waits for them, and re-layouts: 12.7 us -> 0.03 us
    all_to_all x1 -> x0, starting transfers between devices: 6.45 us -> none  [spread(): return lax.all_to_all(copies, axes, 0, 0)]
    pallas_call x2 -> x4, Pallas kernels: 20.6 us -> 26.6 us  [the longest x1 10.4 us: left_factor(): pl.pallas_call(left_kernel, grid_spec=pltpu.PrefetchScalarGridSpec(num_sc...]
    ppermute x3 -> x4, waiting for transfers between devices: 6.19 us -> 3.93 us  [swap(): return lax.ppermute(value, 'core', [(0, 1), (1, 0)])]
    pallas_call x1, Pallas kernels: 6.01 us -> 3.84 us  [right_factor(): pl.pallas_call(right_kernel, grid_spec=pltpu.PrefetchScalarGridSpec(num_s...]
    ppermute x3 -> x4, starting transfers between devices: 8.3 us -> 8.02 us  [swap(): return lax.ppermute(value, 'core', [(0, 1), (1, 0)])]
  transfers between devices with their start and end apart: 4 -> 4, of which waited for: 4 -> 2; matrix products, arithmetic and copies ran while one was open for 0% -> 0% of each run, Pallas kernels for 0% -> 9%
where the time goes in v2:
time: 136 us; the launch traced here: 135 us
  blocking collectives  88.9 us (65%)
  Pallas kernels  30.4 us (22%)
  starting transfers between devices  8.02 us (6%)
  waiting for transfers between devices  3.93 us (3%)
  other arithmetic  3.15 us (2%)
    all_to_all x2, blocking collectives, spread(): return lax.all_to_all(copies, axes, 0, 0)  42.4 us
    all_to_all x1, blocking collectives, local(): summed = lax.all_to_all(chunks, ('x', 'y'), 0, 0).sum(axis=0)  26.3 us
    all_to_all x1, blocking collectives, local(): mine = lax.all_to_all(copies, 'z', 0, 0)  20.2 us
    pallas_call x1, Pallas kernels, left_factor(): pl.pallas_call(left_kernel, grid_spec=pltpu.PrefetchScalarGridSpec(num_sc...  10.4 us
    ppermute x4, starting transfers between devices, swap(): return lax.ppermute(value, 'core', [(0, 1), (1, 0)])  8.02 us
    pallas_call x1, Pallas kernels, solve(): pl.pallas_call(solve_kernel, in_specs=[pl.BlockSpec(memory_space=pltpu.SM...  6.37 us
    pallas_call x1, Pallas kernels, finish_own(): pl.pallas_call(own_kernel, grid_spec=pltpu.PrefetchScalarGridSpec(num_sca...  5.15 us
    pallas_call x1, Pallas kernels, finish_other(): pl.pallas_call(other_kernel, grid_spec=pltpu.PrefetchScalarGridSpec(num_s...  4.71 us
  transfers between devices with their start and end apart: 4, of which 2 were waited for; matrix products, arithmetic and copies ran while one was open for 0% of the time, Pallas kernels for 9%

profile of v2, /device:TPU:1, one launch (start us, length us, event | category | flops | bytes accessed | tf_op | source)
XLA Modules:
  0.0 135.4 jit_solution(9340364705197786844)
XLA Ops:
  0.6 0.6 pad_add_fusion.place
  1.2 0.0 copy-start
  1.2 0.0 copy-start.1
  1.2 10.4 %left.1 = (f32[8,80,128]{2,1,0:T(8,128)}, f32[160,5120]{1,0:T(8,128)}) custom-call(s32[2]{0:T(128)} %pad_add_fusion.place, bf16[160,10240]{1,0:T(8,128)(2,1)} %bitcast.6, bf16[160,10240]{1,0:T(8,128)(2,1)} %bitcast.11, f32[64,10240]{1,0:T(8,128)} %bitcast.17), custom_call_target="tpu_custom_call" | custom-call | flops 209715200 | bytes 13000000 | tf_op jit(solution)/shard_map/left/pallas_call | solution.py:78
  11.6 3.2 %collective-permute-start.1 = (f32[160,5120]{1,0:T(8,128)}, f32[160,5120]{1,0:T(8,128)S(1)}, u32[]{:S(2)}, u32[]{:S(2)}) collective-permute-start(f32[160,5120]{1,0:T(8,128)} %get-tuple-element.11), channel_id=1, source_target_pairs={{0,16},{16,0},{1,17},{17,1},{2,18},{18,2},{3,19},{19,3},{4,20},{20... | collective-permute-start | bytes 9830408 | tf_op jit(solution)/shard_map/ppermute | solution.py:292
  14.8 20.2 %all_to_all.20.mine = f32[8,80,128]{2,1,0:T(8,128)S(1)} all-to-all(f32[8,80,128]{2,1,0:T(8,128)} %get-tuple-element.10), channel_id=1, replica_groups=mesh['z'=8,'core'=2,'x'=4,'y'=4] {'z'}, dimensions={0} | all-to-all | bytes 655360 | tf_op jit(solution)/shard_map/all_to_all | solution.py:305
  35.0 0.5 collective-permute-start
  35.5 1.3 collective-permute-done.theirs
  36.8 0.0 collective-permute-done.1.received
  36.8 0.0 copy-done
  36.8 0.0 copy-done.1
  36.8 0.0 copy-done.5
  36.8 3.8 %right.1 = (f32[16,16,1408]{2,1,0:T(8,128)S(1)}, f32[160,64]{1,0:T(8,128)S(1)}) custom-call(s32[2]{0:T(128)S(1)} %copy-done.5, f32[8,80,128]{2,1,0:T(8,128)S(1)} %all_to_all.20.mine, f32[8,80,128]{2,1,0:T(8,128)S(1)} %collective-permute-done.theirs, bf16[160,10240]{1,0:T(8,128)(2,1)S(1)} %bitcast.7, bf16[160,10240]{1,0:T(8,128)(2,1)S(1)} %bitcast.8, ...), custom_call_target="tpu_custom_call" | custom-call | flops 209715200 | bytes 9000000 | tf_op jit(solution)/shard_map/right/pallas_call | solution.py:136
  40.6 26.3 %all_to_all.21 = f32[16,16,1408]{2,1,0:T(8,128)} all-to-all(f32[16,16,1408]{2,1,0:T(8,128)S(1)} %get-tuple-element.12), channel_id=1, replica_groups=mesh['z'=8,'core'=2,'x'=4,'y'=4] {'x','y'}, dimensions={0} | all-to-all | bytes 2883584 | tf_op jit(solution)/shard_map/all_to_all | solution.py:307
  66.9 1.4 %reduce_sum.18 = f32[16,1408]{1,0:T(8,128)S(1)} reduce(f32[16,16,1408]{2,1,0:T(8,128)} %all_to_all.21, f32[]{:T(128)} %constant.13.clone.1), dimensions={0}, to_apply=%region_0.0 | reduce | flops 337920 | bytes 1531908 | tf_op jit(solution)/shard_map/reduce_sum | solution.py:307
  68.5 20.5 %all_to_all.22 = f32[8,16,1280]{2,1,0:T(8,128)} all-to-all(f32[8,16,1280]{2,1,0:T(8,128)S(1)} %broadcast_in_dim.6), channel_id=1, replica_groups=mesh['z'=8,'core'=2,'x'=4,'y'=4] {'z'}, dimensions={0} | all-to-all | bytes 1310720 | tf_op jit(solution)/shard_map/all_to_all | solution.py:297
  89.0 1.1 reduce_sum.19
  90.1 0.0 copy-start.2
  90.1 0.0 copy-start.3
  90.1 0.0 copy-start.4
  90.1 0.1 broadcast_in_dim.7
  90.2 21.9 %all_to_all.23.right = f32[16,16,1280]{2,1,0:T(8,128)S(1)} all-to-all(f32[16,16,1280]{2,1,0:T(8,128)S(1)} %broadcast_in_dim.7), channel_id=1, replica_groups=mesh['z'=8,'core'=2,'x'=4,'y'=4] {'x','y'}, dimensions={0} | all-to-all | bytes 2621440 | tf_op jit(solution)/shard_map/all_to_all | solution.py:297
  112.1 4.3 %collective-permute-start.3 = (f32[16,16,1280]{2,1,0:T(8,128)S(1)}, f32[16,16,1280]{2,1,0:T(8,128)S(1)}, u32[]{:S(2)}, u32[]{:S(2)}) collective-permute-start(f32[16,16,1280]{2,1,0:T(8,128)S(1)} %all_to_all.23.right), channel_id=1, source_target_pairs={{0,16},{16,0},{1,17},{17,1},{2,18},{18,2},{3,19},{19,3},{4,20},{20... | collective-permute-start | bytes 3932168 | tf_op jit(solution)/shard_map/ppermute | solution.py:292
  116.4 0.0 collective-permute-start.2
  116.4 2.7 %collective-permute-done.2.theirs = f32[16,128]{1,0:T(8,128)S(1)} collective-permute-done((f32[16,128]{1,0:T(8,128)S(1)}, f32[16,128]{1,0:T(8,128)S(1)}, u32[]{:S(2)}, u32[]{:S(2)}) %collective-permute-start.2) | collective-permute-done | bytes 8224 | tf_op jit(solution)/shard_map/ppermute | solution.py:292
  119.1 6.4 %solve.1.factor = bf16[160,192]{1,0:T(8,128)(2,1)S(1)} custom-call(s32[2]{0:T(128)S(1)} %copy-done.5, f32[16,128]{1,0:T(8,128)S(1)} %slice.8.mine, f32[16,128]{1,0:T(8,128)S(1)} %collective-permute-done.2.theirs, f32[160,64]{1,0:T(8,128)S(1)} %get-tuple-element.13.left), custom_call_target="tpu_custom_call" | custom-call | bytes 30000000 | tf_op jit(solution)/shard_map/solve/pallas_call | solution.py:195
  125.5 0.0 copy-done.2
  125.5 0.0 copy-done.3
  125.5 0.0 copy-done.4
  125.5 5.1 %own.1 = (bf16[160,10240]{1,0:T(8,128)(2,1)}, f32[160,640]{1,0:T(8,128)}, f32[160,640]{1,0:T(8,128)}) custom-call(s32[2]{0:T(128)S(1)} %copy-done.5, bf16[160,192]{1,0:T(8,128)(2,1)S(1)} %solve.1.factor, f32[16,16,1280]{2,1,0:T(8,128)S(1)} %all_to_all.23.right, bf16[160,10240]{1,0:T(8,128)(2,1)S(1)} %bitcast.9, bf16[160,10240]{1,0:T(8,128)(2,1)S(1)} %bitcast.14, ...), custom_call_target="tpu_custom_call" | custom-call | flops 104857600 | bytes 8000000 | tf_op jit(solution)/shard_map/own/pallas_call | solution.py:241
  130.7 0.0 collective-permute-done.3.right
  130.7 4.7 %other.1 = bf16[160,10240]{1,0:T(8,128)(2,1)} custom-call(s32[2]{0:T(128)S(1)} %copy-done.5, bf16[160,192]{1,0:T(8,128)(2,1)S(1)} %solve.1.factor, f32[16,16,1280]{2,1,0:T(8,128)S(1)} %collective-permute-done.3.right, bf16[160,10240]{1,0:T(8,128)(2,1)S(1)} %bitcast.10, bf16[160,10240]{1,0:T(8,128)(2,1)S(1)} %bitcast.15, ...), custom_call_target="tpu_custom_call", output_to_operand_aliasing={{}: (5, {})} | custom-call | flops 104857600 | bytes 8000000 | tf_op jit(solution)/shard_map/other/pallas_call | solution.py:269
  (4 shorter events, 0.1 us)
Async XLA Ops:
  1.2 35.5 %copy-start = (bf16[1,160,10240]{2,1,0:T(8,128)(2,1)S(1)}, bf16[1,160,10240]{2,1,0:T(8,128)(2,1)}, u32[]{:S(2)}) copy-start(bf16[1,160,10240]{2,1,0:T(8,128)(2,1)} %param.5) | copy-start | bytes 9830404
  1.2 35.5 %copy-start.1 = (bf16[1,160,10240]{2,1,0:T(8,128)(2,1)S(1)}, bf16[1,160,10240]{2,1,0:T(8,128)(2,1)}, u32[]{:S(2)}) copy-start(bf16[1,160,10240]{2,1,0:T(8,128)(2,1)} %param.6) | copy-start | bytes 9830404
  1.2 35.5 %copy-start.5 = (s32[2]{0:T(128)S(1)}, s32[2]{0:T(128)}, u32[]{:S(2)}) copy-start(s32[2]{0:T(128)} %pad_add_fusion.place) | copy-start | bytes 28
  11.6 25.2 %collective-permute-start.1 = (f32[160,5120]{1,0:T(8,128)}, f32[160,5120]{1,0:T(8,128)S(1)}, u32[]{:S(2)}, u32[]{:S(2)}) collective-permute-start(f32[160,5120]{1,0:T(8,128)} %get-tuple-element.11), channel_id=1, source_target_pairs={{0,16},{16,0},{1,17},{17,1},{2,18},{18,2},{3,19},{19,3},{4,20},{20... | collective-permute-start | bytes 9830408 | tf_op jit(solution)/shard_map/ppermute | solution.py:292
  35.0 1.7 %collective-permute-start = (f32[8,80,128]{2,1,0:T(8,128)S(1)}, f32[8,80,128]{2,1,0:T(8,128)S(1)}, u32[]{:S(2)}, u32[]{:S(2)}) collective-permute-start(f32[8,80,128]{2,1,0:T(8,128)S(1)} %all_to_all.20.mine), channel_id=1, source_target_pairs={{0,16},{16,0},{1,17},{17,1},{2,18},{18,2},{3,19},{19,3},{4,20},{20... | collective-permute-start | bytes 983048 | tf_op jit(solution)/shard_map/ppermute | solution.py:292
  90.1 35.4 %copy-start.2 = (bf16[1,160,10240]{2,1,0:T(8,128)(2,1)S(1)}, bf16[1,160,10240]{2,1,0:T(8,128)(2,1)}, u32[]{:S(2)}) copy-start(bf16[1,160,10240]{2,1,0:T(8,128)(2,1)} %param.6) | copy-start | bytes 9830404
  90.1 35.4 %copy-start.3 = (f32[160,640]{1,0:T(8,128)S(1)}, f32[160,640]{1,0:T(8,128)}, u32[]{:S(2)}) copy-start(f32[160,640]{1,0:T(8,128)} %weights.1) | copy-start | bytes 1228804
  90.1 35.4 %copy-start.4 = (f32[160,640]{1,0:T(8,128)S(1)}, f32[160,640]{1,0:T(8,128)}, u32[]{:S(2)}) copy-start(f32[160,640]{1,0:T(8,128)} %momentum.1) | copy-start | bytes 1228804
  112.1 18.5 %collective-permute-start.3 = (f32[16,16,1280]{2,1,0:T(8,128)S(1)}, f32[16,16,1280]{2,1,0:T(8,128)S(1)}, u32[]{:S(2)}, u32[]{:S(2)}) collective-permute-start(f32[16,16,1280]{2,1,0:T(8,128)S(1)} %all_to_all.23.right), channel_id=1, source_target_pairs={{0,16},{16,0},{1,17},{17,1},{2,18},{18,2},{3,19},{19,3},{4,20},{20... | collective-permute-start | bytes 3932168 | tf_op jit(solution)/shard_map/ppermute | solution.py:292
  116.4 2.7 %collective-permute-start.2 = (f32[16,128]{1,0:T(8,128)S(1)}, f32[16,128]{1,0:T(8,128)S(1)}, u32[]{:S(2)}, u32[]{:S(2)}) collective-permute-start(f32[16,128]{1,0:T(8,128)S(1)} %slice.8.mine), channel_id=1, source_target_pairs={{0,16},{16,0},{1,17},{17,1},{2,18},{18,2},{3,19},{19,3},{4,20},{20... | collective-permute-start | bytes 24584 | tf_op jit(solution)/shard_map/ppermute | solution.py:292

commit v3 on v0

v3 whole, which is shorter than its diff:
```python
import jax
import jax.numpy as jnp
from jax import lax
from jax.experimental import pallas as pl
from jax.experimental.pallas import tpu as pltpu
from jax.sharding import Mesh, PartitionSpec as P

outer_rate = 0.7
momentum_decay = 0.9

rows = 160
cols = 10240
rank = 64
narrow = 640
wide = 1280
blocks = 8
groups = 16
tall = 160
f32 = jnp.float32
bf16 = jnp.bfloat16
exact = lax.Precision.HIGHEST
mib = 1024 * 1024
hbm = pl.BlockSpec(memory_space=pltpu.HBM)
vmem = pl.BlockSpec(memory_space=pltpu.VMEM)


def split(value, pieces):
    out = []
    for _ in range(pieces - 1):
        head = value.astype(bf16)
        out.append(head)
        value = value - head.astype(f32)
    out.append(value.astype(bf16))
    return out


def dot(a, b):
    return jnp.dot(a, b, preferred_element_type=f32)


def dot_rows(a, b):
    return lax.dot_general(a, b, (((1,), (1,)), ((), ())), preferred_element_type=f32)


def call(kernel, name, size, moved, **kwargs):
    return pl.pallas_call(
        kernel,
        name=name,
        compiler_params=pltpu.CompilerParams(vmem_limit_bytes=size * mib),
        cost_estimate=pl.CostEstimate(flops=0, bytes_accessed=moved, transcendentals=0),
        **kwargs,
    )


def shape(*dims, dtype=f32):
    return jax.ShapeDtypeStruct(dims, dtype)


def left_kernel(drift, error, start, out, keep, send, drifts, errors, starts, acc, sems):
    first = lax.axis_index("core") == 0
    copies = []
    for i in range(blocks):
        lanes = pl.ds(i * wide, wide)
        mine = [
            pltpu.make_async_copy(start.at[:, lanes], starts.at[i], sems.at[i, 0]),
            pltpu.make_async_copy(drift.at[:, lanes], drifts.at[i], sems.at[i, 1]),
            pltpu.make_async_copy(error.at[:, lanes], errors.at[i], sems.at[i, 2]),
        ]
        for copy in mine:
            copy.start()
        copies.append(mine)
    for i in range(blocks):
        for copy in copies[i]:
            copy.wait()
        both = jnp.concatenate([drifts[i], errors[i]], axis=0)
        factor = jnp.concatenate(split(starts[i], 3), axis=0)
        term = dot_rows(both, factor)
        if i == 0:
            acc[...] = term
        else:
            acc[...] += term
        merged = drifts[i].astype(f32) + errors[i].astype(f32)
        even, odd = merged[:, :narrow], merged[:, narrow:]
        keep[i] = jnp.where(first, even, odd)
        send[i] = jnp.where(first, odd, even)
    total = acc[:rows, :] + acc[rows:, :]
    left = total[:, :rank] + total[:, rank : 2 * rank] + total[:, 2 * rank :]
    packed = jnp.concatenate([left[: rows // 2], left[rows // 2 :]], axis=1)
    for z in range(8):
        out[z] = packed


def left_factor(drift, error, start):
    return call(
        left_kernel, "left", 24, 13_000_000,
        in_specs=[hbm, hbm, hbm],
        out_specs=[vmem, vmem, vmem],
        out_shape=[
            pltpu.VMEM((8, rows // 2, 2 * rank), f32),
            pltpu.VMEM((blocks, rows, narrow), f32),
            pltpu.VMEM((blocks, rows, narrow), f32),
        ],
        scratch_shapes=[
            pltpu.VMEM((blocks, rows, wide), bf16),
            pltpu.VMEM((blocks, rows, wide), bf16),
            pltpu.VMEM((blocks, rank, wide), f32),
            pltpu.VMEM((2 * rows, 3 * rank), f32),
            pltpu.SemaphoreType.DMA((blocks, 3)),
        ],
    )(*[pltpu.with_memory_space_constraint(value, pltpu.HBM) for value in (drift, error, start)])


def right_kernel(mine, theirs, keep, received, out, left_out, gram):
    total = (jnp.sum(mine[...], axis=0) + jnp.sum(theirs[...], axis=0)) * (1.0 / groups)
    left = jnp.concatenate([total[:, :rank], total[:, rank:]], axis=0)
    left_out[...] = left
    turned = left.T
    pieces = jnp.concatenate(split(turned, 3), axis=0)
    gram[...] = jnp.dot(turned, left, precision=exact, preferred_element_type=f32)
    own = gram[pl.ds(pl.multiple_of(lax.axis_index("core") * 32, 32), 32), :]
    packed = jnp.concatenate([own[:16], own[16:]], axis=1)
    for j in range(16):
        out[j, tall:, :] = packed
    for y in range(4):
        for part in range(2):
            k = 2 * y + part
            high, low = split(keep[k] + received[k], 2)
            term = dot(pieces, high) + dot(pieces, low)
            block = term[:rank] + term[rank : 2 * rank] + term[2 * rank :]
            for x in range(4):
                for t in range(5):
                    begin = 16 * (5 * part + t)
                    out[4 * x + y, begin : begin + 16, :] = block[
                        16 * x : 16 * (x + 1), 128 * t : 128 * (t + 1)
                    ]


def right_factor(mine, theirs, keep, received):
    return call(
        right_kernel, "right", 16, 10_000_000,
        in_specs=[vmem] * 4,
        out_specs=[vmem, vmem],
        out_shape=[shape(16, tall + 16, 128), shape(rows, rank)],
        scratch_shapes=[pltpu.VMEM((rank, rank), f32)],
    )(mine, theirs, keep, received)


def plane_sum_kernel(chunks, out, gram):
    total = chunks[0]
    for j in range(1, 16):
        total += chunks[j]
    gram[...] = total[tall:]
    for z in range(8):
        out[z] = total[:tall]


def plane_sum(chunks):
    return call(
        plane_sum_kernel, "plane_sum", 8, 3_000_000,
        in_specs=[vmem],
        out_specs=[vmem, vmem],
        out_shape=[shape(8, tall, 128), shape(16, 128)],
    )(chunks)


def line_sum_kernel(chunks, out):
    total = chunks[0]
    for j in range(1, 8):
        total += chunks[j]
    for j in range(16):
        out[j] = total


def line_sum(chunks):
    return call(
        line_sum_kernel, "line_sum", 8, 3_000_000,
        in_specs=[vmem],
        out_specs=vmem,
        out_shape=shape(16, tall, 128),
    )(chunks)


def inverse(gram):
    eye = (
        lax.broadcasted_iota(jnp.int32, (rank, rank), 0)
        == lax.broadcasted_iota(jnp.int32, (rank, rank), 1)
    ).astype(f32)
    work = jnp.concatenate([gram, eye], axis=1)
    row_id = lax.broadcasted_iota(jnp.int32, (rank, 2 * rank), 0)
    for k in range(rank):
        pivot = work[k : k + 1, :] / work[k : k + 1, k : k + 1]
        work = jnp.where(row_id == k, pivot, work - work[:, k : k + 1] * pivot)
    return work[:, rank:]


def solve_kernel(mine, theirs, left, out):
    def unpack(packed):
        return jnp.concatenate([packed[:, :rank], packed[:, rank:]], axis=0)

    own, other = unpack(mine[...]), unpack(theirs[...])
    first = lax.axis_index("core") == 0
    gram = jnp.concatenate([jnp.where(first, own, other), jnp.where(first, other, own)], axis=0)
    solved = jnp.dot(
        left[...], inverse(gram) * (1.0 / groups), precision=exact, preferred_element_type=f32
    )
    high, low = split(solved, 2)
    out[...] = jnp.concatenate([high, high, low], axis=1)


def solve(mine, theirs, left):
    return call(
        solve_kernel, "solve", 8, 20_000_000,
        in_specs=[vmem] * 3,
        out_specs=vmem,
        out_shape=shape(rows, 3 * rank, dtype=bf16),
    )(mine, theirs, left)


def block_copy(k, offset, held, new_error, sems):
    begin = pl.multiple_of((2 * k + offset) * narrow, narrow)
    return pltpu.make_async_copy(held.at[k], new_error.at[:, pl.ds(begin, narrow)], sems.at[k])


def approx_block(k, factor, right):
    y, part = k // 2, k % 2
    tiles = []
    for t in range(5):
        begin = 16 * (5 * part + t)
        tiles.append(
            jnp.concatenate([right[4 * x + y, begin : begin + 16, :] for x in range(4)], axis=0)
        )
    high, low = split(jnp.concatenate(tiles, axis=1), 2)
    return dot(factor, jnp.concatenate([high, low, high], axis=0))


def own_kernel(
    factor, right, merged, weights, momentum, new_error, new_weights, new_momentum,
    held, held_weights, held_momentum, sems, state_sems,
):
    core, z = lax.axis_index("core"), lax.axis_index("z")
    left = factor[...]
    copies = []
    state = [
        pltpu.make_async_copy(held_weights, new_weights, state_sems.at[0]),
        pltpu.make_async_copy(held_momentum, new_momentum, state_sems.at[1]),
    ]
    for k in range(blocks):
        approx = approx_block(k, left, right)
        held[k] = (merged[k] - approx).astype(bf16)
        copies.append(block_copy(k, core, held, new_error, sems))
        copies[-1].start()

        @pl.when(z == k)
        def _():
            moved = momentum_decay * momentum[...] + approx
            held_momentum[...] = moved
            held_weights[...] = weights[...] - outer_rate * (approx + momentum_decay * moved)

    for copy in state:
        copy.start()
    for copy in copies + state:
        copy.wait()


def finish_own(factor, right, merged, weights, momentum):
    return call(
        own_kernel, "own", 16, 8_000_000,
        in_specs=[vmem] * 5,
        out_specs=[hbm, hbm, hbm],
        out_shape=[shape(rows, cols, dtype=bf16), shape(rows, narrow), shape(rows, narrow)],
        scratch_shapes=[
            pltpu.VMEM((blocks, rows, narrow), bf16),
            pltpu.VMEM((rows, narrow), f32),
            pltpu.VMEM((rows, narrow), f32),
            pltpu.SemaphoreType.DMA((blocks,)),
            pltpu.SemaphoreType.DMA((2,)),
        ],
    )(factor, right, merged, weights, momentum)


def other_kernel(factor, right, merged, partial, new_error, held, sems):
    offset = 1 - lax.axis_index("core")
    left = factor[...]
    copies = []
    for k in range(blocks):
        held[k] = (merged[k] - approx_block(k, left, right)).astype(bf16)
        copies.append(block_copy(k, offset, held, new_error, sems))
        copies[-1].start()
    for copy in copies:
        copy.wait()


def finish_other(factor, right, merged, partial):
    return call(
        other_kernel, "other", 16, 8_000_000,
        in_specs=[vmem, vmem, vmem, hbm],
        out_specs=hbm,
        out_shape=shape(rows, cols, dtype=bf16),
        input_output_aliases={3: 0},
        scratch_shapes=[
            pltpu.VMEM((blocks, rows, narrow), bf16),
            pltpu.SemaphoreType.DMA((blocks,)),
        ],
    )(factor, right, merged, partial)


def swap(value):
    return lax.ppermute(value, "core", [(0, 1), (1, 0)])


def local(drift, error, start, weights, momentum):
    copies, keep, send = left_factor(drift[0], error[0], start.T)
    received = swap(send)
    mine = lax.all_to_all(copies, "z", 0, 0)
    chunks, left = right_factor(mine, swap(mine), keep, received)
    plane, gram = plane_sum(lax.all_to_all(chunks, ("x", "y"), 0, 0))
    factor = solve(gram, swap(gram), left)
    line = lax.all_to_all(plane, "z", 0, 0)
    line, factor = lax.optimization_barrier((line, factor))
    own = lax.all_to_all(line_sum(line), ("x", "y"), 0, 0)
    other = swap(own)
    partial, new_weights, new_momentum = finish_own(factor, own, keep, weights, momentum)
    new_error = finish_other(factor, other, send, partial)
    return new_weights, new_error[None], new_momentum


def solution(mesh):
    fine = Mesh(mesh.devices.reshape(8, 2, 4, 4), ("z", "core", "x", "y"))
    replica, fsdp = ("z", "core"), ("x", "y")
    return jax.shard_map(
        local,
        mesh=fine,
        in_specs=(
            P(replica, fsdp, None),
            P(replica, fsdp, None),
            P(),
            P(fsdp, replica),
            P(fsdp, replica),
        ),
        out_specs=(P(fsdp, replica), P(replica, fsdp, None), P(fsdp, replica)),
        check_vma=False,
    )
```

time: 439 us -> 119 us (0.27)
  waiting for transfers between devices: 271 us -> 11.5 us
  blocking collectives: 110 us -> 68.9 us
  matrix products: 25.5 us -> 0 us
  Pallas kernels: 0 us -> 21.5 us
  other arithmetic: 16.2 us -> 0 us
  starting transfers between devices: 0.04 us -> 13.7 us
  between operations: 14.1 us -> 0.72 us
    psum x1 -> x0, waiting for transfers between devices: 271 us -> none  [local(): total_q = lax.psum(partial_q, ('replica', 'fsdp'))]
    psum x2 -> x0, blocking collectives: 110 us -> none  [the longest x1 60.7 us: local(): gram = lax.psum(local_gram, 'fsdp')]
    all_to_all x0 -> x3, blocking collectives: none -> 68.9 us  [the longest x1 26.2 us: local(): plane, gram = plane_sum(lax.all_to_all(chunks, ('x', 'y'), 0, 0))]
    dot_general x4 -> x0, matrix products: 25.3 us -> none  [the longest x1 8.91 us: local(): jnp.dot(merged, start, precision=full_prec, preferred_element_type=jnp.fl...]
    pallas_call x0 -> x7, Pallas kernels: none -> 21.5 us  [the longest x1 8.14 us: left_factor(): call(left_kernel, 'left', 24, 13000000, in_specs=[hbm, hbm, hbm], out_spe...]
    another operation x5 -> x0, other arithmetic: 12.1 us -> none  [the longest x3 6.52 us: local(): lower = jnp.linalg.cholesky(gram)]
    ppermute x0 -> x4, starting transfers between devices: none -> 9.55 us  [swap(): return lax.ppermute(value, 'core', [(0, 1), (1, 0)])]
    all_to_all x0 -> x1, waiting for transfers between devices: none -> 9.37 us  [local(): line = lax.all_to_all(plane, 'z', 0, 0)]
  transfers between devices with their start and end apart: 1 -> 5, of which waited for: 1 -> 3; matrix products, arithmetic and copies ran while one was open for 0% -> 0% of each run, Pallas kernels for 0% -> 8%
where the time goes in v3:
time: 119 us
  blocking collectives  68.9 us (58%)
  Pallas kernels  21.5 us (18%)
  starting transfers between devices  13.7 us (12%)
  waiting for transfers between devices  11.5 us (10%)
  local copies, waits for them, and re-layouts  2.53 us (2%)
    all_to_all x1, blocking collectives, local(): plane, gram = plane_sum(lax.all_to_all(chunks, ('x', 'y'), 0, 0))  26.2 us
    all_to_all x1, blocking collectives, local(): own = lax.all_to_all(line_sum(line), ('x', 'y'), 0, 0)  22.6 us
    all_to_all x1, blocking collectives, local(): mine = lax.all_to_all(copies, 'z', 0, 0)  20 us
    ppermute x4, starting transfers between devices, swap(): return lax.ppermute(value, 'core', [(0, 1), (1, 0)])  9.55 us
    all_to_all x1, waiting for transfers between devices, local(): line = lax.all_to_all(plane, 'z', 0, 0)  9.37 us
    pallas_call x1, Pallas kernels, left_factor(): call(left_kernel, 'left', 24, 13000000, in_specs=[hbm, hbm, hbm], out_spe...  8.14 us
    pallas_call x1, Pallas kernels, solve(): call(solve_kernel, 'solve', 8, 20000000, in_specs=[vmem] * 3, out_specs=v...  5.82 us
    all_to_all x1, starting transfers between devices, local(): line = lax.all_to_all(plane, 'z', 0, 0)  4.19 us
  transfers between devices with their start and end apart: 5, of which 3 were waited for; matrix products, arithmetic and copies ran while one was open for 0% of the time, Pallas kernels for 8%

profile of v3, /device:TPU:1, one launch (start us, length us, event | category | flops | bytes accessed | tf_op | source)
XLA Modules:
  0.0 118.8 jit_solution(13904343501747589917)
XLA Ops:
  0.6 8.1 %left.1 = (f32[8,80,128]{2,1,0:T(8,128)S(1)}, f32[8,160,640]{2,1,0:T(8,128)S(1)}, f32[8,160,640]{2,1,0:T(8,128)S(1)}) custom-call(bf16[160,10240]{1,0:T(8,128)(2,1)} %bitcast.4, bf16[160,10240]{1,0:T(8,128)(2,1)} %bitcast.5, f32[64,10240]{1,0:T(8,128)} %bitcast.7), custom_call_target="tpu_custom_call" | custom-call | bytes 13000000 | tf_op jit(solution)/shard_map/left/pallas_call | solution.py:94
  8.8 3.3 %collective-permute-start.1 = (f32[8,160,640]{2,1,0:T(8,128)S(1)}, f32[8,160,640]{2,1,0:T(8,128)S(1)}, u32[]{:S(2)}, u32[]{:S(2)}) collective-permute-start(f32[8,160,640]{2,1,0:T(8,128)S(1)} %get-tuple-element.17.merged), channel_id=1, source_target_pairs={{0,16},{16,0},{1,17},{17,1},{2,18},{18,2},{3,19},{19,3},{4,20},{20... | collective-permute-start | bytes 9830408 | tf_op jit(solution)/shard_map/ppermute | solution.py:308
  12.1 0.0 copy-start
  12.1 1.7 %copy-done = f32[8,160,640]{2,1,0:T(8,128)} copy-done((f32[8,160,640]{2,1,0:T(8,128)}, f32[8,160,640]{2,1,0:T(8,128)S(1)}, u32[]{:S(2)}) %copy-start) | copy-done | bytes 3276824
  13.8 20.0 %all_to_all.20.mine = f32[8,80,128]{2,1,0:T(8,128)S(1)} all-to-all(f32[8,80,128]{2,1,0:T(8,128)S(1)} %get-tuple-element.15), channel_id=1, replica_groups=mesh['z'=8,'core'=2,'x'=4,'y'=4] {'z'}, dimensions={0} | all-to-all | bytes 655360 | tf_op jit(solution)/shard_map/all_to_all | solution.py:314
  33.8 0.5 collective-permute-start
  34.3 1.3 %collective-permute-done.theirs = f32[8,80,128]{2,1,0:T(8,128)S(1)} collective-permute-done((f32[8,80,128]{2,1,0:T(8,128)S(1)}, f32[8,80,128]{2,1,0:T(8,128)S(1)}, u32[]{:S(2)}, u32[]{:S(2)}) %collective-permute-start) | collective-permute-done | bytes 327712 | tf_op jit(solution)/shard_map/ppermute | solution.py:308
  35.5 0.0 collective-permute-done.1.received
  35.5 1.6 %right.1 = (f32[16,176,128]{2,1,0:T(8,128)S(1)}, f32[160,64]{1,0:T(8,128)S(1)}) custom-call(f32[8,80,128]{2,1,0:T(8,128)S(1)} %all_to_all.20.mine, f32[8,80,128]{2,1,0:T(8,128)S(1)} %collective-permute-done.theirs, f32[8,160,640]{2,1,0:T(8,128)S(1)} %get-tuple-element.16.keep.merged, f32[8,160,640]{2,1,0:T(8,128)S(1)} %collective-permute-done.1.received), custom_call_target="tpu_custom_call" | custom-call | bytes 10000000 | tf_op jit(solution)/shard_map/right/pallas_call | solution.py:139
  37.1 26.2 %all_to_all.21.chunks = f32[16,176,128]{2,1,0:T(8,128)S(1)} all-to-all(f32[16,176,128]{2,1,0:T(8,128)S(1)} %get-tuple-element.18), channel_id=1, replica_groups=mesh['z'=8,'core'=2,'x'=4,'y'=4] {'x','y'}, dimensions={0} | all-to-all | bytes 2883584 | tf_op jit(solution)/shard_map/all_to_all | solution.py:316
  63.4 0.1 plane_sum.1
  63.5 0.0 copy-start.2
  63.5 0.8 copy-done.2
  64.3 4.2 %all-to-all-start.2 = ((f32[8,160,128]{2,1,0:T(8,128)}), f32[8,160,128]{2,1,0:T(8,128)}, u32[]{:S(2)}, u32[]{:S(2)}) async-start(f32[8,160,128]{2,1,0:T(8,128)} %copy-done.2), calls=%async_computation.2 | async-start | bytes 1310720 | tf_op jit(solution)/shard_map/all_to_all | solution.py:318
  68.5 2.4 %collective-permute-start.2 = (f32[16,128]{1,0:T(8,128)S(1)}, f32[16,128]{1,0:T(8,128)S(1)}, u32[]{:S(2)}, u32[]{:S(2)}) collective-permute-start(f32[16,128]{1,0:T(8,128)S(1)} %get-tuple-element.20.mine), channel_id=1, source_target_pairs={{0,16},{16,0},{1,17},{17,1},{2,18},{18,2},{3,19},{19,3},{4,20},{20... | collective-permute-start | bytes 24584 | tf_op jit(solution)/shard_map/ppermute | solution.py:308
  70.9 0.8 collective-permute-done.2.theirs
  71.7 5.8 %solve.1.factor = bf16[160,192]{1,0:T(8,128)(2,1)S(1)} custom-call(f32[16,128]{1,0:T(8,128)S(1)} %get-tuple-element.20.mine, f32[16,128]{1,0:T(8,128)S(1)} %collective-permute-done.2.theirs, f32[160,64]{1,0:T(8,128)S(1)} %get-tuple-element.21.left), custom_call_target="tpu_custom_call" | custom-call | bytes 20000000 | tf_op jit(solution)/shard_map/solve/pallas_call | solution.py:211
  77.6 9.4 %all-to-all-done.2.chunks = f32[8,160,128]{2,1,0:T(8,128)} async-done(((f32[8,160,128]{2,1,0:T(8,128)}), f32[8,160,128]{2,1,0:T(8,128)}, u32[]{:S(2)}, u32[]{:S(2)}) %all-to-all-start.2) | async-done | bytes 655392 | tf_op jit(solution)/shard_map/all_to_all | solution.py:318
  86.9 0.0 copy-start.3
  86.9 0.0 copy-start.4
  86.9 1.3 %line_sum.1 = f32[16,160,128]{2,1,0:T(8,128)S(1)} custom-call(f32[8,160,128]{2,1,0:T(8,128)} %all-to-all-done.2.chunks), custom_call_target="tpu_custom_call" | custom-call | bytes 3000000 | tf_op jit(solution)/shard_map/line_sum/pallas_call | solution.py:175
  88.2 22.6 %all_to_all.22.right = f32[16,160,128]{2,1,0:T(8,128)S(1)} all-to-all(f32[16,160,128]{2,1,0:T(8,128)S(1)} %line_sum.1), channel_id=1, replica_groups=mesh['z'=8,'core'=2,'x'=4,'y'=4] {'x','y'}, dimensions={0} | all-to-all | bytes 2621440 | tf_op jit(solution)/shard_map/all_to_all | solution.py:320
  110.9 0.0 copy-start.1
  110.9 3.3 %collective-permute-start.3 = (f32[16,160,128]{2,1,0:T(8,128)S(1)}, f32[16,160,128]{2,1,0:T(8,128)S(1)}, u32[]{:S(2)}, u32[]{:S(2)}) collective-permute-start(f32[16,160,128]{2,1,0:T(8,128)S(1)} %all_to_all.22.right), channel_id=1, source_target_pairs={{0,16},{16,0},{1,17},{17,1},{2,18},{18,2},{3,19},{19,3},{4,20},{20... | collective-permute-start | bytes 3932168 | tf_op jit(solution)/shard_map/ppermute | solution.py:308
  114.2 0.0 copy-done.3
  114.2 0.0 copy-done.4
  114.2 3.1 %own.1 = (bf16[160,10240]{1,0:T(8,128)(2,1)}, f32[160,640]{1,0:T(8,128)}, f32[160,640]{1,0:T(8,128)}) custom-call(bf16[160,192]{1,0:T(8,128)(2,1)S(1)} %solve.1.factor, f32[16,160,128]{2,1,0:T(8,128)S(1)} %all_to_all.22.right, f32[8,160,640]{2,1,0:T(8,128)S(1)} %get-tuple-element.16.keep.merged, f32[160,640]{1,0:T(8,128)S(1)} %copy-done.3, ...), custom_call_target="tpu_custom_call" | custom-call | bytes 8000000 | tf_op jit(solution)/shard_map/own/pallas_call | solution.py:266
  117.3 0.0 collective-permute-done.3.right
  117.3 0.0 copy-done.1
  117.3 1.5 %other.1 = bf16[160,10240]{1,0:T(8,128)(2,1)} custom-call(bf16[160,192]{1,0:T(8,128)(2,1)S(1)} %solve.1.factor, f32[16,160,128]{2,1,0:T(8,128)S(1)} %collective-permute-done.3.right, f32[8,160,640]{2,1,0:T(8,128)S(1)} %copy-done.1, bf16[160,10240]{1,0:T(8,128)(2,1)} %get-tuple-element.25.partial), custom_call_target="tpu_custom_call", output_to_operand_aliasing={{}: (3, {})} | custom-call | bytes 8000000 | tf_op jit(solution)/shard_map/other/pallas_call | solution.py:294
Async XLA Ops:
  8.8 26.7 %collective-permute-start.1 = (f32[8,160,640]{2,1,0:T(8,128)S(1)}, f32[8,160,640]{2,1,0:T(8,128)S(1)}, u32[]{:S(2)}, u32[]{:S(2)}) collective-permute-start(f32[8,160,640]{2,1,0:T(8,128)S(1)} %get-tuple-element.17.merged), channel_id=1, source_target_pairs={{0,16},{16,0},{1,17},{17,1},{2,18},{18,2},{3,19},{19,3},{4,20},{20... | collective-permute-start | bytes 9830408 | tf_op jit(solution)/shard_map/ppermute | solution.py:308
  12.1 1.7 %copy-start = (f32[8,160,640]{2,1,0:T(8,128)}, f32[8,160,640]{2,1,0:T(8,128)S(1)}, u32[]{:S(2)}) copy-start(f32[8,160,640]{2,1,0:T(8,128)S(1)} %get-tuple-element.17.merged) | copy-start | bytes 9830404
  33.8 1.7 %collective-permute-start = (f32[8,80,128]{2,1,0:T(8,128)S(1)}, f32[8,80,128]{2,1,0:T(8,128)S(1)}, u32[]{:S(2)}, u32[]{:S(2)}) collective-permute-start(f32[8,80,128]{2,1,0:T(8,128)S(1)} %all_to_all.20.mine), channel_id=1, source_target_pairs={{0,16},{16,0},{1,17},{17,1},{2,18},{18,2},{3,19},{19,3},{4,20},{20... | collective-permute-start | bytes 983048 | tf_op jit(solution)/shard_map/ppermute | solution.py:308
  63.5 0.8 copy-start.2
  64.3 22.6 %all-to-all-start.2 = ((f32[8,160,128]{2,1,0:T(8,128)}), f32[8,160,128]{2,1,0:T(8,128)}, u32[]{:S(2)}, u32[]{:S(2)}) async-start(f32[8,160,128]{2,1,0:T(8,128)} %copy-done.2), calls=%async_computation.2 | async-start | bytes 1310720 | tf_op jit(solution)/shard_map/all_to_all | solution.py:318
  68.5 3.2 %collective-permute-start.2 = (f32[16,128]{1,0:T(8,128)S(1)}, f32[16,128]{1,0:T(8,128)S(1)}, u32[]{:S(2)}, u32[]{:S(2)}) collective-permute-start(f32[16,128]{1,0:T(8,128)S(1)} %get-tuple-element.20.mine), channel_id=1, source_target_pairs={{0,16},{16,0},{1,17},{17,1},{2,18},{18,2},{3,19},{19,3},{4,20},{20... | collective-permute-start | bytes 24584 | tf_op jit(solution)/shard_map/ppermute | solution.py:308
  86.9 27.3 %copy-start.3 = (f32[160,640]{1,0:T(8,128)S(1)}, f32[160,640]{1,0:T(8,128)}, u32[]{:S(2)}) copy-start(f32[160,640]{1,0:T(8,128)} %weights.1) | copy-start | bytes 1228804
  86.9 27.3 %copy-start.4 = (f32[160,640]{1,0:T(8,128)S(1)}, f32[160,640]{1,0:T(8,128)}, u32[]{:S(2)}) copy-start(f32[160,640]{1,0:T(8,128)} %momentum.1) | copy-start | bytes 1228804
  110.9 6.5 %copy-start.1 = (f32[8,160,640]{2,1,0:T(8,128)S(1)}, f32[8,160,640]{2,1,0:T(8,128)}, u32[]{:S(2)}) copy-start(f32[8,160,640]{2,1,0:T(8,128)} %copy-done) | copy-start | bytes 9830404
  110.9 6.5 %collective-permute-start.3 = (f32[16,160,128]{2,1,0:T(8,128)S(1)}, f32[16,160,128]{2,1,0:T(8,128)S(1)}, u32[]{:S(2)}, u32[]{:S(2)}) collective-permute-start(f32[16,160,128]{2,1,0:T(8,128)S(1)} %all_to_all.22.right), channel_id=1, source_target_pairs={{0,16},{16,0},{1,17},{17,1},{2,18},{18,2},{3,19},{19,3},{4,20},{20... | collective-permute-start | bytes 3932168 | tf_op jit(solution)/shard_map/ppermute | solution.py:308

commit v4 on v3

--- a/solution.py
+++ b/solution.py
@@ -117,10 +117,10 @@
     turned = left.T
     pieces = jnp.concatenate(split(turned, 3), axis=0)
     gram[...] = jnp.dot(turned, left, precision=exact, preferred_element_type=f32)
-    own = gram[pl.ds(pl.multiple_of(lax.axis_index("core") * 32, 32), 32), :]
-    packed = jnp.concatenate([own[:16], own[16:]], axis=1)
+    share = gram[pl.ds(pl.multiple_of(lax.axis_index("z") * 8, 8), 8), :]
+    padded = jnp.concatenate([share, jnp.zeros((8, rank), f32)], axis=1)
     for j in range(16):
-        out[j, tall:, :] = packed
+        out[j, tall:, :] = padded
     for y in range(4):
         for part in range(2):
             k = 2 * y + part
@@ -140,80 +140,79 @@
         right_kernel, "right", 16, 10_000_000,
         in_specs=[vmem] * 4,
         out_specs=[vmem, vmem],
-        out_shape=[shape(16, tall + 16, 128), shape(rows, rank)],
+        out_shape=[shape(16, tall + 8, 128), shape(rows, rank)],
         scratch_shapes=[pltpu.VMEM((rank, rank), f32)],
     )(mine, theirs, keep, received)
 
 
-def plane_sum_kernel(chunks, out, gram):
+def plane_sum_kernel(chunks, out):
     total = chunks[0]
     for j in range(1, 16):
         total += chunks[j]
-    gram[...] = total[tall:]
     for z in range(8):
-        out[z] = total[:tall]
+        out[z] = total
 
 
 def plane_sum(chunks):
     return call(
         plane_sum_kernel, "plane_sum", 8, 3_000_000,
         in_specs=[vmem],
-        out_specs=[vmem, vmem],
-        out_shape=[shape(8, tall, 128), shape(16, 128)],
+        out_specs=vmem,
+        out_shape=shape(8, tall + 8, 128),
     )(chunks)
 
 
-def line_sum_kernel(chunks, out):
-    total = chunks[0]
+def line_sum_kernel(chunks, out, gram):
+    total = chunks[0, :tall, :]
     for j in range(1, 8):
-        total += chunks[j]
+        total += chunks[j, :tall, :]
     for j in range(16):
         out[j] = total
+    for j in range(8):
+        gram[8 * j : 8 * (j + 1), :] = chunks[j, tall:, :]
 
 
 def line_sum(chunks):
     return call(
         line_sum_kernel, "line_sum", 8, 3_000_000,
         in_specs=[vmem],
-        out_specs=vmem,
-        out_shape=shape(16, tall, 128),
+        out_specs=[vmem, vmem],
+        out_shape=[shape(16, tall, 128), shape(rank, 2 * rank)],
     )(chunks)
 
 
 def inverse(gram):
-    eye = (
-        lax.broadcasted_iota(jnp.int32, (rank, rank), 0)
-        == lax.broadcasted_iota(jnp.int32, (rank, rank), 1)
-    ).astype(f32)
-    work = jnp.concatenate([gram, eye], axis=1)
-    row_id = lax.broadcasted_iota(jnp.int32, (rank, 2 * rank), 0)
-    for k in range(rank):
-        pivot = work[k : k + 1, :] / work[k : k + 1, k : k + 1]
-        work = jnp.where(row_id == k, pivot, work - work[:, k : k + 1] * pivot)
+    size = (rank, 2 * rank)
+    row = lax.broadcasted_iota(jnp.int32, size, 0)
+    work = jnp.where(lax.broadcasted_iota(jnp.int32, size, 1) == row + rank, 1.0, gram)
+    step = 8
+    for k in range(0, rank, step):
+        columns = [jnp.broadcast_to(work[:, k + j : k + j + 1], size) for j in range(step)]
+        block = [[columns[j][k + i : k + i + 1, :] for j in range(step)] for i in range(step)]
+        pivots = [work[k + i : k + i + 1, :] for i in range(step)]
+        for j in range(step):
+            scale = 1.0 / block[j][j]
+            pivots[j] = pivots[j] * scale
+            for m in range(j + 1, step):
+                block[j][m] = block[j][m] * scale
+            for i in range(step):
+                if i != j:
+                    pivots[i] = pivots[i] - block[i][j] * pivots[j]
+                    for m in range(j + 1, step):
+                        block[i][m] = block[i][m] - block[i][j] * block[j][m]
+        for j in range(step):
+            work = work - columns[j] * pivots[j]
+        for j in range(step):
+            work = jnp.where(row == k + j, pivots[j], work)
     return work[:, rank:]
 
 
-def solve_kernel(mine, theirs, left, out):
-    def unpack(packed):
-        return jnp.concatenate([packed[:, :rank], packed[:, rank:]], axis=0)
-
-    own, other = unpack(mine[...]), unpack(theirs[...])
-    first = lax.axis_index("core") == 0
-    gram = jnp.concatenate([jnp.where(first, own, other), jnp.where(first, other, own)], axis=0)
+def solve(gram, left):
     solved = jnp.dot(
-        left[...], inverse(gram) * (1.0 / groups), precision=exact, preferred_element_type=f32
+        left, inverse(gram) * (1.0 / groups), precision=exact, preferred_element_type=f32
     )
     high, low = split(solved, 2)
-    out[...] = jnp.concatenate([high, high, low], axis=1)
-
-
-def solve(mine, theirs, left):
-    return call(
-        solve_kernel, "solve", 8, 20_000_000,
-        in_specs=[vmem] * 3,
-        out_specs=vmem,
-        out_shape=shape(rows, 3 * rank, dtype=bf16),
-    )(mine, theirs, left)
+    return jnp.concatenate([high, high, low], axis=1)
 
 
 def block_copy(k, offset, held, new_error, sems):
@@ -234,18 +233,19 @@
 
 
 def own_kernel(
-    factor, right, merged, weights, momentum, new_error, new_weights, new_momentum,
+    gram, left, right, merged, weights, momentum, new_error, new_weights, new_momentum, factor,
     held, held_weights, held_momentum, sems, state_sems,
 ):
     core, z = lax.axis_index("core"), lax.axis_index("z")
-    left = factor[...]
+    solved = solve(gram[...], left[...])
+    factor[...] = solved
     copies = []
     state = [
         pltpu.make_async_copy(held_weights, new_weights, state_sems.at[0]),
         pltpu.make_async_copy(held_momentum, new_momentum, state_sems.at[1]),
     ]
     for k in range(blocks):
-        approx = approx_block(k, left, right)
+        approx = approx_block(k, solved, right)
         held[k] = (merged[k] - approx).astype(bf16)
         copies.append(block_copy(k, core, held, new_error, sems))
         copies[-1].start()
@@ -262,12 +262,17 @@
         copy.wait()
 
 
-def finish_own(factor, right, merged, weights, momentum):
-    return call(
-        own_kernel, "own", 16, 8_000_000,
-        in_specs=[vmem] * 5,
-        out_specs=[hbm, hbm, hbm],
-        out_shape=[shape(rows, cols, dtype=bf16), shape(rows, narrow), shape(rows, narrow)],
+def finish_own(gram, left, right, merged, weights, momentum):
+    return call(
+        own_kernel, "own", 16, 16_000_000,
+        in_specs=[vmem] * 6,
+        out_specs=[hbm, hbm, hbm, vmem],
+        out_shape=[
+            shape(rows, cols, dtype=bf16),
+            shape(rows, narrow),
+            shape(rows, narrow),
+            shape(rows, 3 * rank, dtype=bf16),
+        ],
         scratch_shapes=[
             pltpu.VMEM((blocks, rows, narrow), bf16),
             pltpu.VMEM((rows, narrow), f32),
@@ -275,7 +280,7 @@
             pltpu.SemaphoreType.DMA((blocks,)),
             pltpu.SemaphoreType.DMA((2,)),
         ],
-    )(factor, right, merged, weights, momentum)
+    )(gram, left, right, merged, weights, momentum)
 
 
 def other_kernel(factor, right, merged, partial, new_error, held, sems):
@@ -313,13 +318,13 @@
     received = swap(send)
     mine = lax.all_to_all(copies, "z", 0, 0)
     chunks, left = right_factor(mine, swap(mine), keep, received)
-    plane, gram = plane_sum(lax.all_to_all(chunks, ("x", "y"), 0, 0))
-    factor = solve(gram, swap(gram), left)
-    line = lax.all_to_all(plane, "z", 0, 0)
-    line, factor = lax.optimization_barrier((line, factor))
-    own = lax.all_to_all(line_sum(line), ("x", "y"), 0, 0)
+    plane = plane_sum(lax.all_to_all(chunks, ("x", "y"), 0, 0))
+    line, gram = line_sum(lax.all_to_all(plane, "z", 0, 0))
+    own = lax.all_to_all(line, ("x", "y"), 0, 0)
     other = swap(own)
-    partial, new_weights, new_momentum = finish_own(factor, own, keep, weights, momentum)
+    partial, new_weights, new_momentum, factor = finish_own(
+        gram, left, own, keep, weights, momentum
+    )
     new_error = finish_other(factor, other, send, partial)
     return new_weights, new_error[None], new_momentum
 

time: 119 us -> 115 us (0.966)
  blocking collectives: 68.9 us -> 87.8 us
  waiting for transfers between devices: 11.5 us -> 1.26 us
  starting transfers between devices: 13.7 us -> 8.1 us
  Pallas kernels: 21.5 us -> 17.1 us
  local copies, waits for them, and re-layouts: 2.53 us -> 0.01 us
    all_to_all x2 -> x3, blocking collectives: 48.8 us -> 67.7 us  [the longest x1 25.9 us: local(): plane = plane_sum(lax.all_to_all(chunks, ('x', 'y'), 0, 0))]
    all_to_all x1 -> x0, waiting for transfers between devices: 9.37 us -> none  [local(): line = lax.all_to_all(plane, 'z', 0, 0)]
    all_to_all x1 -> x0, starting transfers between devices: 4.19 us -> none  [local(): line = lax.all_to_all(plane, 'z', 0, 0)]
    pallas_call x2 -> x1, Pallas kernels: 8.92 us -> 5.73 us  [finish_own(): call(own_kernel, 'own', 16, 16000000, in_specs=[vmem] * 6, out_specs=[hbm...]
    unnamed x10 -> x4, local copies, waits for them, and re-layouts: 2.53 us -> 0.01 us
    ppermute x4 -> x3, starting transfers between devices: 9.55 us -> 8.1 us  [swap(): return lax.ppermute(value, 'core', [(0, 1), (1, 0)])]
  transfers between devices with their start and end apart: 5 -> 3, of which waited for: 3 -> 1; matrix products, arithmetic and copies ran while one was open for 0% -> 0% of each run, Pallas kernels for 8% -> 5%
where the time goes in v4:
time: 115 us
  blocking collectives  87.8 us (76%)
  Pallas kernels  17.1 us (15%)
  starting transfers between devices  8.1 us (7%)
  waiting for transfers between devices  1.26 us (1%)
    all_to_all x1, blocking collectives, local(): plane = plane_sum(lax.all_to_all(chunks, ('x', 'y'), 0, 0))  25.9 us
    all_to_all x1, blocking collectives, local(): own = lax.all_to_all(line, ('x', 'y'), 0, 0)  21.3 us
    all_to_all x1, blocking collectives, local(): line, gram = line_sum(lax.all_to_all(plane, 'z', 0, 0))  20.6 us
    all_to_all x1, blocking collectives, local(): mine = lax.all_to_all(copies, 'z', 0, 0)  20 us
    pallas_call x1, Pallas kernels, left_factor(): call(left_kernel, 'left', 24, 13000000, in_specs=[hbm, hbm, hbm], out_spe...  8.14 us
    ppermute x3, starting transfers between devices, swap(): return lax.ppermute(value, 'core', [(0, 1), (1, 0)])  8.1 us
    pallas_call x1, Pallas kernels, finish_own(): call(own_kernel, 'own', 16, 16000000, in_specs=[vmem] * 6, out_specs=[hbm...  5.73 us
  transfers between devices with their start and end apart: 3, of which 1 were waited for; matrix products, arithmetic and copies ran while one was open for 0% of the time, Pallas kernels for 5%

profile of v4, /device:TPU:1, one launch (start us, length us, event | category | flops | bytes accessed | tf_op | source)
XLA Modules:
  0.0 114.9 jit_solution(2729942104750310905)
XLA Ops:
  0.6 8.1 %left.1 = (f32[8,80,128]{2,1,0:T(8,128)S(1)}, f32[8,160,640]{2,1,0:T(8,128)S(1)}, f32[8,160,640]{2,1,0:T(8,128)S(1)}) custom-call(bf16[160,10240]{1,0:T(8,128)(2,1)} %bitcast.4, bf16[160,10240]{1,0:T(8,128)(2,1)} %bitcast.5, f32[64,10240]{1,0:T(8,128)} %bitcast.7), custom_call_target="tpu_custom_call" | custom-call | bytes 13000000 | tf_op jit(solution)/shard_map/left/pallas_call | solution.py:94
  8.8 3.3 %collective-permute-start.1 = (f32[8,160,640]{2,1,0:T(8,128)S(1)}, f32[8,160,640]{2,1,0:T(8,128)S(1)}, u32[]{:S(2)}, u32[]{:S(2)}) collective-permute-start(f32[8,160,640]{2,1,0:T(8,128)S(1)} %get-tuple-element.16.merged), channel_id=1, source_target_pairs={{0,16},{16,0},{1,17},{17,1},{2,18},{18,2},{3,19},{19,3},{4,20},{20... | collective-permute-start | bytes 9830408 | tf_op jit(solution)/shard_map/ppermute | solution.py:313
  12.1 20.0 %all_to_all.20.mine = f32[8,80,128]{2,1,0:T(8,128)S(1)} all-to-all(f32[8,80,128]{2,1,0:T(8,128)S(1)} %get-tuple-element.14), channel_id=1, replica_groups=mesh['z'=8,'core'=2,'x'=4,'y'=4] {'z'}, dimensions={0} | all-to-all | bytes 655360 | tf_op jit(solution)/shard_map/all_to_all | solution.py:319
  32.1 0.5 collective-permute-start
  32.6 1.3 %collective-permute-done.theirs = f32[8,80,128]{2,1,0:T(8,128)S(1)} collective-permute-done((f32[8,80,128]{2,1,0:T(8,128)S(1)}, f32[8,80,128]{2,1,0:T(8,128)S(1)}, u32[]{:S(2)}, u32[]{:S(2)}) %collective-permute-start) | collective-permute-done | bytes 327712 | tf_op jit(solution)/shard_map/ppermute | solution.py:313
  33.8 0.0 collective-permute-done.1.received
  33.8 1.6 %right.1 = (f32[16,168,128]{2,1,0:T(8,128)S(1)}, f32[160,64]{1,0:T(8,128)S(1)}) custom-call(f32[8,80,128]{2,1,0:T(8,128)S(1)} %all_to_all.20.mine, f32[8,80,128]{2,1,0:T(8,128)S(1)} %collective-permute-done.theirs, f32[8,160,640]{2,1,0:T(8,128)S(1)} %get-tuple-element.15.keep.merged, f32[8,160,640]{2,1,0:T(8,128)S(1)} %collective-permute-done.1.received), custom_call_target="tpu_custom_call" | custom-call | bytes 10000000 | tf_op jit(solution)/shard_map/right/pallas_call | solution.py:139
  35.4 25.9 %all_to_all.21.chunks = f32[16,168,128]{2,1,0:T(8,128)S(1)} all-to-all(f32[16,168,128]{2,1,0:T(8,128)S(1)} %get-tuple-element.17), channel_id=1, replica_groups=mesh['z'=8,'core'=2,'x'=4,'y'=4] {'x','y'}, dimensions={0} | all-to-all | bytes 2752512 | tf_op jit(solution)/shard_map/all_to_all | solution.py:321
  61.3 0.0 copy-start
  61.3 0.0 copy-start.1
  61.3 0.1 plane_sum.1
  61.4 20.6 %all_to_all.22.chunks = f32[8,168,128]{2,1,0:T(8,128)S(1)} all-to-all(f32[8,168,128]{2,1,0:T(8,128)S(1)} %plane_sum.1), channel_id=1, replica_groups=mesh['z'=8,'core'=2,'x'=4,'y'=4] {'z'}, dimensions={0} | all-to-all | bytes 1376256 | tf_op jit(solution)/shard_map/all_to_all | solution.py:322
  82.0 0.1 line_sum.1
  82.2 21.3 %all_to_all.23.right = f32[16,160,128]{2,1,0:T(8,128)S(1)} all-to-all(f32[16,160,128]{2,1,0:T(8,128)S(1)} %get-tuple-element.20), channel_id=1, replica_groups=mesh['z'=8,'core'=2,'x'=4,'y'=4] {'x','y'}, dimensions={0} | all-to-all | bytes 2621440 | tf_op jit(solution)/shard_map/all_to_all | solution.py:323
  103.4 4.3 %collective-permute-start.2 = (f32[16,160,128]{2,1,0:T(8,128)S(1)}, f32[16,160,128]{2,1,0:T(8,128)S(1)}, u32[]{:S(2)}, u32[]{:S(2)}) collective-permute-start(f32[16,160,128]{2,1,0:T(8,128)S(1)} %all_to_all.23.right), channel_id=1, source_target_pairs={{0,16},{16,0},{1,17},{17,1},{2,18},{18,2},{3,19},{19,3},{4,20},{20... | collective-permute-start | bytes 3932168 | tf_op jit(solution)/shard_map/ppermute | solution.py:313
  107.7 0.0 copy-done
  107.7 0.0 copy-done.1
  107.7 5.7 %own.1 = (bf16[160,10240]{1,0:T(8,128)(2,1)}, f32[160,640]{1,0:T(8,128)}, f32[160,640]{1,0:T(8,128)}, bf16[160,192]{1,0:T(8,128)(2,1)S(1)}) custom-call(f32[64,128]{1,0:T(8,128)S(1)} %get-tuple-element.18.gram, f32[160,64]{1,0:T(8,128)S(1)} %get-tuple-element.19.left, f32[16,160,128]{2,1,0:T(8,128)S(1)} %all_to_all.23.right, ...), custom_call_target="tpu_custom_call" | custom-call | bytes 16000000 | tf_op jit(solution)/shard_map/own/pallas_call | solution.py:266
  113.5 0.0 collective-permute-done.2.right
  113.5 1.5 %other.1 = bf16[160,10240]{1,0:T(8,128)(2,1)} custom-call(bf16[160,192]{1,0:T(8,128)(2,1)S(1)} %get-tuple-element.22.factor, f32[16,160,128]{2,1,0:T(8,128)S(1)} %collective-permute-done.2.right, f32[8,160,640]{2,1,0:T(8,128)S(1)} %get-tuple-element.16.merged, bf16[160,10240]{1,0:T(8,128)(2,1)} %get-tuple-element.23.partial), custom_call_target="tpu_custom_call", output_to_operand_aliasing={{}: (3, {})} | custom-call | bytes 8000000 | tf_op jit(solution)/shard_map/other/pallas_call | solution.py:299
Async XLA Ops:
  8.8 25.1 %collective-permute-start.1 = (f32[8,160,640]{2,1,0:T(8,128)S(1)}, f32[8,160,640]{2,1,0:T(8,128)S(1)}, u32[]{:S(2)}, u32[]{:S(2)}) collective-permute-start(f32[8,160,640]{2,1,0:T(8,128)S(1)} %get-tuple-element.16.merged), channel_id=1, source_target_pairs={{0,16},{16,0},{1,17},{17,1},{2,18},{18,2},{3,19},{19,3},{4,20},{20... | collective-permute-start | bytes 9830408 | tf_op jit(solution)/shard_map/ppermute | solution.py:313
  32.1 1.7 %collective-permute-start = (f32[8,80,128]{2,1,0:T(8,128)S(1)}, f32[8,80,128]{2,1,0:T(8,128)S(1)}, u32[]{:S(2)}, u32[]{:S(2)}) collective-permute-start(f32[8,80,128]{2,1,0:T(8,128)S(1)} %all_to_all.20.mine), channel_id=1, source_target_pairs={{0,16},{16,0},{1,17},{17,1},{2,18},{18,2},{3,19},{19,3},{4,20},{20... | collective-permute-start | bytes 983048 | tf_op jit(solution)/shard_map/ppermute | solution.py:313
  61.3 46.4 %copy-start = (f32[160,640]{1,0:T(8,128)S(1)}, f32[160,640]{1,0:T(8,128)}, u32[]{:S(2)}) copy-start(f32[160,640]{1,0:T(8,128)} %weights.1) | copy-start | bytes 1228804
  61.3 46.4 %copy-start.1 = (f32[160,640]{1,0:T(8,128)S(1)}, f32[160,640]{1,0:T(8,128)}, u32[]{:S(2)}) copy-start(f32[160,640]{1,0:T(8,128)} %momentum.1) | copy-start | bytes 1228804
  103.4 10.1 %collective-permute-start.2 = (f32[16,160,128]{2,1,0:T(8,128)S(1)}, f32[16,160,128]{2,1,0:T(8,128)S(1)}, u32[]{:S(2)}, u32[]{:S(2)}) collective-permute-start(f32[16,160,128]{2,1,0:T(8,128)S(1)} %all_to_all.23.right), channel_id=1, source_target_pairs={{0,16},{16,0},{1,17},{17,1},{2,18},{18,2},{3,19},{19,3},{4,20},{20... | collective-permute-start | bytes 3932168 | tf_op jit(solution)/shard_map/ppermute | solution.py:313

commit v5 on v4

--- a/solution.py
+++ b/solution.py
@@ -15,7 +15,7 @@
 wide = 1280
 blocks = 8
 groups = 16
-tall = 160
+tall = 80
 f32 = jnp.float32
 bf16 = jnp.bfloat16
 exact = lax.Precision.HIGHEST
@@ -110,6 +110,10 @@
     )(*[pltpu.with_memory_space_constraint(value, pltpu.HBM) for value in (drift, error, start)])
 
 
+def line_index():
+    return 2 * lax.axis_index("zh") + lax.axis_index("zl")
+
+
 def right_kernel(mine, theirs, keep, received, out, left_out, gram):
     total = (jnp.sum(mine[...], axis=0) + jnp.sum(theirs[...], axis=0)) * (1.0 / groups)
     left = jnp.concatenate([total[:, :rank], total[:, rank:]], axis=0)
@@ -117,22 +121,23 @@
     turned = left.T
     pieces = jnp.concatenate(split(turned, 3), axis=0)
     gram[...] = jnp.dot(turned, left, precision=exact, preferred_element_type=f32)
-    share = gram[pl.ds(pl.multiple_of(lax.axis_index("z") * 8, 8), 8), :]
-    padded = jnp.concatenate([share, jnp.zeros((8, rank), f32)], axis=1)
-    for j in range(16):
+    share = gram[pl.ds(pl.multiple_of(line_index() * 8, 8), 8), :]
+    empty = jnp.zeros((8, rank), f32)
+    even = lax.axis_index("zl") == 0
+    padded = jnp.concatenate(
+        [jnp.where(even, share, empty), jnp.where(even, empty, share)], axis=1
+    )
+    for j in range(32):
         out[j, tall:, :] = padded
-    for y in range(4):
-        for part in range(2):
-            k = 2 * y + part
-            high, low = split(keep[k] + received[k], 2)
-            term = dot(pieces, high) + dot(pieces, low)
-            block = term[:rank] + term[rank : 2 * rank] + term[2 * rank :]
-            for x in range(4):
-                for t in range(5):
-                    begin = 16 * (5 * part + t)
-                    out[4 * x + y, begin : begin + 16, :] = block[
-                        16 * x : 16 * (x + 1), 128 * t : 128 * (t + 1)
-                    ]
+    for k in range(blocks):
+        high, low = split(keep[k] + received[k], 2)
+        term = dot(pieces, high) + dot(pieces, low)
+        block = term[:rank] + term[rank : 2 * rank] + term[2 * rank :]
+        for x in range(4):
+            for t in range(5):
+                out[8 * x + k, 16 * t : 16 * (t + 1), :] = block[
+                    16 * x : 16 * (x + 1), 128 * t : 128 * (t + 1)
+                ]
 
 
 def right_factor(mine, theirs, keep, received):
@@ -140,16 +145,16 @@
         right_kernel, "right", 16, 10_000_000,
         in_specs=[vmem] * 4,
         out_specs=[vmem, vmem],
-        out_shape=[shape(16, tall + 8, 128), shape(rows, rank)],
+        out_shape=[shape(32, tall + 8, 128), shape(rows, rank)],
         scratch_shapes=[pltpu.VMEM((rank, rank), f32)],
     )(mine, theirs, keep, received)
 
 
 def plane_sum_kernel(chunks, out):
     total = chunks[0]
-    for j in range(1, 16):
+    for j in range(1, 32):
         total += chunks[j]
-    for z in range(8):
+    for z in range(4):
         out[z] = total
 
 
@@ -158,18 +163,22 @@
         plane_sum_kernel, "plane_sum", 8, 3_000_000,
         in_specs=[vmem],
         out_specs=vmem,
-        out_shape=shape(8, tall + 8, 128),
+        out_shape=shape(4, tall + 8, 128),
     )(chunks)
 
 
 def line_sum_kernel(chunks, out, gram):
     total = chunks[0, :tall, :]
-    for j in range(1, 8):
+    for j in range(1, 4):
         total += chunks[j, :tall, :]
-    for j in range(16):
+    for j in range(32):
         out[j] = total
-    for j in range(8):
-        gram[8 * j : 8 * (j + 1), :] = chunks[j, tall:, :]
+    for j in range(4):
+        pair = chunks[j, tall:, :]
+        gram[16 * j : 16 * j + 8, :] = pair
+        gram[16 * j + 8 : 16 * (j + 1), :] = jnp.concatenate(
+            [pair[:, rank:], pair[:, :rank]], axis=1
+        )
 
 
 def line_sum(chunks):
@@ -177,14 +186,15 @@
         line_sum_kernel, "line_sum", 8, 3_000_000,
         in_specs=[vmem],
         out_specs=[vmem, vmem],
-        out_shape=[shape(16, tall, 128), shape(rank, 2 * rank)],
+        out_shape=[shape(32, tall, 128), shape(rank, 2 * rank)],
     )(chunks)
 
 
 def inverse(gram):
     size = (rank, 2 * rank)
     row = lax.broadcasted_iota(jnp.int32, size, 0)
-    work = jnp.where(lax.broadcasted_iota(jnp.int32, size, 1) == row + rank, 1.0, gram)
+    lane = lax.broadcasted_iota(jnp.int32, size, 1)
+    work = jnp.where(lane < rank, gram, (lane == row + rank).astype(f32))
     step = 8
     for k in range(0, rank, step):
         columns = [jnp.broadcast_to(work[:, k + j : k + j + 1], size) for j in range(step)]
@@ -221,13 +231,10 @@
 
 
 def approx_block(k, factor, right):
-    y, part = k // 2, k % 2
     tiles = []
     for t in range(5):
-        begin = 16 * (5 * part + t)
-        tiles.append(
-            jnp.concatenate([right[4 * x + y, begin : begin + 16, :] for x in range(4)], axis=0)
-        )
+        part = pl.ds(16 * t, 16)
+        tiles.append(jnp.concatenate([right[8 * x + k, part, :] for x in range(4)], axis=0))
     high, low = split(jnp.concatenate(tiles, axis=1), 2)
     return dot(factor, jnp.concatenate([high, low, high], axis=0))
 
@@ -236,7 +243,7 @@
     gram, left, right, merged, weights, momentum, new_error, new_weights, new_momentum, factor,
     held, held_weights, held_momentum, sems, state_sems,
 ):
-    core, z = lax.axis_index("core"), lax.axis_index("z")
+    core, z = lax.axis_index("core"), line_index()
     solved = solve(gram[...], left[...])
     factor[...] = solved
     copies = []
@@ -316,11 +323,11 @@
 def local(drift, error, start, weights, momentum):
     copies, keep, send = left_factor(drift[0], error[0], start.T)
     received = swap(send)
-    mine = lax.all_to_all(copies, "z", 0, 0)
+    mine = lax.all_to_all(copies, ("zh", "zl"), 0, 0)
     chunks, left = right_factor(mine, swap(mine), keep, received)
-    plane = plane_sum(lax.all_to_all(chunks, ("x", "y"), 0, 0))
-    line, gram = line_sum(lax.all_to_all(plane, "z", 0, 0))
-    own = lax.all_to_all(line, ("x", "y"), 0, 0)
+    plane = plane_sum(lax.all_to_all(chunks, ("x", "y", "zl"), 0, 0))
+    line, gram = line_sum(lax.all_to_all(plane, "zh", 0, 0))
+    own = lax.all_to_all(line, ("x", "y", "zl"), 0, 0)
     other = swap(own)
     partial, new_weights, new_momentum, factor = finish_own(
         gram, left, own, keep, weights, momentum
@@ -330,8 +337,8 @@
 
 
 def solution(mesh):
-    fine = Mesh(mesh.devices.reshape(8, 2, 4, 4), ("z", "core", "x", "y"))
-    replica, fsdp = ("z", "core"), ("x", "y")
+    fine = Mesh(mesh.devices.reshape(4, 2, 2, 4, 4), ("zh", "zl", "core", "x", "y"))
+    replica, fsdp = ("zh", "zl", "core"), ("x", "y")
     return jax.shard_map(
         local,
         mesh=fine,

time: 115 us -> 106 us (0.922)
  blocking collectives: 87.8 us -> 79.2 us
    all_to_all x4, blocking collectives: 87.8 us -> 79.2 us  [the longest x1 28.2 us: local(): plane = plane_sum(lax.all_to_all(chunks, ('x', 'y', 'zl'), 0, 0))]
where the time goes in v5:
time: 106 us
  blocking collectives  79.2 us (75%)
  Pallas kernels  17.1 us (16%)
  starting transfers between devices  7.94 us (7%)
  waiting for transfers between devices  1.26 us (1%)
    all_to_all x1, blocking collectives, local(): plane = plane_sum(lax.all_to_all(chunks, ('x', 'y', 'zl'), 0, 0))  28.2 us
    all_to_all x1, blocking collectives, local(): own = lax.all_to_all(line, ('x', 'y', 'zl'), 0, 0)  21 us
    all_to_all x1, blocking collectives, local(): mine = lax.all_to_all(copies, ('zh', 'zl'), 0, 0)  20 us
    all_to_all x1, blocking collectives, local(): line, gram = line_sum(lax.all_to_all(plane, 'zh', 0, 0))  10 us
    pallas_call x1, Pallas kernels, left_factor(): call(left_kernel, 'left', 24, 13000000, in_specs=[hbm, hbm, hbm], out_spe...  8.14 us
    ppermute x3, starting transfers between devices, swap(): return lax.ppermute(value, 'core', [(0, 1), (1, 0)])  7.94 us
    pallas_call x1, Pallas kernels, finish_own(): call(own_kernel, 'own', 16, 16000000, in_specs=[vmem] * 6, out_specs=[hbm...  5.73 us
  transfers between devices with their start and end apart: 3, of which 1 were waited for; matrix products, arithmetic and copies ran while one was open for 0% of the time, Pallas kernels for 5%

profile of v5, /device:TPU:1, one launch (start us, length us, event | category | flops | bytes accessed | tf_op | source)
XLA Modules:
  0.0 106.2 jit_solution(2031291335540899600)
XLA Ops:
  0.6 8.1 %left.1 = (f32[8,80,128]{2,1,0:T(8,128)S(1)}, f32[8,160,640]{2,1,0:T(8,128)S(1)}, f32[8,160,640]{2,1,0:T(8,128)S(1)}) custom-call(bf16[160,10240]{1,0:T(8,128)(2,1)} %bitcast.4, bf16[160,10240]{1,0:T(8,128)(2,1)} %bitcast.5, f32[64,10240]{1,0:T(8,128)} %bitcast.7), custom_call_target="tpu_custom_call" | custom-call | bytes 13000000 | tf_op jit(solution)/shard_map/left/pallas_call | solution.py:94
  8.8 3.3 %collective-permute-start.1 = (f32[8,160,640]{2,1,0:T(8,128)S(1)}, f32[8,160,640]{2,1,0:T(8,128)S(1)}, u32[]{:S(2)}, u32[]{:S(2)}) collective-permute-start(f32[8,160,640]{2,1,0:T(8,128)S(1)} %get-tuple-element.16.merged), channel_id=1, source_target_pairs={{0,16},{16,0},{1,17},{17,1},{2,18},{18,2},{3,19},{19,3},{4,20},{20... | collective-permute-start | bytes 9830408 | tf_op jit(solution)/shard_map/ppermute | solution.py:320
  12.1 20.0 %all_to_all.20.mine = f32[8,80,128]{2,1,0:T(8,128)S(1)} all-to-all(f32[8,80,128]{2,1,0:T(8,128)S(1)} %get-tuple-element.14), channel_id=1, replica_groups=mesh['zh'=4,'zl'=2,'core'=2,'x'=4,'y'=4] {'zh','zl'}, dimensions={0} | all-to-all | bytes 655360 | tf_op jit(solution)/shard_map/all_to_all | solution.py:326
  32.1 0.5 collective-permute-start
  32.6 1.3 %collective-permute-done.theirs = f32[8,80,128]{2,1,0:T(8,128)S(1)} collective-permute-done((f32[8,80,128]{2,1,0:T(8,128)S(1)}, f32[8,80,128]{2,1,0:T(8,128)S(1)}, u32[]{:S(2)}, u32[]{:S(2)}) %collective-permute-start) | collective-permute-done | bytes 327712 | tf_op jit(solution)/shard_map/ppermute | solution.py:320
  33.8 0.0 collective-permute-done.1.received
  33.8 1.6 %right.1 = (f32[32,88,128]{2,1,0:T(8,128)S(1)}, f32[160,64]{1,0:T(8,128)S(1)}) custom-call(f32[8,80,128]{2,1,0:T(8,128)S(1)} %all_to_all.20.mine, f32[8,80,128]{2,1,0:T(8,128)S(1)} %collective-permute-done.theirs, f32[8,160,640]{2,1,0:T(8,128)S(1)} %get-tuple-element.15.keep.merged, f32[8,160,640]{2,1,0:T(8,128)S(1)} %collective-permute-done.1.received), custom_call_target="tpu_custom_call" | custom-call | bytes 10000000 | tf_op jit(solution)/shard_map/right/pallas_call | solution.py:144
  35.4 0.0 copy-start
  35.4 0.0 copy-start.1
  35.5 28.2 %all_to_all.21.chunks = f32[32,88,128]{2,1,0:T(8,128)S(1)} all-to-all(f32[32,88,128]{2,1,0:T(8,128)S(1)} %get-tuple-element.17), channel_id=1, replica_groups=mesh['zh'=4,'zl'=2,'core'=2,'x'=4,'y'=4] {'x','y','zl'}, dimensions={0} | all-to-all | bytes 2883584 | tf_op jit(solution)/shard_map/all_to_all | solution.py:328
  63.6 0.1 plane_sum.1
  63.7 10.0 %all_to_all.22.chunks = f32[4,88,128]{2,1,0:T(8,128)S(1)} all-to-all(f32[4,88,128]{2,1,0:T(8,128)S(1)} %plane_sum.1), channel_id=1, replica_groups=mesh['zh'=4,'zl'=2,'core'=2,'x'=4,'y'=4] {'zh'}, dimensions={0} | all-to-all | bytes 360448 | tf_op jit(solution)/shard_map/all_to_all | solution.py:329
  73.7 0.1 line_sum.1
  73.8 21.0 %all_to_all.23.right = f32[32,80,128]{2,1,0:T(8,128)S(1)} all-to-all(f32[32,80,128]{2,1,0:T(8,128)S(1)} %get-tuple-element.20), channel_id=1, replica_groups=mesh['zh'=4,'zl'=2,'core'=2,'x'=4,'y'=4] {'x','y','zl'}, dimensions={0} | all-to-all | bytes 2621440 | tf_op jit(solution)/shard_map/all_to_all | solution.py:330
  94.8 4.1 %collective-permute-start.2 = (f32[32,80,128]{2,1,0:T(8,128)S(1)}, f32[32,80,128]{2,1,0:T(8,128)S(1)}, u32[]{:S(2)}, u32[]{:S(2)}) collective-permute-start(f32[32,80,128]{2,1,0:T(8,128)S(1)} %all_to_all.23.right), channel_id=1, source_target_pairs={{0,16},{16,0},{1,17},{17,1},{2,18},{18,2},{3,19},{19,3},{4,20},{20... | collective-permute-start | bytes 3932168 | tf_op jit(solution)/shard_map/ppermute | solution.py:320
  99.0 0.0 copy-done
  99.0 0.0 copy-done.1
  99.0 5.7 %own.1 = (bf16[160,10240]{1,0:T(8,128)(2,1)}, f32[160,640]{1,0:T(8,128)}, f32[160,640]{1,0:T(8,128)}, bf16[160,192]{1,0:T(8,128)(2,1)S(1)}) custom-call(f32[64,128]{1,0:T(8,128)S(1)} %get-tuple-element.18.gram, f32[160,64]{1,0:T(8,128)S(1)} %get-tuple-element.19.left, f32[32,80,128]{2,1,0:T(8,128)S(1)} %all_to_all.23.right, ...), custom_call_target="tpu_custom_call" | custom-call | bytes 16000000 | tf_op jit(solution)/shard_map/own/pallas_call | solution.py:273
  104.7 0.0 collective-permute-done.2.right
  104.7 1.5 %other.1 = bf16[160,10240]{1,0:T(8,128)(2,1)} custom-call(bf16[160,192]{1,0:T(8,128)(2,1)S(1)} %get-tuple-element.22.factor, f32[32,80,128]{2,1,0:T(8,128)S(1)} %collective-permute-done.2.right, f32[8,160,640]{2,1,0:T(8,128)S(1)} %get-tuple-element.16.merged, bf16[160,10240]{1,0:T(8,128)(2,1)} %get-tuple-element.23.partial), custom_call_target="tpu_custom_call", output_to_operand_aliasing={{}: (3, {})} | custom-call | bytes 8000000 | tf_op jit(solution)/shard_map/other/pallas_call | solution.py:306
Async XLA Ops:
  8.8 25.1 %collective-permute-start.1 = (f32[8,160,640]{2,1,0:T(8,128)S(1)}, f32[8,160,640]{2,1,0:T(8,128)S(1)}, u32[]{:S(2)}, u32[]{:S(2)}) collective-permute-start(f32[8,160,640]{2,1,0:T(8,128)S(1)} %get-tuple-element.16.merged), channel_id=1, source_target_pairs={{0,16},{16,0},{1,17},{17,1},{2,18},{18,2},{3,19},{19,3},{4,20},{20... | collective-permute-start | bytes 9830408 | tf_op jit(solution)/shard_map/ppermute | solution.py:320
  32.1 1.7 %collective-permute-start = (f32[8,80,128]{2,1,0:T(8,128)S(1)}, f32[8,80,128]{2,1,0:T(8,128)S(1)}, u32[]{:S(2)}, u32[]{:S(2)}) collective-permute-start(f32[8,80,128]{2,1,0:T(8,128)S(1)} %all_to_all.20.mine), channel_id=1, source_target_pairs={{0,16},{16,0},{1,17},{17,1},{2,18},{18,2},{3,19},{19,3},{4,20},{20... | collective-permute-start | bytes 983048 | tf_op jit(solution)/shard_map/ppermute | solution.py:320
  35.4 63.5 %copy-start = (f32[160,640]{1,0:T(8,128)S(1)}, f32[160,640]{1,0:T(8,128)}, u32[]{:S(2)}) copy-start(f32[160,640]{1,0:T(8,128)} %weights.1) | copy-start | bytes 1228804
  35.4 63.5 %copy-start.1 = (f32[160,640]{1,0:T(8,128)S(1)}, f32[160,640]{1,0:T(8,128)}, u32[]{:S(2)}) copy-start(f32[160,640]{1,0:T(8,128)} %momentum.1) | copy-start | bytes 1228804
  94.8 9.9 %collective-permute-start.2 = (f32[32,80,128]{2,1,0:T(8,128)S(1)}, f32[32,80,128]{2,1,0:T(8,128)S(1)}, u32[]{:S(2)}, u32[]{:S(2)}) collective-permute-start(f32[32,80,128]{2,1,0:T(8,128)S(1)} %all_to_all.23.right), channel_id=1, source_target_pairs={{0,16},{16,0},{1,17},{17,1},{2,18},{18,2},{3,19},{19,3},{4,20},{20... | collective-permute-start | bytes 3932168 | tf_op jit(solution)/shard_map/ppermute | solution.py:320

commit v6 on v5

--- a/solution.py
+++ b/solution.py
@@ -16,6 +16,8 @@
 blocks = 8
 groups = 16
 tall = 80
+reads = 4
+chunk = cols // reads
 f32 = jnp.float32
 bf16 = jnp.bfloat16
 exact = lax.Precision.HIGHEST
@@ -56,58 +58,86 @@
     return jax.ShapeDtypeStruct(dims, dtype)
 
 
-def left_kernel(drift, error, start, out, keep, send, drifts, errors, starts, acc, sems):
+def pack(value):
+    count = value.shape[0] // 2
+    return jnp.concatenate([value[:count], value[count:]], axis=1)
+
+
+def unpack(value):
+    return jnp.concatenate([value[:, :rank], value[:, rank:]], axis=0)
+
+
+def left_kernel(drift, error, start, mine, theirs, keep, send, drifts, errors, starts, acc, sems):
     first = lax.axis_index("core") == 0
     copies = []
-    for i in range(blocks):
-        lanes = pl.ds(i * wide, wide)
-        mine = [
+    for i in range(reads):
+        lanes = pl.ds(i * chunk, chunk)
+        group = [
             pltpu.make_async_copy(start.at[:, lanes], starts.at[i], sems.at[i, 0]),
             pltpu.make_async_copy(drift.at[:, lanes], drifts.at[i], sems.at[i, 1]),
             pltpu.make_async_copy(error.at[:, lanes], errors.at[i], sems.at[i, 2]),
         ]
-        for copy in mine:
+        for copy in group:
             copy.start()
-        copies.append(mine)
-    for i in range(blocks):
+        copies.append(group)
+    for i in range(reads):
         for copy in copies[i]:
             copy.wait()
         both = jnp.concatenate([drifts[i], errors[i]], axis=0)
-        factor = jnp.concatenate(split(starts[i], 3), axis=0)
-        term = dot_rows(both, factor)
+        term = dot_rows(both, jnp.concatenate(split(starts[i], 2), axis=0))
         if i == 0:
             acc[...] = term
         else:
             acc[...] += term
         merged = drifts[i].astype(f32) + errors[i].astype(f32)
-        even, odd = merged[:, :narrow], merged[:, narrow:]
-        keep[i] = jnp.where(first, even, odd)
-        send[i] = jnp.where(first, odd, even)
+        for j in range(chunk // wide):
+            even = merged[:, wide * j : wide * j + narrow]
+            odd = merged[:, wide * j + narrow : wide * (j + 1)]
+            k = i * (chunk // wide) + j
+            keep[k] = jnp.where(first, even, odd)
+            send[k] = jnp.where(first, odd, even)
     total = acc[:rows, :] + acc[rows:, :]
-    left = total[:, :rank] + total[:, rank : 2 * rank] + total[:, 2 * rank :]
-    packed = jnp.concatenate([left[: rows // 2], left[rows // 2 :]], axis=1)
-    for z in range(8):
-        out[z] = packed
+    left = total[:, :rank] + total[:, rank:]
+    upper, lower = pack(left[: rows // 2]), pack(left[rows // 2 :])
+    mine[...] = jnp.where(first, upper, lower)
+    theirs[...] = jnp.where(first, lower, upper)
 
 
 def left_factor(drift, error, start):
+    inputs = [pltpu.with_memory_space_constraint(v, pltpu.HBM) for v in (drift, error, start)]
     return call(
         left_kernel, "left", 24, 13_000_000,
         in_specs=[hbm, hbm, hbm],
-        out_specs=[vmem, vmem, vmem],
+        out_specs=[vmem] * 4,
         out_shape=[
-            pltpu.VMEM((8, rows // 2, 2 * rank), f32),
+            pltpu.VMEM((rows // 4, 2 * rank), f32),
+            pltpu.VMEM((rows // 4, 2 * rank), f32),
             pltpu.VMEM((blocks, rows, narrow), f32),
             pltpu.VMEM((blocks, rows, narrow), f32),
         ],
         scratch_shapes=[
-            pltpu.VMEM((blocks, rows, wide), bf16),
-            pltpu.VMEM((blocks, rows, wide), bf16),
-            pltpu.VMEM((blocks, rank, wide), f32),
-            pltpu.VMEM((2 * rows, 3 * rank), f32),
-            pltpu.SemaphoreType.DMA((blocks, 3)),
-        ],
-    )(*[pltpu.with_memory_space_constraint(value, pltpu.HBM) for value in (drift, error, start)])
+            pltpu.VMEM((reads, rows, chunk), bf16),
+            pltpu.VMEM((reads, rows, chunk), bf16),
+            pltpu.VMEM((reads, rank, chunk), f32),
+            pltpu.VMEM((2 * rows, 2 * rank), f32),
+            pltpu.SemaphoreType.DMA((reads, 3)),
+        ],
+    )(*inputs)
+
+
+def pair_sum_kernel(mine, received, out):
+    total = mine[...] + received[...]
+    for z in range(8):
+        out[z] = total
+
+
+def pair_sum(mine, received):
+    return call(
+        pair_sum_kernel, "pair_sum", 4, 500_000,
+        in_specs=[vmem, vmem],
+        out_specs=vmem,
+        out_shape=shape(8, rows // 4, 2 * rank),
+    )(mine, received)
 
 
 def line_index():
@@ -115,8 +145,10 @@
 
 
 def right_kernel(mine, theirs, keep, received, out, left_out, gram):
-    total = (jnp.sum(mine[...], axis=0) + jnp.sum(theirs[...], axis=0)) * (1.0 / groups)
-    left = jnp.concatenate([total[:, :rank], total[:, rank:]], axis=0)
+    own = unpack(jnp.sum(mine[...], axis=0)) * (1.0 / groups)
+    other = unpack(jnp.sum(theirs[...], axis=0)) * (1.0 / groups)
+    first = lax.axis_index("core") == 0
+    left = jnp.concatenate([jnp.where(first, own, other), jnp.where(first, other, own)], axis=0)
     left_out[...] = left
     turned = left.T
     pieces = jnp.concatenate(split(turned, 3), axis=0)
@@ -321,9 +353,10 @@
 
 
 def local(drift, error, start, weights, momentum):
-    copies, keep, send = left_factor(drift[0], error[0], start.T)
+    mine, theirs, keep, send = left_factor(drift[0], error[0], start.T)
+    theirs, send = lax.optimization_barrier((swap(theirs), send))
     received = swap(send)
-    mine = lax.all_to_all(copies, ("zh", "zl"), 0, 0)
+    mine = lax.all_to_all(pair_sum(mine, theirs), ("zh", "zl"), 0, 0)
     chunks, left = right_factor(mine, swap(mine), keep, received)
     plane = plane_sum(lax.all_to_all(chunks, ("x", "y", "zl"), 0, 0))
     line, gram = line_sum(lax.all_to_all(plane, "zh", 0, 0))

time: 106 us -> 104 us (0.981)
  blocking collectives: 79.2 us -> 75 us
  starting transfers between devices: 7.94 us -> 9.37 us
    all_to_all x1, blocking collectives: 20 us -> 15.3 us  [local(): mine = lax.all_to_all(pair_sum(mine, theirs), ('zh', 'zl'), 0, 0)]
    ppermute x3 -> x4, starting transfers between devices: 7.94 us -> 9.37 us  [swap(): return lax.ppermute(value, 'core', [(0, 1), (1, 0)])]
  transfers between devices with their start and end apart: 3 -> 4, of which waited for: 1 -> 2; matrix products, arithmetic and copies ran while one was open for 0% -> 0% of each run, Pallas kernels for 5% -> 6%
where the time goes in v6:
time: 104 us
  blocking collectives  75 us (72%)
  Pallas kernels  16.6 us (16%)
  starting transfers between devices  9.37 us (9%)
  waiting for transfers between devices  1.88 us (2%)
    all_to_all x1, blocking collectives, local(): plane = plane_sum(lax.all_to_all(chunks, ('x', 'y', 'zl'), 0, 0))  28.2 us
    all_to_all x1, blocking collectives, local(): own = lax.all_to_all(line, ('x', 'y', 'zl'), 0, 0)  21.7 us
    all_to_all x1, blocking collectives, local(): mine = lax.all_to_all(pair_sum(mine, theirs), ('zh', 'zl'), 0, 0)  15.3 us
    all_to_all x1, blocking collectives, local(): line, gram = line_sum(lax.all_to_all(plane, 'zh', 0, 0))  9.85 us
    ppermute x4, starting transfers between devices, swap(): return lax.ppermute(value, 'core', [(0, 1), (1, 0)])  9.37 us
    pallas_call x1, Pallas kernels, left_factor(): call(left_kernel, 'left', 24, 13000000, in_specs=[hbm, hbm, hbm], out_spe...  7.52 us
    pallas_call x1, Pallas kernels, finish_own(): call(own_kernel, 'own', 16, 16000000, in_specs=[vmem] * 6, out_specs=[hbm...  5.73 us
  transfers between devices with their start and end apart: 4, of which 2 were waited for; matrix products, arithmetic and copies ran while one was open for 0% of the time, Pallas kernels for 6%

profile of v6, /device:TPU:1, one launch (start us, length us, event | category | flops | bytes accessed | tf_op | source)
XLA Modules:
  0.0 103.5 jit_solution(3687363217992217450)
XLA Ops:
  0.6 7.5 %left.1 = (f32[40,128]{1,0:T(8,128)S(1)}, f32[40,128]{1,0:T(8,128)S(1)}, f32[8,160,640]{2,1,0:T(8,128)S(1)}, f32[8,160,640]{2,1,0:T(8,128)S(1)}) custom-call(bf16[160,10240]{1,0:T(8,128)(2,1)} %bitcast.4, bf16[160,10240]{1,0:T(8,128)(2,1)} %bitcast.5, f32[64,10240]{1,0:T(8,128)} %bitcast.7), custom_call_target="tpu_custom_call" | custom-call | bytes 13000000 | tf_op jit(solution)/shard_map/left/pallas_call | solution.py:108
  8.2 3.3 %collective-permute-start = (f32[40,128]{1,0:T(8,128)S(1)}, f32[40,128]{1,0:T(8,128)S(1)}, u32[]{:S(2)}, u32[]{:S(2)}) collective-permute-start(f32[40,128]{1,0:T(8,128)S(1)} %get-tuple-element.18), channel_id=1, source_target_pairs={{0,16},{16,0},{1,17},{17,1},{2,18},{18,2},{3,19},{19,3},{4,20},{20... | collective-permute-start | bytes 61448 | tf_op jit(solution)/shard_map/ppermute | solution.py:352
  11.5 0.8 collective-permute-done.received
  12.3 0.3 collective-permute-start.2
  12.7 15.3 %all_to_all.20.mine = f32[8,40,128]{2,1,0:T(8,128)S(1)} all-to-all(f32[8,40,128]{2,1,0:T(8,128)S(1)} %pair_sum.1), channel_id=1, replica_groups=mesh['zh'=4,'zl'=2,'core'=2,'x'=4,'y'=4] {'zh','zl'}, dimensions={0} | all-to-all | bytes 327680 | tf_op jit(solution)/shard_map/all_to_all | solution.py:359
  27.9 1.7 %collective-permute-start.1 = (f32[8,40,128]{2,1,0:T(8,128)S(1)}, f32[8,40,128]{2,1,0:T(8,128)S(1)}, u32[]{:S(2)}, u32[]{:S(2)}) collective-permute-start(f32[8,40,128]{2,1,0:T(8,128)S(1)} %all_to_all.20.mine), channel_id=1, source_target_pairs={{0,16},{16,0},{1,17},{17,1},{2,18},{18,2},{3,19},{19,3},{4,20},{20... | collective-permute-start | bytes 491528 | tf_op jit(solution)/shard_map/ppermute | solution.py:352
  29.7 1.0 collective-permute-done.1.theirs
  30.7 0.0 collective-permute-done.2.received
  30.7 1.6 %right.1 = (f32[32,88,128]{2,1,0:T(8,128)S(1)}, f32[160,64]{1,0:T(8,128)S(1)}) custom-call(f32[8,40,128]{2,1,0:T(8,128)S(1)} %all_to_all.20.mine, f32[8,40,128]{2,1,0:T(8,128)S(1)} %collective-permute-done.1.theirs, f32[8,160,640]{2,1,0:T(8,128)S(1)} %get-tuple-element.21.keep.merged, f32[8,160,640]{2,1,0:T(8,128)S(1)} %collective-permute-done.2.received), custom_call_target="tpu_custom_call" | custom-call | bytes 10000000 | tf_op jit(solution)/shard_map/right/pallas_call | solution.py:176
  32.3 0.0 copy-start
  32.4 0.0 copy-start.1
  32.4 28.2 %all_to_all.21.chunks = f32[32,88,128]{2,1,0:T(8,128)S(1)} all-to-all(f32[32,88,128]{2,1,0:T(8,128)S(1)} %get-tuple-element.23), channel_id=1, replica_groups=mesh['zh'=4,'zl'=2,'core'=2,'x'=4,'y'=4] {'x','y','zl'}, dimensions={0} | all-to-all | bytes 2883584 | tf_op jit(solution)/shard_map/all_to_all | solution.py:361
  60.6 0.1 plane_sum.1
  60.7 9.9 %all_to_all.22.chunks = f32[4,88,128]{2,1,0:T(8,128)S(1)} all-to-all(f32[4,88,128]{2,1,0:T(8,128)S(1)} %plane_sum.1), channel_id=1, replica_groups=mesh['zh'=4,'zl'=2,'core'=2,'x'=4,'y'=4] {'zh'}, dimensions={0} | all-to-all | bytes 360448 | tf_op jit(solution)/shard_map/all_to_all | solution.py:362
  70.5 0.1 line_sum.1
  70.6 21.7 %all_to_all.23.right = f32[32,80,128]{2,1,0:T(8,128)S(1)} all-to-all(f32[32,80,128]{2,1,0:T(8,128)S(1)} %get-tuple-element.26), channel_id=1, replica_groups=mesh['zh'=4,'zl'=2,'core'=2,'x'=4,'y'=4] {'x','y','zl'}, dimensions={0} | all-to-all | bytes 2621440 | tf_op jit(solution)/shard_map/all_to_all | solution.py:363
  92.3 4.0 %collective-permute-start.3 = (f32[32,80,128]{2,1,0:T(8,128)S(1)}, f32[32,80,128]{2,1,0:T(8,128)S(1)}, u32[]{:S(2)}, u32[]{:S(2)}) collective-permute-start(f32[32,80,128]{2,1,0:T(8,128)S(1)} %all_to_all.23.right), channel_id=1, source_target_pairs={{0,16},{16,0},{1,17},{17,1},{2,18},{18,2},{3,19},{19,3},{4,20},{20... | collective-permute-start | bytes 3932168 | tf_op jit(solution)/shard_map/ppermute | solution.py:352
  96.3 0.0 copy-done
  96.3 0.0 copy-done.1
  96.3 5.7 %own.1 = (bf16[160,10240]{1,0:T(8,128)(2,1)}, f32[160,640]{1,0:T(8,128)}, f32[160,640]{1,0:T(8,128)}, bf16[160,192]{1,0:T(8,128)(2,1)S(1)}) custom-call(f32[64,128]{1,0:T(8,128)S(1)} %get-tuple-element.24.gram, f32[160,64]{1,0:T(8,128)S(1)} %get-tuple-element.25.left, f32[32,80,128]{2,1,0:T(8,128)S(1)} %all_to_all.23.right, ...), custom_call_target="tpu_custom_call" | custom-call | bytes 16000000 | tf_op jit(solution)/shard_map/own/pallas_call | solution.py:305
  102.0 0.0 collective-permute-done.3.right
  102.0 1.5 %other.1 = bf16[160,10240]{1,0:T(8,128)(2,1)} custom-call(bf16[160,192]{1,0:T(8,128)(2,1)S(1)} %get-tuple-element.28.factor, f32[32,80,128]{2,1,0:T(8,128)S(1)} %collective-permute-done.3.right, f32[8,160,640]{2,1,0:T(8,128)S(1)} %get-tuple-element.22.merged, bf16[160,10240]{1,0:T(8,128)(2,1)} %get-tuple-element.29.partial), custom_call_target="tpu_custom_call", output_to_operand_aliasing={{}: (3, {})} | custom-call | bytes 8000000 | tf_op jit(solution)/shard_map/other/pallas_call | solution.py:338
  (1 shorter events, 0.0 us)
Async XLA Ops:
  8.2 4.2 %collective-permute-start = (f32[40,128]{1,0:T(8,128)S(1)}, f32[40,128]{1,0:T(8,128)S(1)}, u32[]{:S(2)}, u32[]{:S(2)}) collective-permute-start(f32[40,128]{1,0:T(8,128)S(1)} %get-tuple-element.18), channel_id=1, source_target_pairs={{0,16},{16,0},{1,17},{17,1},{2,18},{18,2},{3,19},{19,3},{4,20},{20... | collective-permute-start | bytes 61448 | tf_op jit(solution)/shard_map/ppermute | solution.py:352
  12.3 18.4 %collective-permute-start.2 = (f32[8,160,640]{2,1,0:T(8,128)S(1)}, f32[8,160,640]{2,1,0:T(8,128)S(1)}, u32[]{:S(2)}, u32[]{:S(2)}) collective-permute-start(f32[8,160,640]{2,1,0:T(8,128)S(1)} %get-tuple-element.22.merged), channel_id=1, source_target_pairs={{0,16},{16,0},{1,17},{17,1},{2,18},{18,2},{3,19},{19,3},{4,20},{20... | collective-permute-start | bytes 9830408 | tf_op jit(solution)/shard_map/ppermute | solution.py:352
  27.9 2.8 %collective-permute-start.1 = (f32[8,40,128]{2,1,0:T(8,128)S(1)}, f32[8,40,128]{2,1,0:T(8,128)S(1)}, u32[]{:S(2)}, u32[]{:S(2)}) collective-permute-start(f32[8,40,128]{2,1,0:T(8,128)S(1)} %all_to_all.20.mine), channel_id=1, source_target_pairs={{0,16},{16,0},{1,17},{17,1},{2,18},{18,2},{3,19},{19,3},{4,20},{20... | collective-permute-start | bytes 491528 | tf_op jit(solution)/shard_map/ppermute | solution.py:352
  32.3 63.9 %copy-start = (f32[160,640]{1,0:T(8,128)S(1)}, f32[160,640]{1,0:T(8,128)}, u32[]{:S(2)}) copy-start(f32[160,640]{1,0:T(8,128)} %weights.1) | copy-start | bytes 1228804
  32.4 63.9 %copy-start.1 = (f32[160,640]{1,0:T(8,128)S(1)}, f32[160,640]{1,0:T(8,128)}, u32[]{:S(2)}) copy-start(f32[160,640]{1,0:T(8,128)} %momentum.1) | copy-start | bytes 1228804
  92.3 9.7 %collective-permute-start.3 = (f32[32,80,128]{2,1,0:T(8,128)S(1)}, f32[32,80,128]{2,1,0:T(8,128)S(1)}, u32[]{:S(2)}, u32[]{:S(2)}) collective-permute-start(f32[32,80,128]{2,1,0:T(8,128)S(1)} %all_to_all.23.right), channel_id=1, source_target_pairs={{0,16},{16,0},{1,17},{17,1},{2,18},{18,2},{3,19},{19,3},{4,20},{20... | collective-permute-start | bytes 3932168 | tf_op jit(solution)/shard_map/ppermute | solution.py:352

commit v7 on v6

--- a/solution.py
+++ b/solution.py
@@ -69,27 +69,28 @@
 
 def left_kernel(drift, error, start, mine, theirs, keep, send, drifts, errors, starts, acc, sems):
     first = lax.axis_index("core") == 0
-    copies = []
-    for i in range(reads):
-        lanes = pl.ds(i * chunk, chunk)
-        group = [
+
+    def copies(i):
+        lanes = pl.ds(pl.multiple_of(i * chunk, chunk), chunk)
+        return [
             pltpu.make_async_copy(start.at[:, lanes], starts.at[i], sems.at[i, 0]),
             pltpu.make_async_copy(drift.at[:, lanes], drifts.at[i], sems.at[i, 1]),
             pltpu.make_async_copy(error.at[:, lanes], errors.at[i], sems.at[i, 2]),
         ]
-        for copy in group:
+
+    for i in range(reads):
+        for copy in copies(i):
             copy.start()
-        copies.append(group)
-    for i in range(reads):
-        for copy in copies[i]:
+    acc[...] = jnp.zeros_like(acc)
+
+    @pl.loop(0, reads)
+    def _(i):
+        for copy in copies(i):
             copy.wait()
-        both = jnp.concatenate([drifts[i], errors[i]], axis=0)
-        term = dot_rows(both, jnp.concatenate(split(starts[i], 2), axis=0))
-        if i == 0:
-            acc[...] = term
-        else:
-            acc[...] += term
-        merged = drifts[i].astype(f32) + errors[i].astype(f32)
+        first_part, second_part = drifts[i], errors[i]
+        merged = first_part.astype(f32) + second_part.astype(f32)
+        both = jnp.concatenate([first_part, second_part], axis=0)
+        acc[...] += dot_rows(both, jnp.concatenate(split(starts[i], 2), axis=0))
         for j in range(chunk // wide):
             even = merged[:, wide * j : wide * j + narrow]
             odd = merged[:, wide * j + narrow : wide * (j + 1)]
@@ -161,6 +162,7 @@
     )
     for j in range(32):
         out[j, tall:, :] = padded
+
     for k in range(blocks):
         high, low = split(keep[k] + received[k], 2)
         term = dot(pieces, high) + dot(pieces, low)
@@ -228,10 +230,15 @@
     lane = lax.broadcasted_iota(jnp.int32, size, 1)
     work = jnp.where(lane < rank, gram, (lane == row + rank).astype(f32))
     step = 8
-    for k in range(0, rank, step):
-        columns = [jnp.broadcast_to(work[:, k + j : k + j + 1], size) for j in range(step)]
-        block = [[columns[j][k + i : k + i + 1, :] for j in range(step)] for i in range(step)]
-        pivots = [work[k + i : k + i + 1, :] for i in range(step)]
+    count = rank // step
+
+    def eliminate(_, work):
+        columns = [
+            [jnp.broadcast_to(part[:, j : j + 1], (step, 2 * rank)) for j in range(step)]
+            for part in work
+        ]
+        block = [[columns[0][j][i : i + 1, :] for j in range(step)] for i in range(step)]
+        pivots = [work[0][i : i + 1, :] for i in range(step)]
         for j in range(step):
             scale = 1.0 / block[j][j]
             pivots[j] = pivots[j] * scale
@@ -242,11 +249,17 @@
                     pivots[i] = pivots[i] - block[i][j] * pivots[j]
                     for m in range(j + 1, step):
                         block[i][m] = block[i][m] - block[i][j] * block[j][m]
-        for j in range(step):
-            work = work - columns[j] * pivots[j]
-        for j in range(step):
-            work = jnp.where(row == k + j, pivots[j], work)
-    return work[:, rank:]
+        done = []
+        for part, factors in zip(work[1:], columns[1:]):
+            for j in range(step):
+                part = part - factors[j] * pivots[j]
+            done.append(part)
+        done.append(jnp.concatenate(pivots, axis=0))
+        return tuple(pltpu.roll(part, 2 * rank - step, axis=1) for part in done)
+
+    parts = tuple(work[step * i : step * (i + 1)] for i in range(count))
+    parts = lax.fori_loop(0, count, eliminate, parts)
+    return jnp.concatenate(parts, axis=0)[:, :rank]
 
 
 def solve(gram, left):
@@ -276,18 +289,13 @@
     held, held_weights, held_momentum, sems, state_sems,
 ):
     core, z = lax.axis_index("core"), line_index()
-    solved = solve(gram[...], left[...])
-    factor[...] = solved
-    copies = []
-    state = [
-        pltpu.make_async_copy(held_weights, new_weights, state_sems.at[0]),
-        pltpu.make_async_copy(held_momentum, new_momentum, state_sems.at[1]),
-    ]
-    for k in range(blocks):
-        approx = approx_block(k, solved, right)
+    factor[...] = solve(gram[...], left[...])
+
+    @pl.loop(0, blocks)
+    def _(k):
+        approx = approx_block(k, factor[...], right)
         held[k] = (merged[k] - approx).astype(bf16)
-        copies.append(block_copy(k, core, held, new_error, sems))
-        copies[-1].start()
+        block_copy(k, core, held, new_error, sems).start()
 
         @pl.when(z == k)
         def _():
@@ -295,9 +303,18 @@
             held_momentum[...] = moved
             held_weights[...] = weights[...] - outer_rate * (approx + momentum_decay * moved)
 
+    state = [
+        pltpu.make_async_copy(held_weights, new_weights, state_sems.at[0]),
+        pltpu.make_async_copy(held_momentum, new_momentum, state_sems.at[1]),
+    ]
     for copy in state:
         copy.start()
-    for copy in copies + state:
+
+    @pl.loop(0, blocks)
+    def _(k):
+        block_copy(k, core, held, new_error, sems).wait()
+
+    for copy in state:
         copy.wait()
 
 
@@ -324,14 +341,14 @@
 
 def other_kernel(factor, right, merged, partial, new_error, held, sems):
     offset = 1 - lax.axis_index("core")
-    left = factor[...]
-    copies = []
+
     for k in range(blocks):
-        held[k] = (merged[k] - approx_block(k, left, right)).astype(bf16)
-        copies.append(block_copy(k, offset, held, new_error, sems))
-        copies[-1].start()
-    for copy in copies:
-        copy.wait()
+        held[k] = (merged[k] - approx_block(k, factor[...], right)).astype(bf16)
+        block_copy(k, offset, held, new_error, sems).start()
+
+    @pl.loop(0, blocks)
+    def _(k):
+        block_copy(k, offset, held, new_error, sems).wait()
 
 
 def finish_other(factor, right, merged, partial):

time: 104 us -> 101 us (0.971)
  Pallas kernels: 16.6 us -> 13.4 us
    pallas_call x1, Pallas kernels: 7.52 us -> 4.57 us  [left_factor(): call(left_kernel, 'left', 24, 13000000, in_specs=[hbm, hbm, hbm], out_spe...]
  transfers between devices with their start and end apart: 4 -> 4, of which waited for: 2 -> 2; matrix products, arithmetic and copies ran while one was open for 0% -> 0% of each run, Pallas kernels for 6% -> 5%
where the time goes in v7:
time: 101 us; the launch traced here: 100 us
  blocking collectives  75 us (74%)
  Pallas kernels  13.4 us (13%)
  starting transfers between devices  9.39 us (9%)
  waiting for transfers between devices  1.88 us (2%)
    all_to_all x1, blocking collectives, local(): plane = plane_sum(lax.all_to_all(chunks, ('x', 'y', 'zl'), 0, 0))  28.2 us
    all_to_all x1, blocking collectives, local(): own = lax.all_to_all(line, ('x', 'y', 'zl'), 0, 0)  21.7 us
    all_to_all x1, blocking collectives, local(): mine = lax.all_to_all(pair_sum(mine, theirs), ('zh', 'zl'), 0, 0)  15.3 us
    all_to_all x1, blocking collectives, local(): line, gram = line_sum(lax.all_to_all(plane, 'zh', 0, 0))  9.85 us
    ppermute x4, starting transfers between devices, swap(): return lax.ppermute(value, 'core', [(0, 1), (1, 0)])  9.39 us
    pallas_call x1, Pallas kernels, finish_own(): call(own_kernel, 'own', 16, 16000000, in_specs=[vmem] * 6, out_specs=[hbm...  5.46 us
    pallas_call x1, Pallas kernels, left_factor(): call(left_kernel, 'left', 24, 13000000, in_specs=[hbm, hbm, hbm], out_spe...  4.57 us
  transfers between devices with their start and end apart: 4, of which 2 were waited for; matrix products, arithmetic and copies ran while one was open for 0% of the time, Pallas kernels for 5%

profile of v7, /device:TPU:1, one launch (start us, length us, event | category | flops | bytes accessed | tf_op | source)
XLA Modules:
  0.0 100.3 jit_solution(8646914797134741742)
XLA Ops:
  0.6 4.6 %left.1 = (f32[40,128]{1,0:T(8,128)S(1)}, f32[40,128]{1,0:T(8,128)S(1)}, f32[8,160,640]{2,1,0:T(8,128)S(1)}, f32[8,160,640]{2,1,0:T(8,128)S(1)}) custom-call(bf16[160,10240]{1,0:T(8,128)(2,1)} %bitcast.4, bf16[160,10240]{1,0:T(8,128)(2,1)} %bitcast.5, f32[64,10240]{1,0:T(8,128)} %bitcast.7), custom_call_target="tpu_custom_call" | custom-call | bytes 13000000 | tf_op jit(solution)/shard_map/left/pallas_call | solution.py:109
  5.2 3.3 %collective-permute-start = (f32[40,128]{1,0:T(8,128)S(1)}, f32[40,128]{1,0:T(8,128)S(1)}, u32[]{:S(2)}, u32[]{:S(2)}) collective-permute-start(f32[40,128]{1,0:T(8,128)S(1)} %get-tuple-element.18), channel_id=1, source_target_pairs={{0,16},{16,0},{1,17},{17,1},{2,18},{18,2},{3,19},{19,3},{4,20},{20... | collective-permute-start | bytes 61448 | tf_op jit(solution)/shard_map/ppermute | solution.py:369
  8.5 0.8 collective-permute-done.received
  9.4 0.3 collective-permute-start.2
  9.7 15.3 %all_to_all.20.mine = f32[8,40,128]{2,1,0:T(8,128)S(1)} all-to-all(f32[8,40,128]{2,1,0:T(8,128)S(1)} %pair_sum.1), channel_id=1, replica_groups=mesh['zh'=4,'zl'=2,'core'=2,'x'=4,'y'=4] {'zh','zl'}, dimensions={0} | all-to-all | bytes 327680 | tf_op jit(solution)/shard_map/all_to_all | solution.py:376
  25.0 1.7 %collective-permute-start.1 = (f32[8,40,128]{2,1,0:T(8,128)S(1)}, f32[8,40,128]{2,1,0:T(8,128)S(1)}, u32[]{:S(2)}, u32[]{:S(2)}) collective-permute-start(f32[8,40,128]{2,1,0:T(8,128)S(1)} %all_to_all.20.mine), channel_id=1, source_target_pairs={{0,16},{16,0},{1,17},{17,1},{2,18},{18,2},{3,19},{19,3},{4,20},{20... | collective-permute-start | bytes 491528 | tf_op jit(solution)/shard_map/ppermute | solution.py:369
  26.7 1.0 %collective-permute-done.1.theirs = f32[8,40,128]{2,1,0:T(8,128)S(1)} collective-permute-done((f32[8,40,128]{2,1,0:T(8,128)S(1)}, f32[8,40,128]{2,1,0:T(8,128)S(1)}, u32[]{:S(2)}, u32[]{:S(2)}) %collective-permute-start.1) | collective-permute-done | bytes 163872 | tf_op jit(solution)/shard_map/ppermute | solution.py:369
  27.7 0.0 collective-permute-done.2.received
  27.7 1.6 %right.1 = (f32[32,88,128]{2,1,0:T(8,128)S(1)}, f32[160,64]{1,0:T(8,128)S(1)}) custom-call(f32[8,40,128]{2,1,0:T(8,128)S(1)} %all_to_all.20.mine, f32[8,40,128]{2,1,0:T(8,128)S(1)} %collective-permute-done.1.theirs, f32[8,160,640]{2,1,0:T(8,128)S(1)} %get-tuple-element.21.keep.merged, f32[8,160,640]{2,1,0:T(8,128)S(1)} %collective-permute-done.2.received), custom_call_target="tpu_custom_call" | custom-call | bytes 10000000 | tf_op jit(solution)/shard_map/right/pallas_call | solution.py:178
  29.4 0.0 copy-start
  29.4 0.0 copy-start.1
  29.4 28.2 %all_to_all.21.chunks = f32[32,88,128]{2,1,0:T(8,128)S(1)} all-to-all(f32[32,88,128]{2,1,0:T(8,128)S(1)} %get-tuple-element.23), channel_id=1, replica_groups=mesh['zh'=4,'zl'=2,'core'=2,'x'=4,'y'=4] {'x','y','zl'}, dimensions={0} | all-to-all | bytes 2883584 | tf_op jit(solution)/shard_map/all_to_all | solution.py:378
  57.6 0.1 plane_sum.1
  57.7 9.9 %all_to_all.22.chunks = f32[4,88,128]{2,1,0:T(8,128)S(1)} all-to-all(f32[4,88,128]{2,1,0:T(8,128)S(1)} %plane_sum.1), channel_id=1, replica_groups=mesh['zh'=4,'zl'=2,'core'=2,'x'=4,'y'=4] {'zh'}, dimensions={0} | all-to-all | bytes 360448 | tf_op jit(solution)/shard_map/all_to_all | solution.py:379
  67.6 0.1 line_sum.1
  67.7 21.7 %all_to_all.23.right = f32[32,80,128]{2,1,0:T(8,128)S(1)} all-to-all(f32[32,80,128]{2,1,0:T(8,128)S(1)} %get-tuple-element.26), channel_id=1, replica_groups=mesh['zh'=4,'zl'=2,'core'=2,'x'=4,'y'=4] {'x','y','zl'}, dimensions={0} | all-to-all | bytes 2621440 | tf_op jit(solution)/shard_map/all_to_all | solution.py:380
  89.3 4.0 %collective-permute-start.3 = (f32[32,80,128]{2,1,0:T(8,128)S(1)}, f32[32,80,128]{2,1,0:T(8,128)S(1)}, u32[]{:S(2)}, u32[]{:S(2)}) collective-permute-start(f32[32,80,128]{2,1,0:T(8,128)S(1)} %all_to_all.23.right), channel_id=1, source_target_pairs={{0,16},{16,0},{1,17},{17,1},{2,18},{18,2},{3,19},{19,3},{4,20},{20... | collective-permute-start | bytes 3932168 | tf_op jit(solution)/shard_map/ppermute | solution.py:369
  93.3 0.0 copy-done
  93.3 0.0 copy-done.1
  93.3 5.5 %own.1 = (bf16[160,10240]{1,0:T(8,128)(2,1)}, f32[160,640]{1,0:T(8,128)}, f32[160,640]{1,0:T(8,128)}, bf16[160,192]{1,0:T(8,128)(2,1)S(1)}) custom-call(f32[64,128]{1,0:T(8,128)S(1)} %get-tuple-element.24.gram, f32[160,64]{1,0:T(8,128)S(1)} %get-tuple-element.25.left, f32[32,80,128]{2,1,0:T(8,128)S(1)} %all_to_all.23.right, ...), custom_call_target="tpu_custom_call" | custom-call | bytes 16000000 | tf_op jit(solution)/shard_map/own/pallas_call | solution.py:322
  98.8 0.0 collective-permute-done.3.right
  98.8 1.5 %other.1 = bf16[160,10240]{1,0:T(8,128)(2,1)} custom-call(bf16[160,192]{1,0:T(8,128)(2,1)S(1)} %get-tuple-element.28.factor, f32[32,80,128]{2,1,0:T(8,128)S(1)} %collective-permute-done.3.right, f32[8,160,640]{2,1,0:T(8,128)S(1)} %get-tuple-element.22.merged, bf16[160,10240]{1,0:T(8,128)(2,1)} %get-tuple-element.29.partial), custom_call_target="tpu_custom_call", output_to_operand_aliasing={{}: (3, {})} | custom-call | bytes 8000000 | tf_op jit(solution)/shard_map/other/pallas_call | solution.py:355
  (1 shorter events, 0.0 us)
Async XLA Ops:
  5.2 4.2 %collective-permute-start = (f32[40,128]{1,0:T(8,128)S(1)}, f32[40,128]{1,0:T(8,128)S(1)}, u32[]{:S(2)}, u32[]{:S(2)}) collective-permute-start(f32[40,128]{1,0:T(8,128)S(1)} %get-tuple-element.18), channel_id=1, source_target_pairs={{0,16},{16,0},{1,17},{17,1},{2,18},{18,2},{3,19},{19,3},{4,20},{20... | collective-permute-start | bytes 61448 | tf_op jit(solution)/shard_map/ppermute | solution.py:369
  9.4 18.4 %collective-permute-start.2 = (f32[8,160,640]{2,1,0:T(8,128)S(1)}, f32[8,160,640]{2,1,0:T(8,128)S(1)}, u32[]{:S(2)}, u32[]{:S(2)}) collective-permute-start(f32[8,160,640]{2,1,0:T(8,128)S(1)} %get-tuple-element.22.merged), channel_id=1, source_target_pairs={{0,16},{16,0},{1,17},{17,1},{2,18},{18,2},{3,19},{19,3},{4,20},{20... | collective-permute-start | bytes 9830408 | tf_op jit(solution)/shard_map/ppermute | solution.py:369
  25.0 2.8 %collective-permute-start.1 = (f32[8,40,128]{2,1,0:T(8,128)S(1)}, f32[8,40,128]{2,1,0:T(8,128)S(1)}, u32[]{:S(2)}, u32[]{:S(2)}) collective-permute-start(f32[8,40,128]{2,1,0:T(8,128)S(1)} %all_to_all.20.mine), channel_id=1, source_target_pairs={{0,16},{16,0},{1,17},{17,1},{2,18},{18,2},{3,19},{19,3},{4,20},{20... | collective-permute-start | bytes 491528 | tf_op jit(solution)/shard_map/ppermute | solution.py:369
  29.4 63.9 %copy-start = (f32[160,640]{1,0:T(8,128)S(1)}, f32[160,640]{1,0:T(8,128)}, u32[]{:S(2)}) copy-start(f32[160,640]{1,0:T(8,128)} %weights.1) | copy-start | bytes 1228804
  29.4 63.9 %copy-start.1 = (f32[160,640]{1,0:T(8,128)S(1)}, f32[160,640]{1,0:T(8,128)}, u32[]{:S(2)}) copy-start(f32[160,640]{1,0:T(8,128)} %momentum.1) | copy-start | bytes 1228804
  89.3 9.5 %collective-permute-start.3 = (f32[32,80,128]{2,1,0:T(8,128)S(1)}, f32[32,80,128]{2,1,0:T(8,128)S(1)}, u32[]{:S(2)}, u32[]{:S(2)}) collective-permute-start(f32[32,80,128]{2,1,0:T(8,128)S(1)} %all_to_all.23.right), channel_id=1, source_target_pairs={{0,16},{16,0},{1,17},{17,1},{2,18},{18,2},{3,19},{19,3},{4,20},{20... | collective-permute-start | bytes 3932168 | tf_op jit(solution)/shard_map/ppermute | solution.py:369

commit v8 on v7

--- a/solution.py
+++ b/solution.py
@@ -289,26 +289,22 @@
     held, held_weights, held_momentum, sems, state_sems,
 ):
     core, z = lax.axis_index("core"), line_index()
-    factor[...] = solve(gram[...], left[...])
-
-    @pl.loop(0, blocks)
-    def _(k):
-        approx = approx_block(k, factor[...], right)
-        held[k] = (merged[k] - approx).astype(bf16)
-        block_copy(k, core, held, new_error, sems).start()
-
-        @pl.when(z == k)
-        def _():
-            moved = momentum_decay * momentum[...] + approx
-            held_momentum[...] = moved
-            held_weights[...] = weights[...] - outer_rate * (approx + momentum_decay * moved)
-
     state = [
         pltpu.make_async_copy(held_weights, new_weights, state_sems.at[0]),
         pltpu.make_async_copy(held_momentum, new_momentum, state_sems.at[1]),
     ]
+    factor[...] = solve(gram[...], left[...])
+
+    approx = approx_block(z, factor[...], right)
+    moved = momentum_decay * momentum[...] + approx
+    held_momentum[...] = moved
+    held_weights[...] = weights[...] - outer_rate * (approx + momentum_decay * moved)
     for copy in state:
         copy.start()
+
+    for k in range(blocks):
+        held[k] = (merged[k] - approx_block(k, factor[...], right)).astype(bf16)
+        block_copy(k, core, held, new_error, sems).start()
 
     @pl.loop(0, blocks)
     def _(k):

time: 101 us -> 99.5 us (0.985)
  Pallas kernels: 13.4 us -> 12.3 us
where the time goes in v8:
time: 99.5 us; the launch traced here: 99.3 us
  blocking collectives  75 us (75%)
  Pallas kernels  12.3 us (12%)
  starting transfers between devices  9.39 us (9%)
  waiting for transfers between devices  1.88 us (2%)
    all_to_all x1, blocking collectives, local(): plane = plane_sum(lax.all_to_all(chunks, ('x', 'y', 'zl'), 0, 0))  28.2 us
    all_to_all x1, blocking collectives, local(): own = lax.all_to_all(line, ('x', 'y', 'zl'), 0, 0)  21.7 us
    all_to_all x1, blocking collectives, local(): mine = lax.all_to_all(pair_sum(mine, theirs), ('zh', 'zl'), 0, 0)  15.3 us
    all_to_all x1, blocking collectives, local(): line, gram = line_sum(lax.all_to_all(plane, 'zh', 0, 0))  9.85 us
    ppermute x4, starting transfers between devices, swap(): return lax.ppermute(value, 'core', [(0, 1), (1, 0)])  9.39 us
    pallas_call x1, Pallas kernels, left_factor(): call(left_kernel, 'left', 24, 13000000, in_specs=[hbm, hbm, hbm], out_spe...  4.57 us
    pallas_call x1, Pallas kernels, finish_own(): call(own_kernel, 'own', 16, 16000000, in_specs=[vmem] * 6, out_specs=[hbm...  4.46 us
  transfers between devices with their start and end apart: 4, of which 2 were waited for; matrix products, arithmetic and copies ran while one was open for 0% of the time, Pallas kernels for 5%

profile of v8, /device:TPU:1, one launch (start us, length us, event | category | flops | bytes accessed | tf_op | source)
XLA Modules:
  0.0 99.3 jit_solution(4392144489042669358)
XLA Ops:
  0.6 4.6 %left.1 = (f32[40,128]{1,0:T(8,128)S(1)}, f32[40,128]{1,0:T(8,128)S(1)}, f32[8,160,640]{2,1,0:T(8,128)S(1)}, f32[8,160,640]{2,1,0:T(8,128)S(1)}) custom-call(bf16[160,10240]{1,0:T(8,128)(2,1)} %bitcast.4, bf16[160,10240]{1,0:T(8,128)(2,1)} %bitcast.5, f32[64,10240]{1,0:T(8,128)} %bitcast.7), custom_call_target="tpu_custom_call" | custom-call | bytes 13000000 | tf_op jit(solution)/shard_map/left/pallas_call | solution.py:109
  5.2 3.3 %collective-permute-start = (f32[40,128]{1,0:T(8,128)S(1)}, f32[40,128]{1,0:T(8,128)S(1)}, u32[]{:S(2)}, u32[]{:S(2)}) collective-permute-start(f32[40,128]{1,0:T(8,128)S(1)} %get-tuple-element.18), channel_id=1, source_target_pairs={{0,16},{16,0},{1,17},{17,1},{2,18},{18,2},{3,19},{19,3},{4,20},{20... | collective-permute-start | bytes 61448 | tf_op jit(solution)/shard_map/ppermute | solution.py:365
  8.5 0.8 collective-permute-done.received
  9.4 0.3 collective-permute-start.2
  9.7 15.3 %all_to_all.20.mine = f32[8,40,128]{2,1,0:T(8,128)S(1)} all-to-all(f32[8,40,128]{2,1,0:T(8,128)S(1)} %pair_sum.1), channel_id=1, replica_groups=mesh['zh'=4,'zl'=2,'core'=2,'x'=4,'y'=4] {'zh','zl'}, dimensions={0} | all-to-all | bytes 327680 | tf_op jit(solution)/shard_map/all_to_all | solution.py:372
  25.0 1.7 %collective-permute-start.1 = (f32[8,40,128]{2,1,0:T(8,128)S(1)}, f32[8,40,128]{2,1,0:T(8,128)S(1)}, u32[]{:S(2)}, u32[]{:S(2)}) collective-permute-start(f32[8,40,128]{2,1,0:T(8,128)S(1)} %all_to_all.20.mine), channel_id=1, source_target_pairs={{0,16},{16,0},{1,17},{17,1},{2,18},{18,2},{3,19},{19,3},{4,20},{20... | collective-permute-start | bytes 491528 | tf_op jit(solution)/shard_map/ppermute | solution.py:365
  26.7 1.0 %collective-permute-done.1.theirs = f32[8,40,128]{2,1,0:T(8,128)S(1)} collective-permute-done((f32[8,40,128]{2,1,0:T(8,128)S(1)}, f32[8,40,128]{2,1,0:T(8,128)S(1)}, u32[]{:S(2)}, u32[]{:S(2)}) %collective-permute-start.1) | collective-permute-done | bytes 163872 | tf_op jit(solution)/shard_map/ppermute | solution.py:365
  27.7 0.0 collective-permute-done.2.received
  27.7 1.6 %right.1 = (f32[32,88,128]{2,1,0:T(8,128)S(1)}, f32[160,64]{1,0:T(8,128)S(1)}) custom-call(f32[8,40,128]{2,1,0:T(8,128)S(1)} %all_to_all.20.mine, f32[8,40,128]{2,1,0:T(8,128)S(1)} %collective-permute-done.1.theirs, f32[8,160,640]{2,1,0:T(8,128)S(1)} %get-tuple-element.21.keep.merged, f32[8,160,640]{2,1,0:T(8,128)S(1)} %collective-permute-done.2.received), custom_call_target="tpu_custom_call" | custom-call | bytes 10000000 | tf_op jit(solution)/shard_map/right/pallas_call | solution.py:178
  29.4 0.0 copy-start
  29.4 0.0 copy-start.1
  29.4 28.2 %all_to_all.21.chunks = f32[32,88,128]{2,1,0:T(8,128)S(1)} all-to-all(f32[32,88,128]{2,1,0:T(8,128)S(1)} %get-tuple-element.23), channel_id=1, replica_groups=mesh['zh'=4,'zl'=2,'core'=2,'x'=4,'y'=4] {'x','y','zl'}, dimensions={0} | all-to-all | bytes 2883584 | tf_op jit(solution)/shard_map/all_to_all | solution.py:374
  57.6 0.1 plane_sum.1
  57.7 9.9 %all_to_all.22.chunks = f32[4,88,128]{2,1,0:T(8,128)S(1)} all-to-all(f32[4,88,128]{2,1,0:T(8,128)S(1)} %plane_sum.1), channel_id=1, replica_groups=mesh['zh'=4,'zl'=2,'core'=2,'x'=4,'y'=4] {'zh'}, dimensions={0} | all-to-all | bytes 360448 | tf_op jit(solution)/shard_map/all_to_all | solution.py:375
  67.6 0.1 line_sum.1
  67.7 21.7 %all_to_all.23.right = f32[32,80,128]{2,1,0:T(8,128)S(1)} all-to-all(f32[32,80,128]{2,1,0:T(8,128)S(1)} %get-tuple-element.26), channel_id=1, replica_groups=mesh['zh'=4,'zl'=2,'core'=2,'x'=4,'y'=4] {'x','y','zl'}, dimensions={0} | all-to-all | bytes 2621440 | tf_op jit(solution)/shard_map/all_to_all | solution.py:376
  89.3 4.0 %collective-permute-start.3 = (f32[32,80,128]{2,1,0:T(8,128)S(1)}, f32[32,80,128]{2,1,0:T(8,128)S(1)}, u32[]{:S(2)}, u32[]{:S(2)}) collective-permute-start(f32[32,80,128]{2,1,0:T(8,128)S(1)} %all_to_all.23.right), channel_id=1, source_target_pairs={{0,16},{16,0},{1,17},{17,1},{2,18},{18,2},{3,19},{19,3},{4,20},{20... | collective-permute-start | bytes 3932168 | tf_op jit(solution)/shard_map/ppermute | solution.py:365
  93.3 0.0 copy-done
  93.3 0.0 copy-done.1
  93.3 4.5 %own.1 = (bf16[160,10240]{1,0:T(8,128)(2,1)}, f32[160,640]{1,0:T(8,128)}, f32[160,640]{1,0:T(8,128)}, bf16[160,192]{1,0:T(8,128)(2,1)S(1)}) custom-call(f32[64,128]{1,0:T(8,128)S(1)} %get-tuple-element.24.gram, f32[160,64]{1,0:T(8,128)S(1)} %get-tuple-element.25.left, f32[32,80,128]{2,1,0:T(8,128)S(1)} %all_to_all.23.right, ...), custom_call_target="tpu_custom_call" | custom-call | bytes 16000000 | tf_op jit(solution)/shard_map/own/pallas_call | solution.py:318
  97.8 0.0 collective-permute-done.3.right
  97.8 1.5 %other.1 = bf16[160,10240]{1,0:T(8,128)(2,1)} custom-call(bf16[160,192]{1,0:T(8,128)(2,1)S(1)} %get-tuple-element.28.factor, f32[32,80,128]{2,1,0:T(8,128)S(1)} %collective-permute-done.3.right, f32[8,160,640]{2,1,0:T(8,128)S(1)} %get-tuple-element.22.merged, bf16[160,10240]{1,0:T(8,128)(2,1)} %get-tuple-element.29.partial), custom_call_target="tpu_custom_call", output_to_operand_aliasing={{}: (3, {})} | custom-call | bytes 8000000 | tf_op jit(solution)/shard_map/other/pallas_call | solution.py:351
  (1 shorter events, 0.0 us)
Async XLA Ops:
  5.2 4.2 %collective-permute-start = (f32[40,128]{1,0:T(8,128)S(1)}, f32[40,128]{1,0:T(8,128)S(1)}, u32[]{:S(2)}, u32[]{:S(2)}) collective-permute-start(f32[40,128]{1,0:T(8,128)S(1)} %get-tuple-element.18), channel_id=1, source_target_pairs={{0,16},{16,0},{1,17},{17,1},{2,18},{18,2},{3,19},{19,3},{4,20},{20... | collective-permute-start | bytes 61448 | tf_op jit(solution)/shard_map/ppermute | solution.py:365
  9.4 18.4 %collective-permute-start.2 = (f32[8,160,640]{2,1,0:T(8,128)S(1)}, f32[8,160,640]{2,1,0:T(8,128)S(1)}, u32[]{:S(2)}, u32[]{:S(2)}) collective-permute-start(f32[8,160,640]{2,1,0:T(8,128)S(1)} %get-tuple-element.22.merged), channel_id=1, source_target_pairs={{0,16},{16,0},{1,17},{17,1},{2,18},{18,2},{3,19},{19,3},{4,20},{20... | collective-permute-start | bytes 9830408 | tf_op jit(solution)/shard_map/ppermute | solution.py:365
  25.0 2.8 %collective-permute-start.1 = (f32[8,40,128]{2,1,0:T(8,128)S(1)}, f32[8,40,128]{2,1,0:T(8,128)S(1)}, u32[]{:S(2)}, u32[]{:S(2)}) collective-permute-start(f32[8,40,128]{2,1,0:T(8,128)S(1)} %all_to_all.20.mine), channel_id=1, source_target_pairs={{0,16},{16,0},{1,17},{17,1},{2,18},{18,2},{3,19},{19,3},{4,20},{20... | collective-permute-start | bytes 491528 | tf_op jit(solution)/shard_map/ppermute | solution.py:365
  29.4 63.9 %copy-start = (f32[160,640]{1,0:T(8,128)S(1)}, f32[160,640]{1,0:T(8,128)}, u32[]{:S(2)}) copy-start(f32[160,640]{1,0:T(8,128)} %weights.1) | copy-start | bytes 1228804
  29.4 63.9 %copy-start.1 = (f32[160,640]{1,0:T(8,128)S(1)}, f32[160,640]{1,0:T(8,128)}, u32[]{:S(2)}) copy-start(f32[160,640]{1,0:T(8,128)} %momentum.1) | copy-start | bytes 1228804
  89.3 8.5 %collective-permute-start.3 = (f32[32,80,128]{2,1,0:T(8,128)S(1)}, f32[32,80,128]{2,1,0:T(8,128)S(1)}, u32[]{:S(2)}, u32[]{:S(2)}) collective-permute-start(f32[32,80,128]{2,1,0:T(8,128)S(1)} %all_to_all.23.right), channel_id=1, source_target_pairs={{0,16},{16,0},{1,17},{17,1},{2,18},{18,2},{3,19},{19,3},{4,20},{20... | collective-permute-start | bytes 3932168 | tf_op jit(solution)/shard_map/ppermute | solution.py:365

commit v9 on v8

--- a/solution.py
+++ b/solution.py
@@ -22,6 +22,7 @@
 bf16 = jnp.bfloat16
 exact = lax.Precision.HIGHEST
 mib = 1024 * 1024
+around = ("zl", "x", "y")
 hbm = pl.BlockSpec(memory_space=pltpu.HBM)
 vmem = pl.BlockSpec(memory_space=pltpu.VMEM)
 
@@ -141,6 +142,10 @@
     )(mine, received)
 
 
+def member(x, k):
+    return 16 * (k % 2) + 4 * x + (k // 2)
+
+
 def line_index():
     return 2 * lax.axis_index("zh") + lax.axis_index("zl")
 
@@ -169,7 +174,7 @@
         block = term[:rank] + term[rank : 2 * rank] + term[2 * rank :]
         for x in range(4):
             for t in range(5):
-                out[8 * x + k, 16 * t : 16 * (t + 1), :] = block[
+                out[member(x, k), 16 * t : 16 * (t + 1), :] = block[
                     16 * x : 16 * (x + 1), 128 * t : 128 * (t + 1)
                 ]
 
@@ -279,7 +284,7 @@
     tiles = []
     for t in range(5):
         part = pl.ds(16 * t, 16)
-        tiles.append(jnp.concatenate([right[8 * x + k, part, :] for x in range(4)], axis=0))
+        tiles.append(jnp.concatenate([right[member(x, k), part, :] for x in range(4)], axis=0))
     high, low = split(jnp.concatenate(tiles, axis=1), 2)
     return dot(factor, jnp.concatenate([high, low, high], axis=0))
 
@@ -371,9 +376,9 @@
     received = swap(send)
     mine = lax.all_to_all(pair_sum(mine, theirs), ("zh", "zl"), 0, 0)
     chunks, left = right_factor(mine, swap(mine), keep, received)
-    plane = plane_sum(lax.all_to_all(chunks, ("x", "y", "zl"), 0, 0))
+    plane = plane_sum(lax.all_to_all(chunks, around, 0, 0))
     line, gram = line_sum(lax.all_to_all(plane, "zh", 0, 0))
-    own = lax.all_to_all(line, ("x", "y", "zl"), 0, 0)
+    own = lax.all_to_all(line, around, 0, 0)
     other = swap(own)
     partial, new_weights, new_momentum, factor = finish_own(
         gram, left, own, keep, weights, momentum

time: 99.5 us -> 98.7 us (level)
  blocking collectives: 75 us -> 73.8 us
    all_to_all x2, blocking collectives: 49.9 us -> 47.9 us  [the longest x1 27.3 us: local(): plane = plane_sum(lax.all_to_all(chunks, around, 0, 0))]
where the time goes in v9:
time: 98.7 us; the launch traced here: 98.5 us
  blocking collectives  73.8 us (75%)
  Pallas kernels  12.4 us (13%)
  starting transfers between devices  9.82 us (10%)
  waiting for transfers between devices  1.88 us (2%)
    all_to_all x1, blocking collectives, local(): plane = plane_sum(lax.all_to_all(chunks, around, 0, 0))  27.3 us
    all_to_all x1, blocking collectives, local(): own = lax.all_to_all(line, around, 0, 0)  20.6 us
    all_to_all x1, blocking collectives, local(): mine = lax.all_to_all(pair_sum(mine, theirs), ('zh', 'zl'), 0, 0)  15.3 us
    all_to_all x1, blocking collectives, local(): line, gram = line_sum(lax.all_to_all(plane, 'zh', 0, 0))  10.6 us
    ppermute x4, starting transfers between devices, swap(): return lax.ppermute(value, 'core', [(0, 1), (1, 0)])  9.82 us
    pallas_call x1, Pallas kernels, left_factor(): call(left_kernel, 'left', 24, 13000000, in_specs=[hbm, hbm, hbm], out_spe...  4.57 us
    pallas_call x1, Pallas kernels, finish_own(): call(own_kernel, 'own', 16, 16000000, in_specs=[vmem] * 6, out_specs=[hbm...  4.46 us
  transfers between devices with their start and end apart: 4, of which 2 were waited for; matrix products, arithmetic and copies ran while one was open for 0% of the time, Pallas kernels for 5%

profile of v9, /device:TPU:1, one launch (start us, length us, event | category | flops | bytes accessed | tf_op | source)
XLA Modules:
  0.0 98.5 jit_solution(5952261064800087269)
XLA Ops:
  0.6 4.6 %left.1 = (f32[40,128]{1,0:T(8,128)S(1)}, f32[40,128]{1,0:T(8,128)S(1)}, f32[8,160,640]{2,1,0:T(8,128)S(1)}, f32[8,160,640]{2,1,0:T(8,128)S(1)}) custom-call(bf16[160,10240]{1,0:T(8,128)(2,1)} %bitcast.4, bf16[160,10240]{1,0:T(8,128)(2,1)} %bitcast.5, f32[64,10240]{1,0:T(8,128)} %bitcast.7), custom_call_target="tpu_custom_call" | custom-call | bytes 13000000 | tf_op jit(solution)/shard_map/left/pallas_call | solution.py:110
  5.2 3.3 %collective-permute-start = (f32[40,128]{1,0:T(8,128)S(1)}, f32[40,128]{1,0:T(8,128)S(1)}, u32[]{:S(2)}, u32[]{:S(2)}) collective-permute-start(f32[40,128]{1,0:T(8,128)S(1)} %get-tuple-element.18), channel_id=1, source_target_pairs={{0,16},{16,0},{1,17},{17,1},{2,18},{18,2},{3,19},{19,3},{4,20},{20... | collective-permute-start | bytes 61448 | tf_op jit(solution)/shard_map/ppermute | solution.py:370
  8.5 0.8 collective-permute-done.received
  9.4 0.3 collective-permute-start.2
  9.7 15.3 %all_to_all.20.mine = f32[8,40,128]{2,1,0:T(8,128)S(1)} all-to-all(f32[8,40,128]{2,1,0:T(8,128)S(1)} %pair_sum.1), channel_id=1, replica_groups=mesh['zh'=4,'zl'=2,'core'=2,'x'=4,'y'=4] {'zh','zl'}, dimensions={0} | all-to-all | bytes 327680 | tf_op jit(solution)/shard_map/all_to_all | solution.py:377
  25.0 1.7 %collective-permute-start.1 = (f32[8,40,128]{2,1,0:T(8,128)S(1)}, f32[8,40,128]{2,1,0:T(8,128)S(1)}, u32[]{:S(2)}, u32[]{:S(2)}) collective-permute-start(f32[8,40,128]{2,1,0:T(8,128)S(1)} %all_to_all.20.mine), channel_id=1, source_target_pairs={{0,16},{16,0},{1,17},{17,1},{2,18},{18,2},{3,19},{19,3},{4,20},{20... | collective-permute-start | bytes 491528 | tf_op jit(solution)/shard_map/ppermute | solution.py:370
  26.7 1.0 %collective-permute-done.1.theirs = f32[8,40,128]{2,1,0:T(8,128)S(1)} collective-permute-done((f32[8,40,128]{2,1,0:T(8,128)S(1)}, f32[8,40,128]{2,1,0:T(8,128)S(1)}, u32[]{:S(2)}, u32[]{:S(2)}) %collective-permute-start.1) | collective-permute-done | bytes 163872 | tf_op jit(solution)/shard_map/ppermute | solution.py:370
  27.7 0.0 collective-permute-done.2.received
  27.7 1.6 %right.1 = (f32[32,88,128]{2,1,0:T(8,128)S(1)}, f32[160,64]{1,0:T(8,128)S(1)}) custom-call(f32[8,40,128]{2,1,0:T(8,128)S(1)} %all_to_all.20.mine, f32[8,40,128]{2,1,0:T(8,128)S(1)} %collective-permute-done.1.theirs, f32[8,160,640]{2,1,0:T(8,128)S(1)} %get-tuple-element.21.keep.merged, f32[8,160,640]{2,1,0:T(8,128)S(1)} %collective-permute-done.2.received), custom_call_target="tpu_custom_call" | custom-call | bytes 10000000 | tf_op jit(solution)/shard_map/right/pallas_call | solution.py:183
  29.4 0.0 copy-start
  29.4 0.0 copy-start.1
  29.4 27.3 %all_to_all.21.chunks = f32[32,88,128]{2,1,0:T(8,128)S(1)} all-to-all(f32[32,88,128]{2,1,0:T(8,128)S(1)} %get-tuple-element.23), channel_id=1, replica_groups=mesh['zh'=4,'zl'=2,'core'=2,'x'=4,'y'=4] {'zl','x','y'}, dimensions={0} | all-to-all | bytes 2883584 | tf_op jit(solution)/shard_map/all_to_all | solution.py:379
  56.7 0.1 plane_sum.1
  56.8 10.6 %all_to_all.22.chunks = f32[4,88,128]{2,1,0:T(8,128)S(1)} all-to-all(f32[4,88,128]{2,1,0:T(8,128)S(1)} %plane_sum.1), channel_id=1, replica_groups=mesh['zh'=4,'zl'=2,'core'=2,'x'=4,'y'=4] {'zh'}, dimensions={0} | all-to-all | bytes 360448 | tf_op jit(solution)/shard_map/all_to_all | solution.py:380
  67.4 0.1 line_sum.1
  67.5 20.6 %all_to_all.23.right = f32[32,80,128]{2,1,0:T(8,128)S(1)} all-to-all(f32[32,80,128]{2,1,0:T(8,128)S(1)} %get-tuple-element.26), channel_id=1, replica_groups=mesh['zh'=4,'zl'=2,'core'=2,'x'=4,'y'=4] {'zl','x','y'}, dimensions={0} | all-to-all | bytes 2621440 | tf_op jit(solution)/shard_map/all_to_all | solution.py:381
  88.1 4.4 %collective-permute-start.3 = (f32[32,80,128]{2,1,0:T(8,128)S(1)}, f32[32,80,128]{2,1,0:T(8,128)S(1)}, u32[]{:S(2)}, u32[]{:S(2)}) collective-permute-start(f32[32,80,128]{2,1,0:T(8,128)S(1)} %all_to_all.23.right), channel_id=1, source_target_pairs={{0,16},{16,0},{1,17},{17,1},{2,18},{18,2},{3,19},{19,3},{4,20},{20... | collective-permute-start | bytes 3932168 | tf_op jit(solution)/shard_map/ppermute | solution.py:370
  92.5 0.0 copy-done
  92.5 0.0 copy-done.1
  92.5 4.5 %own.1 = (bf16[160,10240]{1,0:T(8,128)(2,1)}, f32[160,640]{1,0:T(8,128)}, f32[160,640]{1,0:T(8,128)}, bf16[160,192]{1,0:T(8,128)(2,1)S(1)}) custom-call(f32[64,128]{1,0:T(8,128)S(1)} %get-tuple-element.24.gram, f32[160,64]{1,0:T(8,128)S(1)} %get-tuple-element.25.left, f32[32,80,128]{2,1,0:T(8,128)S(1)} %all_to_all.23.right, ...), custom_call_target="tpu_custom_call" | custom-call | bytes 16000000 | tf_op jit(solution)/shard_map/own/pallas_call | solution.py:323
  97.0 0.0 collective-permute-done.3.right
  97.0 1.5 %other.1 = bf16[160,10240]{1,0:T(8,128)(2,1)} custom-call(bf16[160,192]{1,0:T(8,128)(2,1)S(1)} %get-tuple-element.28.factor, f32[32,80,128]{2,1,0:T(8,128)S(1)} %collective-permute-done.3.right, f32[8,160,640]{2,1,0:T(8,128)S(1)} %get-tuple-element.22.merged, bf16[160,10240]{1,0:T(8,128)(2,1)} %get-tuple-element.29.partial), custom_call_target="tpu_custom_call", output_to_operand_aliasing={{}: (3, {})} | custom-call | bytes 8000000 | tf_op jit(solution)/shard_map/other/pallas_call | solution.py:356
  (1 shorter events, 0.0 us)
Async XLA Ops:
  5.2 4.2 %collective-permute-start = (f32[40,128]{1,0:T(8,128)S(1)}, f32[40,128]{1,0:T(8,128)S(1)}, u32[]{:S(2)}, u32[]{:S(2)}) collective-permute-start(f32[40,128]{1,0:T(8,128)S(1)} %get-tuple-element.18), channel_id=1, source_target_pairs={{0,16},{16,0},{1,17},{17,1},{2,18},{18,2},{3,19},{19,3},{4,20},{20... | collective-permute-start | bytes 61448 | tf_op jit(solution)/shard_map/ppermute | solution.py:370
  9.4 18.4 %collective-permute-start.2 = (f32[8,160,640]{2,1,0:T(8,128)S(1)}, f32[8,160,640]{2,1,0:T(8,128)S(1)}, u32[]{:S(2)}, u32[]{:S(2)}) collective-permute-start(f32[8,160,640]{2,1,0:T(8,128)S(1)} %get-tuple-element.22.merged), channel_id=1, source_target_pairs={{0,16},{16,0},{1,17},{17,1},{2,18},{18,2},{3,19},{19,3},{4,20},{20... | collective-permute-start | bytes 9830408 | tf_op jit(solution)/shard_map/ppermute | solution.py:370
  25.0 2.8 %collective-permute-start.1 = (f32[8,40,128]{2,1,0:T(8,128)S(1)}, f32[8,40,128]{2,1,0:T(8,128)S(1)}, u32[]{:S(2)}, u32[]{:S(2)}) collective-permute-start(f32[8,40,128]{2,1,0:T(8,128)S(1)} %all_to_all.20.mine), channel_id=1, source_target_pairs={{0,16},{16,0},{1,17},{17,1},{2,18},{18,2},{3,19},{19,3},{4,20},{20... | collective-permute-start | bytes 491528 | tf_op jit(solution)/shard_map/ppermute | solution.py:370
  29.4 63.1 %copy-start = (f32[160,640]{1,0:T(8,128)S(1)}, f32[160,640]{1,0:T(8,128)}, u32[]{:S(2)}) copy-start(f32[160,640]{1,0:T(8,128)} %weights.1) | copy-start | bytes 1228804
  29.4 63.1 %copy-start.1 = (f32[160,640]{1,0:T(8,128)S(1)}, f32[160,640]{1,0:T(8,128)}, u32[]{:S(2)}) copy-start(f32[160,640]{1,0:T(8,128)} %momentum.1) | copy-start | bytes 1228804
  88.1 8.9 %collective-permute-start.3 = (f32[32,80,128]{2,1,0:T(8,128)S(1)}, f32[32,80,128]{2,1,0:T(8,128)S(1)}, u32[]{:S(2)}, u32[]{:S(2)}) collective-permute-start(f32[32,80,128]{2,1,0:T(8,128)S(1)} %all_to_all.23.right), channel_id=1, source_target_pairs={{0,16},{16,0},{1,17},{17,1},{2,18},{18,2},{3,19},{19,3},{4,20},{20... | collective-permute-start | bytes 3932168 | tf_op jit(solution)/shard_map/ppermute | solution.py:370

commit v10 on v9

--- a/solution.py
+++ b/solution.py
@@ -245,7 +245,7 @@
         block = [[columns[0][j][i : i + 1, :] for j in range(step)] for i in range(step)]
         pivots = [work[0][i : i + 1, :] for i in range(step)]
         for j in range(step):
-            scale = 1.0 / block[j][j]
+            scale = pl.reciprocal(block[j][j], approx=False)
             pivots[j] = pivots[j] * scale
             for m in range(j + 1, step):
                 block[j][m] = block[j][m] * scale

time: 98.7 us -> 98.7 us (level)
  no operation moved by 1% of the time
where the time goes in v10:
time: 98.7 us; the launch traced here: 98.5 us
  blocking collectives  73.8 us (75%)
  Pallas kernels  12.4 us (13%)
  starting transfers between devices  9.82 us (10%)
  waiting for transfers between devices  1.88 us (2%)
    all_to_all x1, blocking collectives, local(): plane = plane_sum(lax.all_to_all(chunks, around, 0, 0))  27.3 us
    all_to_all x1, blocking collectives, local(): own = lax.all_to_all(line, around, 0, 0)  20.6 us
    all_to_all x1, blocking collectives, local(): mine = lax.all_to_all(pair_sum(mine, theirs), ('zh', 'zl'), 0, 0)  15.3 us
    all_to_all x1, blocking collectives, local(): line, gram = line_sum(lax.all_to_all(plane, 'zh', 0, 0))  10.6 us
    ppermute x4, starting transfers between devices, swap(): return lax.ppermute(value, 'core', [(0, 1), (1, 0)])  9.82 us
    pallas_call x1, Pallas kernels, left_factor(): call(left_kernel, 'left', 24, 13000000, in_specs=[hbm, hbm, hbm], out_spe...  4.57 us
    pallas_call x1, Pallas kernels, finish_own(): call(own_kernel, 'own', 16, 16000000, in_specs=[vmem] * 6, out_specs=[hbm...  4.46 us
  transfers between devices with their start and end apart: 4, of which 2 were waited for; matrix products, arithmetic and copies ran while one was open for 0% of the time, Pallas kernels for 5%

profile of v10, /device:TPU:1, one launch (start us, length us, event | category | flops | bytes accessed | tf_op | source)
XLA Modules:
  0.0 98.5 jit_solution(5952261064800087269)
XLA Ops:
  0.6 4.6 %left.1 = (f32[40,128]{1,0:T(8,128)S(1)}, f32[40,128]{1,0:T(8,128)S(1)}, f32[8,160,640]{2,1,0:T(8,128)S(1)}, f32[8,160,640]{2,1,0:T(8,128)S(1)}) custom-call(bf16[160,10240]{1,0:T(8,128)(2,1)} %bitcast.4, bf16[160,10240]{1,0:T(8,128)(2,1)} %bitcast.5, f32[64,10240]{1,0:T(8,128)} %bitcast.7), custom_call_target="tpu_custom_call" | custom-call | bytes 13000000 | tf_op jit(solution)/shard_map/left/pallas_call | solution.py:110
  5.2 3.3 %collective-permute-start = (f32[40,128]{1,0:T(8,128)S(1)}, f32[40,128]{1,0:T(8,128)S(1)}, u32[]{:S(2)}, u32[]{:S(2)}) collective-permute-start(f32[40,128]{1,0:T(8,128)S(1)} %get-tuple-element.18), channel_id=1, source_target_pairs={{0,16},{16,0},{1,17},{17,1},{2,18},{18,2},{3,19},{19,3},{4,20},{20... | collective-permute-start | bytes 61448 | tf_op jit(solution)/shard_map/ppermute | solution.py:370
  8.5 0.8 collective-permute-done.received
  9.4 0.3 collective-permute-start.2
  9.7 15.3 %all_to_all.20.mine = f32[8,40,128]{2,1,0:T(8,128)S(1)} all-to-all(f32[8,40,128]{2,1,0:T(8,128)S(1)} %pair_sum.1), channel_id=1, replica_groups=mesh['zh'=4,'zl'=2,'core'=2,'x'=4,'y'=4] {'zh','zl'}, dimensions={0} | all-to-all | bytes 327680 | tf_op jit(solution)/shard_map/all_to_all | solution.py:377
  25.0 1.7 %collective-permute-start.1 = (f32[8,40,128]{2,1,0:T(8,128)S(1)}, f32[8,40,128]{2,1,0:T(8,128)S(1)}, u32[]{:S(2)}, u32[]{:S(2)}) collective-permute-start(f32[8,40,128]{2,1,0:T(8,128)S(1)} %all_to_all.20.mine), channel_id=1, source_target_pairs={{0,16},{16,0},{1,17},{17,1},{2,18},{18,2},{3,19},{19,3},{4,20},{20... | collective-permute-start | bytes 491528 | tf_op jit(solution)/shard_map/ppermute | solution.py:370
  26.7 1.0 %collective-permute-done.1.theirs = f32[8,40,128]{2,1,0:T(8,128)S(1)} collective-permute-done((f32[8,40,128]{2,1,0:T(8,128)S(1)}, f32[8,40,128]{2,1,0:T(8,128)S(1)}, u32[]{:S(2)}, u32[]{:S(2)}) %collective-permute-start.1) | collective-permute-done | bytes 163872 | tf_op jit(solution)/shard_map/ppermute | solution.py:370
  27.7 0.0 collective-permute-done.2.received
  27.7 1.6 %right.1 = (f32[32,88,128]{2,1,0:T(8,128)S(1)}, f32[160,64]{1,0:T(8,128)S(1)}) custom-call(f32[8,40,128]{2,1,0:T(8,128)S(1)} %all_to_all.20.mine, f32[8,40,128]{2,1,0:T(8,128)S(1)} %collective-permute-done.1.theirs, f32[8,160,640]{2,1,0:T(8,128)S(1)} %get-tuple-element.21.keep.merged, f32[8,160,640]{2,1,0:T(8,128)S(1)} %collective-permute-done.2.received), custom_call_target="tpu_custom_call" | custom-call | bytes 10000000 | tf_op jit(solution)/shard_map/right/pallas_call | solution.py:183
  29.4 0.0 copy-start
  29.4 0.0 copy-start.1
  29.4 27.3 %all_to_all.21.chunks = f32[32,88,128]{2,1,0:T(8,128)S(1)} all-to-all(f32[32,88,128]{2,1,0:T(8,128)S(1)} %get-tuple-element.23), channel_id=1, replica_groups=mesh['zh'=4,'zl'=2,'core'=2,'x'=4,'y'=4] {'zl','x','y'}, dimensions={0} | all-to-all | bytes 2883584 | tf_op jit(solution)/shard_map/all_to_all | solution.py:379
  56.7 0.1 plane_sum.1
  56.8 10.6 %all_to_all.22.chunks = f32[4,88,128]{2,1,0:T(8,128)S(1)} all-to-all(f32[4,88,128]{2,1,0:T(8,128)S(1)} %plane_sum.1), channel_id=1, replica_groups=mesh['zh'=4,'zl'=2,'core'=2,'x'=4,'y'=4] {'zh'}, dimensions={0} | all-to-all | bytes 360448 | tf_op jit(solution)/shard_map/all_to_all | solution.py:380
  67.4 0.1 line_sum.1
  67.5 20.6 %all_to_all.23.right = f32[32,80,128]{2,1,0:T(8,128)S(1)} all-to-all(f32[32,80,128]{2,1,0:T(8,128)S(1)} %get-tuple-element.26), channel_id=1, replica_groups=mesh['zh'=4,'zl'=2,'core'=2,'x'=4,'y'=4] {'zl','x','y'}, dimensions={0} | all-to-all | bytes 2621440 | tf_op jit(solution)/shard_map/all_to_all | solution.py:381
  88.1 4.4 %collective-permute-start.3 = (f32[32,80,128]{2,1,0:T(8,128)S(1)}, f32[32,80,128]{2,1,0:T(8,128)S(1)}, u32[]{:S(2)}, u32[]{:S(2)}) collective-permute-start(f32[32,80,128]{2,1,0:T(8,128)S(1)} %all_to_all.23.right), channel_id=1, source_target_pairs={{0,16},{16,0},{1,17},{17,1},{2,18},{18,2},{3,19},{19,3},{4,20},{20... | collective-permute-start | bytes 3932168 | tf_op jit(solution)/shard_map/ppermute | solution.py:370
  92.5 0.0 copy-done
  92.5 0.0 copy-done.1
  92.5 4.5 %own.1 = (bf16[160,10240]{1,0:T(8,128)(2,1)}, f32[160,640]{1,0:T(8,128)}, f32[160,640]{1,0:T(8,128)}, bf16[160,192]{1,0:T(8,128)(2,1)S(1)}) custom-call(f32[64,128]{1,0:T(8,128)S(1)} %get-tuple-element.24.gram, f32[160,64]{1,0:T(8,128)S(1)} %get-tuple-element.25.left, f32[32,80,128]{2,1,0:T(8,128)S(1)} %all_to_all.23.right, ...), custom_call_target="tpu_custom_call" | custom-call | bytes 16000000 | tf_op jit(solution)/shard_map/own/pallas_call | solution.py:323
  97.0 0.0 collective-permute-done.3.right
  97.0 1.5 %other.1 = bf16[160,10240]{1,0:T(8,128)(2,1)} custom-call(bf16[160,192]{1,0:T(8,128)(2,1)S(1)} %get-tuple-element.28.factor, f32[32,80,128]{2,1,0:T(8,128)S(1)} %collective-permute-done.3.right, f32[8,160,640]{2,1,0:T(8,128)S(1)} %get-tuple-element.22.merged, bf16[160,10240]{1,0:T(8,128)(2,1)} %get-tuple-element.29.partial), custom_call_target="tpu_custom_call", output_to_operand_aliasing={{}: (3, {})} | custom-call | bytes 8000000 | tf_op jit(solution)/shard_map/other/pallas_call | solution.py:356
  (1 shorter events, 0.0 us)
Async XLA Ops:
  5.2 4.2 %collective-permute-start = (f32[40,128]{1,0:T(8,128)S(1)}, f32[40,128]{1,0:T(8,128)S(1)}, u32[]{:S(2)}, u32[]{:S(2)}) collective-permute-start(f32[40,128]{1,0:T(8,128)S(1)} %get-tuple-element.18), channel_id=1, source_target_pairs={{0,16},{16,0},{1,17},{17,1},{2,18},{18,2},{3,19},{19,3},{4,20},{20... | collective-permute-start | bytes 61448 | tf_op jit(solution)/shard_map/ppermute | solution.py:370
  9.4 18.4 %collective-permute-start.2 = (f32[8,160,640]{2,1,0:T(8,128)S(1)}, f32[8,160,640]{2,1,0:T(8,128)S(1)}, u32[]{:S(2)}, u32[]{:S(2)}) collective-permute-start(f32[8,160,640]{2,1,0:T(8,128)S(1)} %get-tuple-element.22.merged), channel_id=1, source_target_pairs={{0,16},{16,0},{1,17},{17,1},{2,18},{18,2},{3,19},{19,3},{4,20},{20... | collective-permute-start | bytes 9830408 | tf_op jit(solution)/shard_map/ppermute | solution.py:370
  25.0 2.8 %collective-permute-start.1 = (f32[8,40,128]{2,1,0:T(8,128)S(1)}, f32[8,40,128]{2,1,0:T(8,128)S(1)}, u32[]{:S(2)}, u32[]{:S(2)}) collective-permute-start(f32[8,40,128]{2,1,0:T(8,128)S(1)} %all_to_all.20.mine), channel_id=1, source_target_pairs={{0,16},{16,0},{1,17},{17,1},{2,18},{18,2},{3,19},{19,3},{4,20},{20... | collective-permute-start | bytes 491528 | tf_op jit(solution)/shard_map/ppermute | solution.py:370
  29.4 63.1 %copy-start = (f32[160,640]{1,0:T(8,128)S(1)}, f32[160,640]{1,0:T(8,128)}, u32[]{:S(2)}) copy-start(f32[160,640]{1,0:T(8,128)} %weights.1) | copy-start | bytes 1228804
  29.4 63.1 %copy-start.1 = (f32[160,640]{1,0:T(8,128)S(1)}, f32[160,640]{1,0:T(8,128)}, u32[]{:S(2)}) copy-start(f32[160,640]{1,0:T(8,128)} %momentum.1) | copy-start | bytes 1228804
  88.1 8.9 %collective-permute-start.3 = (f32[32,80,128]{2,1,0:T(8,128)S(1)}, f32[32,80,128]{2,1,0:T(8,128)S(1)}, u32[]{:S(2)}, u32[]{:S(2)}) collective-permute-start(f32[32,80,128]{2,1,0:T(8,128)S(1)} %all_to_all.23.right), channel_id=1, source_target_pairs={{0,16},{16,0},{1,17},{17,1},{2,18},{18,2},{3,19},{19,3},{4,20},{20... | collective-permute-start | bytes 3932168 | tf_op jit(solution)/shard_map/ppermute | solution.py:370
